TPU v7x, 32 devices: a whole 2x2x4 slice. The times are simulated.
32 devices in a mesh: dp: 8 (over z, y), fsdp: 4 (over x, core).
Axes of the slice: x: 2, y: 2, z: 4, core: 2. Of those that a mesh axis runs over, the one named last changes fastest.
Arguments:
- hidden_in: bfloat16 [2, 32, 512, 1024], P(None, ('dp', 'fsdp')), may hold values from -6 to 6
- cotangent: bfloat16 [2, 32, 512, 1024], P(None, ('dp', 'fsdp')), may hold values from -6 to 6
- seg_lengths: int32 [2, 32, 4], P(None, ('dp', 'fsdp')), may hold values from 1 to 400, as said below
- retrieved: int32 [2, 32, 4, 5], P(None, ('dp', 'fsdp')), may hold values from 0 to 255, as said below
- encoder_states: bfloat16 [256, 64, 1024], P(('dp', 'fsdp')), may hold values from -6 to 6
- master_weights: float32 [1024, 16384], P(None, ('dp', 'fsdp')), as said below
- first_moment: float32 [1024, 16384], P(None, ('dp', 'fsdp')), may hold values from -40 to 40
- second_moment: float32 [1024, 16384], P(None, ('dp', 'fsdp')), may hold values from 2.94912 to 11.79648
- slot_block: int32 [128], replicated, may hold values from 0 to 127, as said below
- bases: float32 [10, 1024, 1024], replicated, may hold values from -0.1875 to 0.1875
- vector_params: float32 [17, 1024], P(None, ('dp', 'fsdp')), as said below
- vector_first: float32 [17, 1024], P(None, ('dp', 'fsdp')), may hold values from -40 to 40
- vector_second: float32 [17, 1024], P(None, ('dp', 'fsdp')), may hold values from 2.94912 to 11.79648
Outputs:
- block_out: bfloat16 [2, 32, 512, 1024], P(None, ('dp', 'fsdp'))
- hidden_grad: bfloat16 [2, 32, 512, 1024], P(None, ('dp', 'fsdp'))
- encoder_grad: bfloat16 [256, 64, 1024], P(('dp', 'fsdp'))
- new_first: float32 [1024, 16384], P(None, ('dp', 'fsdp'))
- new_second: float32 [1024, 16384], P(None, ('dp', 'fsdp'))
- new_master: float32 [1024, 16384], P(None, ('dp', 'fsdp'))
- vector_first_new: float32 [17, 1024], P(None, ('dp', 'fsdp'))
- vector_second_new: float32 [17, 1024], P(None, ('dp', 'fsdp'))
- vector_new: float32 [17, 1024], P(None, ('dp', 'fsdp'))
- vector_grad: float32 [17, 1024], P(None, ('dp', 'fsdp'))
Inputs may be any that keep to these rules, and one draw needn't show every extreme that they name: `seg_lengths`: each row's 4 lengths sum to 512; the first row holds a segment of 400. `retrieved`: A row's passages lie among the 32 passages of the rows' index of dp, in order of devices. `slot_block`: A permutation of the 128 blocks. `master_weights`: entries of order of the weights' spread. `vector_params`: gains near 1, biases of order a third.
All inputs are finite; a program needn't handle non-finite values.
Results may differ from a plain program's by a relative error of at most 0.022.
The roundings to bfloat16 on the way count: a program that leaves them out, or rounds other values in their place, can miss the bound.
Values may be sent and summed in bfloat16 or wider, within the bound.
No kernel may reach another device: no remote copies, remote signals or barrier semaphores. Data moves between devices by JAX's collectives and lax.ppermute only.
A program may use at most 576 MiB of HBM per device.

v0:
```python
import jax
import jax.numpy as jnp
from jax import lax
from jax.sharding import PartitionSpec as P

HD = 64
STEP = 5


HIGH = lax.Precision.HIGHEST
eps_norm = 1e-05
beta_one = 0.9
beta_two = 0.999
adam_eps = 1e-08
rate_mat = 0.03
rate_vec = 0.25
decay = 0.01
neg_big = -1e30
head_group = 4


def product(left, right):
    return jnp.dot(left, right, preferred_element_type=jnp.float32)


def product_tn(left, right):
    return lax.dot_general(
        left, right, (((0,), (0,)), ((), ())), preferred_element_type=jnp.float32
    )


def product_nt(left, right):
    return lax.dot_general(
        left, right, (((1,), (1,)), ((), ())), preferred_element_type=jnp.float32
    )


def norm_forward(resid, gain, shift):
    mean_row = jnp.mean(resid, axis=-1, keepdims=True)
    centred = resid - mean_row
    inv = lax.rsqrt(jnp.mean(centred * centred, axis=-1, keepdims=True) + eps_norm)
    normed = centred * inv
    return (normed * gain + shift, normed, inv)


def norm_backward(grad_out, normed, inv, gain):
    scaled = grad_out * gain
    grad_in = inv * (
        scaled
        - jnp.mean(scaled, axis=-1, keepdims=True)
        - normed * jnp.mean(scaled * normed, axis=-1, keepdims=True)
    )
    return (grad_in, jnp.sum(grad_out * normed, axis=0), jnp.sum(grad_out, axis=0))


def head_slices(query, keys, values, first, count):
    rows = query.shape[0]
    width = keys.shape[0]
    cols = slice(first * HD, (first + count) * HD)
    return (
        query[:, cols].reshape(rows, count, HD),
        keys[:, cols].reshape(width, count, HD),
        values[:, cols].reshape(width, count, HD),
    )


def masked_scores(q_heads, k_heads, allowed):
    scores = jnp.einsum(
        "thd,shd->hts", q_heads, k_heads, preferred_element_type=jnp.float32
    ) * HD ** (-0.5)
    return jnp.where(allowed[None], scores, neg_big)


def attend_forward(query, keys, values, allowed):
    rows = query.shape[0]
    heads = query.shape[1] // HD
    outputs = []
    logsums = []
    for first in range(0, heads, head_group):
        count = min(head_group, heads - first)
        q_heads, k_heads, v_heads = head_slices(query, keys, values, first, count)
        scores = masked_scores(q_heads, k_heads, allowed)
        top = jnp.max(scores, axis=-1, keepdims=True)
        expo = jnp.exp(scores - top)
        total = jnp.sum(expo, axis=-1, keepdims=True)
        probs = (expo / total).astype(jnp.bfloat16)
        out = jnp.einsum("hts,shd->thd", probs, v_heads, preferred_element_type=jnp.float32)
        outputs.append(out.reshape(rows, count * HD))
        logsums.append(top + jnp.log(total))
    return (jnp.concatenate(outputs, axis=1).astype(jnp.bfloat16), logsums)


def attend_backward(query, keys, values, allowed, logsums, grad_out):
    rows = query.shape[0]
    width = keys.shape[0]
    heads = query.shape[1] // HD
    grads_q = []
    grads_k = []
    grads_v = []
    for index, first in enumerate(range(0, heads, head_group)):
        count = min(head_group, heads - first)
        q_heads, k_heads, v_heads = head_slices(query, keys, values, first, count)
        scores = masked_scores(q_heads, k_heads, allowed)
        probs = jnp.exp(scores - logsums[index])
        g_heads = grad_out[:, first * HD : (first + count) * HD].reshape(rows, count, HD)
        grad_probs = jnp.einsum(
            "thd,shd->hts", g_heads, v_heads, preferred_element_type=jnp.float32
        )
        delta = jnp.sum(probs * grad_probs, axis=-1, keepdims=True)
        grad_scores = (probs * (grad_probs - delta)).astype(jnp.bfloat16)
        g_query = jnp.einsum(
            "hts,shd->thd", grad_scores, k_heads, preferred_element_type=jnp.float32
        ) * HD ** (-0.5)
        g_keys = jnp.einsum(
            "hts,thd->shd", grad_scores, q_heads, preferred_element_type=jnp.float32
        ) * HD ** (-0.5)
        g_values = jnp.einsum(
            "hts,thd->shd", probs.astype(jnp.bfloat16), g_heads, preferred_element_type=jnp.float32
        )
        grads_q.append(g_query.reshape(rows, count * HD))
        grads_k.append(g_keys.reshape(width, count * HD))
        grads_v.append(g_values.reshape(width, count * HD))
    return (
        jnp.concatenate(grads_q, axis=1).astype(jnp.bfloat16),
        jnp.concatenate(grads_k, axis=1).astype(jnp.bfloat16),
        jnp.concatenate(grads_v, axis=1).astype(jnp.bfloat16),
    )


def gelu_slope(upper):
    cdf = 0.5 * (1.0 + jax.scipy.special.erf(upper * 2.0 ** (-0.5)))
    dens = jnp.exp(-0.5 * upper * upper) * (2.0 * jnp.pi) ** (-0.5)
    return cdf + upper * dens


def row_forward(mats, vecs, x_row, enc_row, allowed_self, allowed_cross):
    w_q, w_k, w_v, w_o, c_q, c_k, c_v, c_o, w_up, w_downt = mats
    b_up = vecs[13:].reshape(-1)
    query = (product(x_row, w_q) + vecs[0]).astype(jnp.bfloat16)
    keys = product(x_row, w_k).astype(jnp.bfloat16)
    values = (product(x_row, w_v) + vecs[1]).astype(jnp.bfloat16)
    attn_self, lse_self = attend_forward(query, keys, values, allowed_self)
    resid_one = x_row.astype(jnp.float32) + product(attn_self, w_o) + vecs[2]
    hid_one, normed_one, inv_one = norm_forward(resid_one, vecs[3], vecs[4])
    hid_low = hid_one.astype(jnp.bfloat16)
    c_query = (product(hid_low, c_q) + vecs[5]).astype(jnp.bfloat16)
    c_keys = product(enc_row, c_k).astype(jnp.bfloat16)
    c_values = (product(enc_row, c_v) + vecs[6]).astype(jnp.bfloat16)
    attn_cross, lse_cross = attend_forward(c_query, c_keys, c_values, allowed_cross)
    resid_two = hid_one + product(attn_cross, c_o) + vecs[7]
    hid_two, normed_two, inv_two = norm_forward(resid_two, vecs[8], vecs[9])
    hid_two_low = hid_two.astype(jnp.bfloat16)
    upper = product(hid_two_low, w_up) + b_up
    act = jax.nn.gelu(upper, approximate=False).astype(jnp.bfloat16)
    resid_three = hid_two + product_nt(act, w_downt) + vecs[10]
    out, normed_three, inv_three = norm_forward(resid_three, vecs[11], vecs[12])
    saved = (
        query,
        keys,
        values,
        attn_self,
        lse_self,
        normed_one,
        inv_one,
        hid_low,
        c_query,
        c_keys,
        c_values,
        attn_cross,
        lse_cross,
        normed_two,
        inv_two,
        hid_two_low,
        upper,
        act,
        normed_three,
        inv_three,
    )
    return (out.astype(jnp.bfloat16), saved)


def row_backward(mats, vecs, x_row, enc_row, allowed_self, allowed_cross, saved, cot_row):
    w_q, w_k, w_v, w_o, c_q, c_k, c_v, c_o, w_up, w_downt = mats
    (
        query,
        keys,
        values,
        attn_self,
        lse_self,
        normed_one,
        inv_one,
        hid_low,
        c_query,
        c_keys,
        c_values,
        attn_cross,
        lse_cross,
        normed_two,
        inv_two,
        hid_two_low,
        upper,
        act,
        normed_three,
        inv_three,
    ) = saved
    d_resid3, d_g3, d_e3 = norm_backward(
        cot_row.astype(jnp.float32), normed_three, inv_three, vecs[11]
    )
    d_branch3 = d_resid3.astype(jnp.bfloat16)
    d_bdown = jnp.sum(d_branch3.astype(jnp.float32), axis=0)
    d_wdownt = product_tn(d_branch3, act)
    d_act = product(d_branch3, w_downt)
    d_upper = (d_act * gelu_slope(upper)).astype(jnp.bfloat16)
    d_bup = jnp.sum(d_upper.astype(jnp.float32), axis=0)
    d_wup = product_tn(hid_two_low, d_upper)
    d_hid_two = d_resid3 + product_nt(d_upper, w_up)
    d_resid2, d_g2, d_e2 = norm_backward(d_hid_two, normed_two, inv_two, vecs[8])
    d_branch2 = d_resid2.astype(jnp.bfloat16)
    d_cbo = jnp.sum(d_branch2.astype(jnp.float32), axis=0)
    d_co = product_tn(attn_cross, d_branch2)
    d_attn_cross = product_nt(d_branch2, c_o).astype(jnp.bfloat16)
    g_cq, g_ck, g_cv = attend_backward(
        c_query, c_keys, c_values, allowed_cross, lse_cross, d_attn_cross
    )
    d_cbq = jnp.sum(g_cq.astype(jnp.float32), axis=0)
    d_cbv = jnp.sum(g_cv.astype(jnp.float32), axis=0)
    d_cq = product_tn(hid_low, g_cq)
    d_ck = product_tn(enc_row, g_ck)
    d_cv = product_tn(enc_row, g_cv)
    d_enc = product_nt(g_ck, c_k) + product_nt(g_cv, c_v)
    d_hid_one = d_resid2 + product_nt(g_cq, c_q)
    d_resid1, d_g1, d_e1 = norm_backward(d_hid_one, normed_one, inv_one, vecs[3])
    d_branch1 = d_resid1.astype(jnp.bfloat16)
    d_bo = jnp.sum(d_branch1.astype(jnp.float32), axis=0)
    d_wo = product_tn(attn_self, d_branch1)
    d_attn_self = product_nt(d_branch1, w_o).astype(jnp.bfloat16)
    g_q, g_k, g_v = attend_backward(query, keys, values, allowed_self, lse_self, d_attn_self)
    d_bq = jnp.sum(g_q.astype(jnp.float32), axis=0)
    d_bv = jnp.sum(g_v.astype(jnp.float32), axis=0)
    d_wq = product_tn(x_row, g_q)
    d_wk = product_tn(x_row, g_k)
    d_wv = product_tn(x_row, g_v)
    d_x = d_resid1 + product_nt(g_q, w_q) + product_nt(g_k, w_k) + product_nt(g_v, w_v)
    mat_grads = [d_wq, d_wk, d_wv, d_wo, d_cq, d_ck, d_cv, d_co, d_wup, d_wdownt]
    head_rows = jnp.stack(
        [d_bq, d_bv, d_bo, d_g1, d_e1, d_cbq, d_cbv, d_cbo, d_g2, d_e2, d_bdown, d_g3, d_e3], axis=0
    )
    vec_grad = jnp.concatenate([head_rows, d_bup.reshape(-1, head_rows.shape[1])], axis=0)
    return (d_x, d_enc, mat_grads, vec_grad)


def natural_order(gathered, inverse, block_cols):
    wide, vecs = gathered
    width = wide.shape[0]
    blocks = wide.reshape(width, -1, block_cols)
    wide = jnp.take(blocks, inverse, axis=1).reshape(width, -1)
    hidden = (wide.shape[1] - 8 * width) // 2
    mats = [wide[:, j * width : (j + 1) * width] for j in range(8)]
    mats = mats + [wide[:, 8 * width : 8 * width + hidden], wide[:, 8 * width + hidden :]]
    return (tuple(mats), vecs.astype(jnp.float32))


def slot_layout(mat_grads, slot_block, block_cols):
    whole = jnp.concatenate(mat_grads, axis=1)
    width = whole.shape[0]
    return jnp.take(whole.reshape(width, -1, block_cols), slot_block, axis=1).reshape(width, -1)


def shards(
    hidden_in,
    cotangent,
    seg_lengths,
    retrieved,
    encoder_states,
    master_weights,
    first_moment,
    second_moment,
    slot_block,
    bases,
    vector_params,
    vector_first,
    vector_second,
):
    micro, rows_dev, row_len, width = hidden_in.shape
    segs = seg_lengths.shape[2]
    nret = retrieved.shape[3]
    enc_len = encoder_states.shape[1]
    pass_grp = encoder_states.shape[0] * lax.axis_size("fsdp")
    nblk = slot_block.shape[0]
    cols = master_weights.shape[1] * lax.axis_size(("dp", "fsdp"))
    block_cols = cols // nblk
    per_dev = master_weights.shape[1] // block_cols
    local_ids = retrieved.reshape(-1) - lax.axis_index("dp") * pass_grp
    needed = local_ids.shape[0]
    inverse = jnp.zeros((nblk,), jnp.int32).at[slot_block].set(jnp.arange(nblk, dtype=jnp.int32))
    piece = lax.all_gather(encoder_states, "fsdp", axis=0, tiled=True)
    ids_here = jnp.arange(piece.shape[0], dtype=jnp.int32)
    onehot = (local_ids[:, None] == ids_here[None, :]).astype(jnp.bfloat16)
    taken = jnp.dot(onehot, piece.reshape(piece.shape[0], -1), preferred_element_type=jnp.float32)
    chosen = taken.reshape(jnp.zeros((needed, enc_len, width), jnp.bfloat16).shape).astype(
        jnp.bfloat16
    )
    send_wide = master_weights.astype(jnp.bfloat16)
    send_vecs = vector_params.astype(jnp.bfloat16)
    position = jnp.arange(row_len, dtype=jnp.int32)
    key_seg = jnp.arange(segs * nret * enc_len, dtype=jnp.int32) // (nret * enc_len)
    outs_y = []
    outs_dx = []
    enc_grads = []
    share_mat = None
    share_vec = None
    for mb in range(micro):
        fwd_mats, fwd_vecs = natural_order(
            (
                lax.all_gather(send_wide, ("dp", "fsdp"), axis=1, tiled=True),
                lax.all_gather(send_vecs, ("dp", "fsdp"), axis=1, tiled=True),
            ),
            inverse,
            block_cols,
        )
        rr = 0
        ends = jnp.cumsum(seg_lengths[mb, rr])
        qseg = jnp.sum((position[:, None] >= ends[None, :-1]).astype(jnp.int32), axis=1)
        allowed_self = (qseg[:, None] == qseg[None, :]) & (position[:, None] >= position[None, :])
        allowed_cross = qseg[:, None] == key_seg[None, :]
        first_pass = (mb * rows_dev + rr) * segs * nret
        enc_row = chosen[first_pass : first_pass + segs * nret].reshape(-1, width)
        y_row, saved = row_forward(
            fwd_mats, fwd_vecs, hidden_in[mb, rr], enc_row, allowed_self, allowed_cross
        )
        outs_y.append(y_row)
        rows_info = [(allowed_self, allowed_cross, enc_row, saved)]
        bwd_mats, bwd_vecs = natural_order(
            (
                lax.all_gather(send_wide, ("dp", "fsdp"), axis=1, tiled=True),
                lax.all_gather(send_vecs, ("dp", "fsdp"), axis=1, tiled=True),
            ),
            inverse,
            block_cols,
        )
        mb_mat = None
        mb_vec = None
        rr = 0
        allowed_self, allowed_cross, enc_row, saved = rows_info[rr]
        d_x, d_enc, mat_grads, vec_grad = row_backward(
            bwd_mats,
            bwd_vecs,
            hidden_in[mb, rr],
            enc_row,
            allowed_self,
            allowed_cross,
            saved,
            cotangent[mb, rr],
        )
        outs_dx.append(d_x.astype(jnp.bfloat16))
        enc_grads.append(d_enc.reshape(segs * nret, enc_len, width))
        mb_mat = mat_grads
        mb_vec = vec_grad
        part_mat, part_vec = (
            lax.psum_scatter(
                slot_layout(mb_mat, slot_block, block_cols),
                ("dp", "fsdp"),
                scatter_dimension=1,
                tiled=True,
            ),
            lax.psum_scatter(mb_vec, ("dp", "fsdp"), scatter_dimension=1, tiled=True),
        )
        if share_mat is None:
            share_mat, share_vec = (part_mat, part_vec)
        else:
            share_mat = share_mat + part_mat
            share_vec = share_vec + part_vec
    enc_sel = jnp.concatenate(enc_grads, axis=0).reshape(needed, -1)
    count = encoder_states.shape[0] * lax.axis_size("fsdp")
    ids_here = jnp.arange(count, dtype=jnp.int32)
    onehot = (local_ids[:, None] == ids_here[None, :]).astype(jnp.float32)
    term = lax.dot_general(
        onehot,
        enc_sel,
        (((0,), (0,)), ((), ())),
        precision=HIGH,
        preferred_element_type=jnp.float32,
    )
    encoder_grad = lax.psum_scatter(
        term.reshape(count, enc_len, width).astype(jnp.bfloat16),
        "fsdp",
        scatter_dimension=0,
        tiled=True,
    )
    my_slots = lax.axis_index(("dp", "fsdp")) * per_dev + jnp.arange(per_dev, dtype=jnp.int32)
    my_blocks = jnp.take(slot_block, my_slots)
    hidden = (cols - 8 * width) // 2
    bounds = jnp.array([width * j for j in range(1, 9)] + [8 * width + hidden], jnp.int32)
    which = jnp.sum((my_blocks[:, None] * block_cols >= bounds[None, :]).astype(jnp.int32), axis=1)
    my_bases = jnp.take(bases, which, axis=0)
    corr_one = 1.0 - beta_one**STEP
    corr_two = 1.0 - beta_two**STEP
    grad_blocks = share_mat.reshape(width, per_dev, block_cols)
    turned = jnp.einsum(
        "ndk,dnb->knb", my_bases, grad_blocks, precision=HIGH, preferred_element_type=jnp.float32
    )
    first_new = (
        beta_one * first_moment.reshape(width, per_dev, block_cols) + (1.0 - beta_one) * turned
    )
    second_new = (
        beta_two * second_moment.reshape(width, per_dev, block_cols)
        + (1.0 - beta_two) * turned * turned
    )
    step = first_new / corr_one / (jnp.sqrt(second_new / corr_two) + adam_eps)
    back = jnp.einsum(
        "ndk,knb->dnb", my_bases, step, precision=HIGH, preferred_element_type=jnp.float32
    )
    master_new = master_weights - rate_mat * (back.reshape(width, -1) + decay * master_weights)
    vf_new = beta_one * vector_first + (1.0 - beta_one) * share_vec
    vs_new = beta_two * vector_second + (1.0 - beta_two) * share_vec * share_vec
    vec_new = vector_params - rate_vec * (vf_new / corr_one) / (
        jnp.sqrt(vs_new / corr_two) + adam_eps
    )
    block_out = jnp.stack(outs_y, axis=0).reshape(micro, rows_dev, row_len, width)
    hidden_grad = jnp.stack(outs_dx, axis=0).reshape(micro, rows_dev, row_len, width)
    return (
        block_out,
        hidden_grad,
        encoder_grad,
        first_new.reshape(width, -1),
        second_new.reshape(width, -1),
        master_new,
        vf_new,
        vs_new,
        vec_new,
        share_vec,
    )


def solution(mesh):
    in_specs = (
        P(None, ("dp", "fsdp"), None, None),
        P(None, ("dp", "fsdp"), None, None),
        P(None, ("dp", "fsdp"), None),
        P(None, ("dp", "fsdp"), None, None),
        P(("dp", "fsdp"), None, None),
        P(None, ("dp", "fsdp")),
        P(None, ("dp", "fsdp")),
        P(None, ("dp", "fsdp")),
        P(),
        P(),
        P(None, ("dp", "fsdp")),
        P(None, ("dp", "fsdp")),
        P(None, ("dp", "fsdp")),
    )
    out_specs = (
        P(None, ("dp", "fsdp"), None, None),
        P(None, ("dp", "fsdp"), None, None),
        P(("dp", "fsdp"), None, None),
        P(None, ("dp", "fsdp")),
        P(None, ("dp", "fsdp")),
        P(None, ("dp", "fsdp")),
        P(None, ("dp", "fsdp")),
        P(None, ("dp", "fsdp")),
        P(None, ("dp", "fsdp")),
        P(None, ("dp", "fsdp")),
    )
    return jax.shard_map(shards, mesh=mesh, in_specs=in_specs, out_specs=out_specs, check_vma=False)
```

profile of v0, /device:TPU:0, one launch (start us, length us, event | category | flops | bytes accessed | tf_op | source)
XLA Modules:
  0.0 2247.9 jit_solution(3157157080465597757)
XLA Ops:
  11.1 44.3 %all-gather = bf16[32,32,17]{1,2,0:T(8,128)(2,1)S(1)} all-gather(bf16[1,32,17]{1,2,0:T(8,128)(2,1)S(1)} %convert_bitcast_fusion.3), channel_id=1, replica_groups=mesh['dp'=8,'fsdp'=4] {'dp','fsdp'}, dimensions={0}, use_global_device_ids=true | all-gather | bytes 35904 | tf_op jit(solution)/shard_map/all_gather | solution.py:316
  63.1 8.2 fusion.122
  77.5 169.1 %all-gather.4.cloned.1.call-done = bf16[1024,16384]{0,1:T(8,128)(2,1)} async-done(((bf16[1024,512]{0,1:T(8,128)(2,1)}), bf16[1024,16384]{0,1:T(8,128)(2,1)}) %all-gather.4.cloned.1.call-update) | async-done | bytes 33554448 | tf_op jit(solution)/shard_map/all_gather | solution.py:315
  246.5 44.2 %copy.490 = bf16[1024,128,128]{2,0,1:T(8,128)(2,1)} copy(bf16[1024,128,128]{0,2,1:T(8,128)(2,1)} %bitcast.731) | data formatting | bytes 67108864 | tf_op jit(solution)/shard_map/reshape | solution.py:255
  290.8 22.9 %gather_fusion.3 = bf16[128,1024,128]{2,1,0:T(8,128)(2,1)} fusion(bf16[1024,128,128]{2,0,1:T(8,128)(2,1)} %copy.490, s32[1024]{0:T(1024)S(1)} %pad_clamp_fusion.3), kind=kCustom, calls=%fused_computation.clone | custom fusion | bytes 67109376 | tf_op jit(solution)/shard_map/jit(_take)/gather | solution.py:256
  313.6 22.8 %select_bitcast_fusion = bf16[1024,128,128]{2,0,1:T(8,128)(2,1)} fusion(bf16[128,1024,128]{2,1,0:T(8,128)(2,1)} %gather_fusion.3, pred[128]{0:T(512)(128)(4,1)S(1)} %compare_and_fusion.1), kind=kLoop, calls=%fused_computation.10 | loop fusion | flops 16777216 | bytes 67108992 | tf_op jit(solution)/shard_map/jit(_take)/select_n | solution.py:256
  336.5 44.0 %copy.491 = bf16[1024,128,128]{0,2,1:T(8,128)(2,1)} copy(bf16[1024,128,128]{2,0,1:T(8,128)(2,1)} %select_bitcast_fusion) | data formatting | bytes 67108864 | tf_op jit(solution)/shard_map/jit(_take)/select_n | solution.py:256
  570.5 10.7 fusion.67
  581.2 44.2 %fusion.15 = (bf16[512,4096]{1,0:T(8,128)(2,1)S(1)}, bf16[512,4096]{1,0:T(8,128)(2,1)S(1)}, f32[512,4096]{1,0:T(8,128)}) fusion(f32[4096]{0:T(1024)S(1)} %bitcast.1044, f32[512,4096]{1,0:T(8,128)} %fusion.67, bf16[1024,16384]{0,1:T(8,128)(2,1)} %bitcast.699, f32[512,1024]{1,0:T(8,128)S(1)} %get-tuple-element.234, f32[1024]{0:T(1024)S(1)} %bitcast.1050, ...), kind=kOutput, calls=%fused_computation.84 | convolution fusion | flops 4574412800 | bytes 35680256 | tf_op jit(solution)/shard_map/dot_general | solution.py:23
  625.4 10.4 fusion.470
  650.1 14.1 convert_reduce_fusion
  664.3 11.4 convert_reduce_fusion.1
  675.7 9.7 multiply_reduce_fusion.18
  685.5 12.1 convert_reduce_fusion.13
  1088.6 8.5 convolution_dynamic-update-slice_fusion.1
  1097.1 8.2 convolution_dynamic-update-slice_fusion
  1105.3 44.5 %copy_bitcast_fusion = f32[1024,128,128]{2,0,1:T(8,128)} fusion(f32[1024,16384]{1,0:T(8,128)} %convolution_dynamic-update-slice_fusion), kind=kLoop, calls=%fused_computation.7 | loop fusion | bytes 134217728 | tf_op jit(solution)/shard_map/reshape | solution.py:266
  1185.8 8.5 convolution_dynamic-update-slice_fusion.3
  1194.4 8.4 convolution_dynamic-update-slice_fusion.2
  1202.7 9.4 pad_maximum_fusion
  1212.1 8.7 convert_bitcast_fusion
  1223.3 45.8 %copy_bitcast_fusion.1 = f32[1024,128,128]{2,0,1:T(8,128)} fusion(f32[1024,16384]{1,0:T(8,128)} %convolution_dynamic-update-slice_fusion.2), kind=kLoop, calls=%fused_computation.8 | loop fusion | bytes 134217728 | tf_op jit(solution)/shard_map/reshape | solution.py:266
  1269.1 44.7 %gather_fusion.5 = f32[128,1024,128]{2,1,0:T(8,128)} fusion(f32[1024,128,128]{2,0,1:T(8,128)} %copy_bitcast_fusion, s32[1024]{0:T(1024)} %get-tuple-element.301), kind=kCustom, calls=%fused_computation.2.clone | custom fusion | bytes 134218240 | tf_op jit(solution)/shard_map/jit(_take)/gather | solution.py:266
  1313.8 44.9 %gather_fusion.4 = f32[128,1024,128]{2,1,0:T(8,128)} fusion(f32[1024,128,128]{2,0,1:T(8,128)} %copy_bitcast_fusion.1, s32[1024]{0:T(1024)} %get-tuple-element.301), kind=kCustom, calls=%fused_computation.1.clone | custom fusion | bytes 134218240 | tf_op jit(solution)/shard_map/jit(_take)/gather | solution.py:266
  1358.7 64.6 %bitcast_add_fusion = f32[1024,128,128]{2,0,1:T(8,128)} fusion(f32[128,1024,128]{2,1,0:T(8,128)} %gather_fusion.5, f32[128,1024,128]{2,1,0:T(8,128)} %gather_fusion.4, pred[128]{0:T(512)(128)(4,1)S(1)} %copy-done.331), kind=kLoop, calls=%fused_computation.9 | loop fusion | flops 50331648 | bytes 201326720 | tf_op jit(solution)/shard_map/add | solution.py:371
  1423.3 65.9 %copy.572 = f32[1024,128,128]{0,2,1:T(8,128)} copy(f32[1024,128,128]{2,0,1:T(8,128)} %bitcast_add_fusion) | data formatting | bytes 134217728 | tf_op jit(solution)/shard_map/add | solution.py:371
  1500.6 30.7 %fusion.431 = (f32[10,512,1024]{2,1,0:T(8,128)}, f32[10,512,1024]{2,1,0:T(8,128)}) fusion(f32[10,1024,1024]{2,1,0:T(8,128)} %param.27), kind=kLoop, calls=%fused_computation.730 | loop fusion | bytes 83886080 | tf_op jit(solution)/shard_map/jit(_take)/gather | solution.py:395
  1531.4 11.5 gather_fusion.1
  1542.9 11.7 gather_fusion.2
  1581.6 608.8 %reduce-scatter.8.cloned.1.call-done = f32[1024,512]{0,1:T(8,128)} async-done(((f32[1024,16384]{0,1:T(8,128)}), f32[1024,512]{0,1:T(8,128)}) %reduce-scatter.8.cloned.1.call-update) | async-done | bytes 2097168 | tf_op jit(solution)/shard_map/reduce_scatter | solution.py:360
  2190.4 15.0 fusion.177
  2205.4 24.2 %fusion = f32[4,128,1024]{2,1,0:T(8,128)} fusion(f32[4,512,1024]{2,1,0:T(8,128)} %gather_fusion.2, f32[4,512,1024]{2,1,0:T(8,128)} %gather_fusion.1, pred[4]{0:T(512)(128)(4,1)S(1)} %compare_and_fusion.2, f32[1024,4,128]{0,2,1:T(8,128)S(1)} %get-tuple-element.138, f32[1024,4,128]{0,2,1:T(8,128)S(1)} %get-tuple-element.139), kind=kOutput, calls=%fused_computation.12 | convolution fusion | flops 6452936704 | bytes 23068676 | tf_op jit(solution)/shard_map/ndk,knb->dnb/dot_general | solution.py:410
  (1182 shorter events, 696.3 us)
Async XLA Ops:
  7.2 49.0 %copy-start = (s32[128]{0:T(128)S(1)}, s32[128]{0:T(128)}, u32[]{:S(2)}) copy-start(s32[128]{0:T(128)} %param.26) | copy-start | bytes 1540
  7.2 50.7 %copy-start.27 = (bf16[2,1,512,1024]{3,2,1,0:T(8,128)(2,1)S(1)}, bf16[2,1,512,1024]{3,2,1,0:T(8,128)(2,1)}, u32[]{:S(2)}) copy-start(bf16[2,1,512,1024]{3,2,1,0:T(8,128)(2,1)} %param.19) | copy-start | bytes 6291460
  7.2 55.8 %all-gather.6.cloned.1.call-start = ((), (), s32[]{:S(2)}) async-start(), calls=%async_computation.4 | async-start | bytes 5242880 | tf_op jit(solution)/shard_map/all_gather | solution.py:296
  8.0 238.6 %all-gather.4.cloned.1.call-start = ((), (), s32[]{:S(2)}) async-start(), calls=%async_computation.3 | async-start | bytes 34603008 | tf_op jit(solution)/shard_map/all_gather | solution.py:315
  10.6 1566.8 %reduce-scatter.12.cloned.1.call-start = ((), (), s32[]{:S(2)}) async-start(), calls=%async_computation.7 | async-start | bytes 540672
  11.1 60.2 %copy-start.306 = (s32[40]{0:T(128)}, s32[40]{0:T(128)S(1)}, u32[]{:S(2)}) copy-start(s32[40]{0:T(128)S(1)} %sub.537) | copy-start | bytes 484
  74.5 332.0 %copy-start.92 = (bf16[20,64,1024]{2,1,0:T(8,128)(2,1)}, bf16[20,64,1024]{2,1,0:T(8,128)(2,1)S(1)}, u32[]{:S(2)}) copy-start(bf16[20,64,1024]{2,1,0:T(8,128)(2,1)S(1)} %copy.498) | copy-start | bytes 7864324
  435.7 55.3 %copy-start.45 = (bf16[1280,256]{0,1:T(8,128)(2,1)}, bf16[1280,256]{0,1:T(8,128)(2,1)S(1)}, u32[]{:S(2)}) copy-start(bf16[1280,256]{0,1:T(8,128)(2,1)S(1)} %get-tuple-element.128) | copy-start | bytes 1966084
  478.7 48.3 %copy-start.36 = (f32[512,1024]{1,0:T(8,128)}, f32[512,1024]{1,0:T(8,128)S(1)}, u32[]{:S(2)}) copy-start(f32[512,1024]{1,0:T(8,128)S(1)} %get-tuple-element.244) | copy-start | bytes 6291460
  478.7 48.3 %copy-start.272 = (f32[512]{0:T(512)}, f32[512]{0:T(512)S(1)}, u32[]{:S(2)}) copy-start(f32[512]{0:T(512)S(1)} %broadcast_multiply_fusion.16) | copy-start | bytes 6148
  479.0 47.9 %copy-start.295 = (f32[512]{0:T(512)}, f32[512]{0:T(512)S(1)}, u32[]{:S(2)}) copy-start(f32[512]{0:T(512)S(1)} %add_rsqrt_fusion.2) | copy-start | bytes 6148
  530.6 39.8 %copy-start.38 = (f32[512,1024]{1,0:T(8,128)}, f32[512,1024]{1,0:T(8,128)S(1)}, u32[]{:S(2)}) copy-start(f32[512,1024]{1,0:T(8,128)S(1)} %get-tuple-element.254) | copy-start | bytes 6291460
  530.6 39.8 %copy-start.274 = (f32[512]{0:T(512)}, f32[512]{0:T(512)S(1)}, u32[]{:S(2)}) copy-start(f32[512]{0:T(512)S(1)} %broadcast_multiply_fusion.15) | copy-start | bytes 6148
  531.0 39.4 %copy-start.297 = (f32[512]{0:T(512)}, f32[512]{0:T(512)S(1)}, u32[]{:S(2)}) copy-start(f32[512]{0:T(512)S(1)} %add_rsqrt_fusion.1) | copy-start | bytes 6148
  539.7 26.7 %copy-start.352 = (bf16[4,64,512]{2,1,0:T(8,128)(2,1)}, bf16[4,64,512]{2,1,0:T(8,128)(2,1)S(1)}, u32[]{:S(2)}) copy-start(bf16[4,64,512]{2,1,0:T(8,128)(2,1)S(1)} %fusion.338) | copy-start | bytes 786436
  570.0 115.4 %copy-start.161 = (f32[512,1024]{1,0:T(8,128)}, f32[512,1024]{1,0:T(8,128)S(1)}, u32[]{:S(2)}) copy-start(f32[512,1024]{1,0:T(8,128)S(1)} %get-tuple-element.234) | copy-start | bytes 6291460
  570.1 115.4 %copy-start.304 = (f32[512]{0:T(512)}, f32[512]{0:T(512)S(1)}, u32[]{:S(2)}) copy-start(f32[512]{0:T(512)S(1)} %broadcast_multiply_fusion.18) | copy-start | bytes 6148
  570.4 115.0 %copy-start.328 = (f32[512]{0:T(512)}, f32[512]{0:T(512)S(1)}, u32[]{:S(2)}) copy-start(f32[512]{0:T(512)S(1)} %add_rsqrt_fusion.4) | copy-start | bytes 6148
  581.2 44.2 %copy-start.313 = (f32[1,1024]{1,0:T(1,128)S(1)}, f32[1,1024]{1,0:T(1,128)}, u32[]{:S(2)}) copy-start(f32[1,1024]{1,0:T(1,128)} %get-tuple-element.190) | copy-start | bytes 12292
  650.1 35.3 %copy-start.165 = (f32[512,1024]{1,0:T(8,128)}, f32[512,1024]{1,0:T(8,128)S(1)}, u32[]{:S(2)}) copy-start(f32[512,1024]{1,0:T(8,128)S(1)} %get-tuple-element.102) | copy-start | bytes 6291460
  718.2 58.9 %copy-start.170 = (bf16[4,64,512]{2,1,0:T(8,128)(2,1)}, bf16[4,64,512]{2,1,0:T(8,128)(2,1)S(1)}, u32[]{:S(2)}) copy-start(bf16[4,64,512]{2,1,0:T(8,128)(2,1)S(1)} %fusion.276) | copy-start | bytes 786436
  736.8 40.3 %copy-start.172 = (bf16[4,64,512]{2,1,0:T(8,128)(2,1)}, bf16[4,64,512]{2,1,0:T(8,128)(2,1)S(1)}, u32[]{:S(2)}) copy-start(bf16[4,64,512]{2,1,0:T(8,128)(2,1)S(1)} %fusion.279) | copy-start | bytes 786436
  804.6 58.4 %copy-start.196 = (bf16[4,64,512]{2,1,0:T(8,128)(2,1)}, bf16[4,64,512]{2,1,0:T(8,128)(2,1)S(1)}, u32[]{:S(2)}) copy-start(bf16[4,64,512]{2,1,0:T(8,128)(2,1)S(1)} %fusion.280) | copy-start | bytes 786436
  823.2 39.8 %copy-start.200 = (bf16[4,64,512]{2,1,0:T(8,128)(2,1)}, bf16[4,64,512]{2,1,0:T(8,128)(2,1)S(1)}, u32[]{:S(2)}) copy-start(bf16[4,64,512]{2,1,0:T(8,128)(2,1)S(1)} %fusion.283) | copy-start | bytes 786436
  877.7 31.0 %copy-start.178 = (bf16[4,64,512]{2,1,0:T(8,128)(2,1)}, bf16[4,64,512]{2,1,0:T(8,128)(2,1)S(1)}, u32[]{:S(2)}) copy-start(bf16[4,64,512]{2,1,0:T(8,128)(2,1)S(1)} %fusion.287) | copy-start | bytes 786436
  881.8 30.4 %copy-start.182 = (bf16[4,64,512]{2,1,0:T(8,128)(2,1)}, bf16[4,64,512]{2,1,0:T(8,128)(2,1)S(1)}, u32[]{:S(2)}) copy-start(bf16[4,64,512]{2,1,0:T(8,128)(2,1)S(1)} %fusion.309) | copy-start | bytes 786436
  924.3 31.6 %copy-start.194 = (bf16[4,64,512]{2,1,0:T(8,128)(2,1)}, bf16[4,64,512]{2,1,0:T(8,128)(2,1)S(1)}, u32[]{:S(2)}) copy-start(bf16[4,64,512]{2,1,0:T(8,128)(2,1)S(1)} %fusion.299) | copy-start | bytes 786436
  928.7 30.5 %copy-start.202 = (bf16[4,64,512]{2,1,0:T(8,128)(2,1)}, bf16[4,64,512]{2,1,0:T(8,128)(2,1)S(1)}, u32[]{:S(2)}) copy-start(bf16[4,64,512]{2,1,0:T(8,128)(2,1)S(1)} %fusion.317) | copy-start | bytes 786436
  1014.2 564.6 %reduce-scatter.10.cloned.1.call-start = ((), (), s32[]{:S(2)}) async-start(), calls=%async_computation.6 | async-start | bytes 5242880
  1223.2 967.1 %reduce-scatter.8.cloned.1.call-start = ((), (), s32[]{:S(2)}) async-start(), calls=%async_computation.5 | async-start | bytes 69206016 | tf_op jit(solution)/shard_map/reduce_scatter | solution.py:360
  1313.8 44.9 %copy-start.331 = (pred[128]{0:T(512)(128)(4,1)S(1)}, pred[128]{0:T(512)(128)(4,1)}, u32[]{:S(2)}) copy-start(pred[128]{0:T(512)(128)(4,1)} %compare_and_fusion) | copy-start | bytes 388
  1578.2 627.2 %copy-start.268 = (f32[17,32]{1,0:T(8,128)}, f32[17,32]{1,0:T(8,128)S(1)}, u32[]{:S(2)}) copy-start(f32[17,32]{1,0:T(8,128)S(1)} %copy.625) | copy-start | bytes 6532
  (380 other events, 1961.9 us)
Sparse Core Ops, SparseCore 0:
  9.6 38.6 all-gather.5
  51.8 194.7 all-gather.3
  1014.3 132.1 reduce-scatter.11
  1223.4 42.9 reduce-scatter.9
  1489.3 701.0 reduce-scatter.7
where the time goes:
time: 2270 us; the launch traced here: 2250 us
  waiting for transfers between devices  779 us (34%)
  matrix products  637 us (28%)
  local copies, waits for them, and re-layouts  570 us (25%)
  other arithmetic  198 us (9%)
  blocking collectives  44.3 us (2%)
    reduce_scatter x1, waiting for transfers between devices, shards(): lax.psum_scatter(slot_layout(mb_mat, slot_block, block_cols), ('dp', 'fsd...  609 us
    all_gather x1, waiting for transfers between devices, shards(): lax.all_gather(send_wide, ('dp', 'fsdp'), axis=1, tiled=True)  169 us
    dot_general x20, matrix products, product(): return jnp.dot(left, right, preferred_element_type=jnp.float32)  137 us
    dot_general x20, matrix products, product_nt(): lax.dot_general(left, right, (((1,), (1,)), ((), ())), preferred_element_...  106 us
    dot_general x20, matrix products, product_tn(): lax.dot_general(left, right, (((0,), (0,)), ((), ())), preferred_element_...  103 us
    reshape x2, local copies, waits for them, and re-layouts, slot_layout(): whole.reshape(width, -1, block_cols)  90.3 us
    gather x2, local copies, waits for them, and re-layouts, slot_layout(): jnp.take(whole.reshape(width, -1, block_cols), slot_block, axis=1)  89.6 us
    dot_general x16, matrix products, attend_backward(): jnp.einsum('hts,thd->shd', probs.astype(jnp.bfloat16), g_heads, preferred...  79.2 us
  transfers between devices with their start and end apart: 5, of which 2 were waited for; matrix products, arithmetic and copies ran while one was open for 26% of the time, Pallas kernels for 0%

commit v1 on v0

v1 whole, which is shorter than its diff:
```python
import functools

import jax
import jax.numpy as jnp
from jax import lax
from jax.experimental import pallas as pl
from jax.experimental.pallas import tpu as pltpu
from jax.sharding import PartitionSpec as P

HD = 64
STEP = 5
NH = 4
TR = 64
AXES = ("dp", "fsdp")
HI = 8

bf = jnp.bfloat16
f32 = jnp.float32
eps_norm = 1e-05
beta_one = 0.9
beta_two = 0.999
adam_eps = 1e-08
rate_mat = 0.03
rate_vec = 0.25
decay = 0.01

def nt(a,b): return lax.dot_general(a,b,(((1,),(1,)),((),())),preferred_element_type=f32)
def nn(a,b): return lax.dot_general(a,b,(((1,),(0,)),((),())),preferred_element_type=f32)
def tn(a,b): return lax.dot_general(a,b,(((0,),(0,)),((),())),preferred_element_type=f32)

def spread(tile, scale):
    lane_head = lax.broadcasted_iota(jnp.int32, tile.shape, 1) // HD
    tile = tile * jnp.asarray(scale, tile.dtype) if scale != 1.0 else tile
    zero = jnp.zeros_like(tile)
    return jnp.concatenate([jnp.where(lane_head == h, tile, zero) for h in range(NH)], axis=0)

def collect(big):
    tr = big.shape[0] // NH
    lane_head = lax.broadcasted_iota(jnp.int32, (tr, big.shape[1]), 1) // HD
    out = big[:tr]
    for h in range(1, NH):
        out = jnp.where(lane_head == h, big[h*tr:(h+1)*tr], out)
    return out

def softmax_t(scores):
    top = jnp.max(scores, axis=0, keepdims=True)
    expo = jnp.exp(scores - top)
    total = jnp.sum(expo, axis=0, keepdims=True)
    return expo * (1.0 / total)

def seg_of(pos, lens_ref, row, segs):
    end = lens_ref[row, 0]
    seg = (pos >= end).astype(jnp.int32)
    for i in range(1, segs - 1):
        end = end + lens_ref[row, i]
        seg = seg + (pos >= end).astype(jnp.int32)
    return seg

def build_bias(bias_ref, lens_ref, row, segs):
    n = bias_ref.shape[0]
    key = lax.broadcasted_iota(jnp.int32, (n, n), 0)
    que = lax.broadcasted_iota(jnp.int32, (n, n), 1)
    kseg = seg_of(lax.broadcasted_iota(jnp.int32, (n, 1), 0), lens_ref, row, segs)
    qseg = seg_of(lax.broadcasted_iota(jnp.int32, (1, n), 1), lens_ref, row, segs)
    ok = (kseg == qseg) & (key <= que)
    bias_ref[...] = jnp.where(ok, 0.0, -1e30)

def bias_tile(bias_ref, first, width, tr):
    piece = bias_ref[:width, first:first+tr]
    return jnp.concatenate([piece]*NH, axis=1)

def self_fwd_kernel(segs, lens_ref, q_ref, k_ref, v_ref, o_ref, bias_ref):
    row = pl.program_id(0)
    n = q_ref.shape[0]
    @pl.when(pl.program_id(1) == 0)
    def _():
        build_bias(bias_ref, lens_ref, row, segs)
    for t in range(n // TR):
        w = (t + 1) * TR
        big = spread(q_ref[t*TR:(t+1)*TR, :], HD ** -0.5)
        s = nt(k_ref[:w, :], big) + bias_tile(bias_ref, t*TR, w, TR)
        p = softmax_t(s).astype(bf)
        o_ref[t*TR:(t+1)*TR, :] = collect(tn(p, v_ref[:w, :])).astype(bf)

def self_fwd(lens, qkv, rows):
    tok, width3 = qkv.shape
    width = width3 // 3
    n = tok // rows
    lanes = NH * HD
    nb = width // lanes
    spec = lambda off: pl.BlockSpec((n, lanes), lambda r, h, *_: (r, off*nb + h))
    return pl.pallas_call(
        functools.partial(self_fwd_kernel, lens.shape[1]),
        grid_spec=pltpu.PrefetchScalarGridSpec(num_scalar_prefetch=1, grid=(rows, nb),
            in_specs=[spec(0), spec(1), spec(2)], out_specs=spec(0),
            scratch_shapes=[pltpu.VMEM((n, n), f32)]),
        out_shape=jax.ShapeDtypeStruct((tok, width), bf),
        compiler_params=pltpu.CompilerParams(vmem_limit_bytes=48<<20),
        cost_estimate=pl.CostEstimate(flops=2*tok*n*width, bytes_accessed=8*tok*width, transcendentals=tok*n*width//HD//2),
    )(lens, qkv, qkv, qkv)

def self_bwd_kernel(segs, lens_ref, q_ref, k_ref, v_ref, g_ref, out_ref, bias_ref, dq_ref, ak_ref, av_ref):
    row = pl.program_id(0)
    part = pl.program_id(2)

    @pl.when((pl.program_id(1) == 0) & (part == 0))
    def _():
        build_bias(bias_ref, lens_ref, row, segs)

    @pl.when(part == 0)
    def _():
        self_bwd_body(q_ref, k_ref, v_ref, g_ref, bias_ref, dq_ref, ak_ref, av_ref)
        out_ref[...] = dq_ref[...]

    @pl.when(part == 1)
    def _():
        out_ref[...] = ak_ref[...].astype(bf)

    @pl.when(part == 2)
    def _():
        out_ref[...] = av_ref[...].astype(bf)

def self_bwd_body(q_ref, k_ref, v_ref, g_ref, bias_ref, dq_ref, ak_ref, av_ref):
    n = q_ref.shape[0]
    for t in reversed(range(n // TR)):
        w = (t + 1) * TR
        big = spread(q_ref[t*TR:(t+1)*TR, :], HD ** -0.5)
        gbig = spread(g_ref[t*TR:(t+1)*TR, :], 1.0)
        k = k_ref[:w, :]
        p = softmax_t(nt(k, big) + bias_tile(bias_ref, t*TR, w, TR))
        u = p * nt(v_ref[:w, :], gbig)
        ds = (u - p * jnp.sum(u, axis=0, keepdims=True)).astype(bf)
        av = nn(p.astype(bf), gbig)
        ak = nn(ds, big)
        if t == n // TR - 1:
            av_ref[...] = av
            ak_ref[...] = ak
        else:
            av_ref[:w, :] += av
            ak_ref[:w, :] += ak
        dq_ref[t*TR:(t+1)*TR, :] = (collect(tn(ds, k)) * HD ** -0.5).astype(bf)

def self_bwd(lens, qkv, grad, rows):
    tok, width3 = qkv.shape
    width = width3 // 3
    n = tok // rows
    lanes = NH * HD
    nb = width // lanes
    spec = lambda off: pl.BlockSpec((n, lanes), lambda r, h, *_: (r, off*nb + h))
    return pl.pallas_call(
        functools.partial(self_bwd_kernel, lens.shape[1]),
        grid_spec=pltpu.PrefetchScalarGridSpec(num_scalar_prefetch=1, grid=(rows, nb, 3),
            in_specs=[spec(0), spec(1), spec(2), spec(0)],
            out_specs=pl.BlockSpec((n, lanes), lambda r, h, p, *_: (r, p*nb + h)),
            scratch_shapes=[pltpu.VMEM((n, n), f32), pltpu.VMEM((n, lanes), bf), pltpu.VMEM((n, lanes), f32), pltpu.VMEM((n, lanes), f32)]),
        out_shape=jax.ShapeDtypeStruct((tok, width3), bf),
        compiler_params=pltpu.CompilerParams(vmem_limit_bytes=48<<20),
        cost_estimate=pl.CostEstimate(flops=5*tok*n*width, bytes_accessed=14*tok*width, transcendentals=tok*n*width//HD//2),
    )(lens, qkv, qkv, qkv, grad)

def seg_bounds(lens_ref, row, segs):
    ends = []
    acc = 0
    for i in range(segs):
        acc = acc + lens_ref[row, i]
        ends.append(acc)
    return ends

def first_seg(ends, pos):
    seg = 0
    for e in ends[:-1]:
        seg = seg + (pos >= e).astype(jnp.int32)
    return seg

def load_keys(ids_ref, row, segs, nret, elen, src_ref, dst_ref):
    for j in range(segs * nret):
        ident = ids_ref[row, j]
        dst_ref[j*elen:(j+1)*elen, :] = src_ref[pl.ds(pl.multiple_of(ident*elen, elen), elen), :]

def lane_seg(ends, t):
    pos = lax.broadcasted_iota(jnp.int32, (1, TR), 1) + t * TR
    seg = jnp.zeros((1, TR), jnp.int32)
    for e in ends[:-1]:
        seg = seg + (pos >= e).astype(jnp.int32)
    return jnp.concatenate([seg]*NH, axis=1)

def row_seg(ends, t, lanes):
    pos = lax.broadcasted_iota(jnp.int32, (TR, 1), 0) + t * TR
    seg = jnp.zeros((TR, 1), jnp.int32)
    for e in ends[:-1]:
        seg = seg + (pos >= e).astype(jnp.int32)
    return seg

def cross_fwd_kernel(segs, nret, elen, lens_ref, ids_ref, q_ref, k_ref, v_ref, o_ref, ks_ref, vs_ref):
    row = pl.program_id(1)
    n = q_ref.shape[0]
    width = nret * elen
    load_keys(ids_ref, row, segs, nret, elen, k_ref, ks_ref)
    load_keys(ids_ref, row, segs, nret, elen, v_ref, vs_ref)
    ends = seg_bounds(lens_ref, row, segs)
    def tile(t, carry):
        rows = pl.ds(pl.multiple_of(t * TR, TR), TR)
        big = spread(q_ref[rows, :], HD ** -0.5)
        lo = first_seg(ends, t * TR)
        hi = first_seg(ends, t * TR + TR - 1)
        qseg = row_seg(ends, t, q_ref.shape[1])
        def pair(s, acc):
            keys = pl.ds(pl.multiple_of(s * width, elen), width)
            p = softmax_t(nt(ks_ref[keys, :], big)).astype(bf)
            got = collect(tn(p, vs_ref[keys, :])).astype(f32)
            return jnp.where(qseg == s, got, acc)
        out = lax.fori_loop(lo, hi + 1, pair, jnp.zeros((TR, q_ref.shape[1]), f32))
        o_ref[rows, :] = out.astype(bf)
        return carry
    lax.fori_loop(0, n // TR, tile, 0)

def cross_fwd(lens, ids, cq, kv, rows, nret, elen):
    tok, width = cq.shape
    n = tok // rows
    lanes = NH * HD
    nb = width // lanes
    segs = lens.shape[1]
    pool = kv.shape[0]
    qspec = pl.BlockSpec((n, lanes), lambda h, r, *_: (r, h))
    kspec = lambda off: pl.BlockSpec((pool, lanes), lambda h, r, *_: (0, off*nb + h))
    keys = segs*nret*elen
    return pl.pallas_call(
        functools.partial(cross_fwd_kernel, segs, nret, elen),
        grid_spec=pltpu.PrefetchScalarGridSpec(num_scalar_prefetch=2, grid=(nb, rows),
            in_specs=[qspec, kspec(0), kspec(1)], out_specs=qspec,
            scratch_shapes=[pltpu.VMEM((keys, lanes), bf)]*2),
        out_shape=jax.ShapeDtypeStruct((tok, width), bf),
        compiler_params=pltpu.CompilerParams(vmem_limit_bytes=48<<20),
        cost_estimate=pl.CostEstimate(flops=2*tok*keys*width, bytes_accessed=8*tok*width, transcendentals=tok*keys*width//HD//2),
    )(lens, ids, cq, kv, kv)

def cross_bwd_kernel(segs, nret, elen, rows_n, lens_ref, ids_ref, q_ref, k_ref, v_ref, g_ref, dq_ref, dkv_ref, ks_ref, vs_ref, ak_ref, av_ref, pk_ref, pv_ref):
    row = pl.program_id(1)

    @pl.when(row < rows_n)
    def _():
        cross_bwd_body(segs, nret, elen, row, lens_ref, ids_ref, q_ref, k_ref, v_ref, g_ref, dq_ref, ks_ref, vs_ref, ak_ref, av_ref, pk_ref, pv_ref)

    @pl.when(row == rows_n - 1)
    def _():
        dkv_ref[...] = pk_ref[...].astype(bf)

    @pl.when(row == rows_n)
    def _():
        dkv_ref[...] = pv_ref[...].astype(bf)

def cross_bwd_body(segs, nret, elen, row, lens_ref, ids_ref, q_ref, k_ref, v_ref, g_ref, dq_ref, ks_ref, vs_ref, ak_ref, av_ref, pk_ref, pv_ref):
    n = q_ref.shape[0]
    width = nret * elen
    load_keys(ids_ref, row, segs, nret, elen, k_ref, ks_ref)
    load_keys(ids_ref, row, segs, nret, elen, v_ref, vs_ref)
    ak_ref[...] = jnp.zeros_like(ak_ref)
    av_ref[...] = jnp.zeros_like(av_ref)
    @pl.when(row == 0)
    def _():
        pk_ref[...] = jnp.zeros_like(pk_ref)
        pv_ref[...] = jnp.zeros_like(pv_ref)
    ends = seg_bounds(lens_ref, row, segs)
    def tile(t, carry):
        rows = pl.ds(pl.multiple_of(t * TR, TR), TR)
        big = spread(q_ref[rows, :], HD ** -0.5)
        gbig = spread(g_ref[rows, :], 1.0)
        lo = first_seg(ends, t * TR)
        hi = first_seg(ends, t * TR + TR - 1)
        qseg = lane_seg(ends, t)
        def pair(s, acc):
            keys = pl.ds(pl.multiple_of(s * width, elen), width)
            k = ks_ref[keys, :]
            sc = nt(k, big)
            top = jnp.max(sc, axis=0, keepdims=True)
            expo = jnp.exp(sc - top)
            inv = 1.0 / jnp.sum(expo, axis=0, keepdims=True)
            inv = jnp.where(qseg == s, inv, 0.0)
            p = expo * inv
            u = p * nt(vs_ref[keys, :], gbig)
            ds = (u - p * jnp.sum(u, axis=0, keepdims=True)).astype(bf)
            av_ref[keys, :] += nn(p.astype(bf), gbig)
            ak_ref[keys, :] += nn(ds, big)
            return acc + collect(tn(ds, k))
        out = lax.fori_loop(lo, hi + 1, pair, jnp.zeros((TR, q_ref.shape[1]), f32))
        dq_ref[rows, :] = (out * HD ** -0.5).astype(bf)
        return carry
    lax.fori_loop(0, n // TR, tile, 0)
    for j in range(segs * nret):
        spot = pl.ds(pl.multiple_of(ids_ref[row, j] * elen, elen), elen)
        pk_ref[spot, :] += ak_ref[j*elen:(j+1)*elen, :]
        pv_ref[spot, :] += av_ref[j*elen:(j+1)*elen, :]

def cross_bwd(lens, ids, cq, kv, grad, rows, nret, elen):
    tok, width = cq.shape
    n = tok // rows
    lanes = NH * HD
    nb = width // lanes
    segs = lens.shape[1]
    pool = kv.shape[0]
    qspec = pl.BlockSpec((n, lanes), lambda h, r, *_: (jnp.minimum(r, rows - 1), h))
    kspec = lambda off: pl.BlockSpec((pool, lanes), lambda h, r, *_: (0, off*nb + h))
    keys = segs*nret*elen
    return pl.pallas_call(
        functools.partial(cross_bwd_kernel, segs, nret, elen, rows),
        grid_spec=pltpu.PrefetchScalarGridSpec(num_scalar_prefetch=2, grid=(nb, rows + 1),
            in_specs=[qspec, kspec(0), kspec(1), qspec], out_specs=[qspec, pl.BlockSpec((pool, lanes), lambda h, r, *_: (0, jnp.where(r < rows, 0, nb) + h))],
            scratch_shapes=[pltpu.VMEM((keys, lanes), bf)]*2+[pltpu.VMEM((keys, lanes), f32)]*2+[pltpu.VMEM((pool, lanes), f32)]*2),
        out_shape=[jax.ShapeDtypeStruct((tok, width), bf)]+[jax.ShapeDtypeStruct(kv.shape, bf)],
        compiler_params=pltpu.CompilerParams(vmem_limit_bytes=56<<20),
        cost_estimate=pl.CostEstimate(flops=5*tok*keys*width, bytes_accessed=14*tok*width, transcendentals=tok*keys*width//HD//2),
    )(lens, ids, cq, kv, kv, grad)


def norm_forward(resid, gain, shift):
    mean_row = jnp.mean(resid, axis=-1, keepdims=True)
    centred = resid - mean_row
    inv = lax.rsqrt(jnp.mean(centred * centred, axis=-1, keepdims=True) + eps_norm)
    normed = centred * inv
    return (normed * gain + shift, normed, inv)


def norm_backward(grad_out, normed, inv, gain):
    scaled = grad_out * gain
    grad_in = inv * (
        scaled
        - jnp.mean(scaled, axis=-1, keepdims=True)
        - normed * jnp.mean(scaled * normed, axis=-1, keepdims=True)
    )
    return (grad_in, jnp.sum(grad_out * normed, axis=0), jnp.sum(grad_out, axis=0))


def gelu_slope(upper):
    cdf = 0.5 * (1.0 + jax.scipy.special.erf(upper * 2.0 ** (-0.5)))
    dens = jnp.exp(-0.5 * upper * upper) * (2.0 * jnp.pi) ** (-0.5)
    return cdf + upper * dens


def swap(value, mask):
    size = lax.axis_size(AXES)
    return lax.ppermute(value, AXES, [(i, i ^ mask) for i in range(size)])


def place_kernel(moves, where_ref, *refs):
    pieces, out_ref, sems = refs[:-2], refs[-2], refs[-1]
    copies = []
    for index, (src, src_row, rows, slot, col, cols) in enumerate(moves):
        first = pl.multiple_of(where_ref[slot], rows)
        copies.append(
            pltpu.make_async_copy(
                pieces[src].at[pl.ds(src_row, rows), :],
                out_ref.at[pl.ds(first, rows), pl.ds(col, cols)],
                sems.at[index],
            )
        )
    for copy in copies:
        copy.start()
    for copy in copies:
        copy.wait()


def place(pieces, where, moves, shape):
    anywhere = pl.BlockSpec(memory_space=pl.ANY)
    return pl.pallas_call(
        functools.partial(place_kernel, tuple(moves)),
        grid_spec=pltpu.PrefetchScalarGridSpec(
            num_scalar_prefetch=1,
            grid=(),
            in_specs=[anywhere] * len(pieces),
            out_specs=anywhere,
            scratch_shapes=[pltpu.SemaphoreType.DMA((len(moves),))],
        ),
        out_shape=jax.ShapeDtypeStruct(shape, bf),
        compiler_params=pltpu.CompilerParams(vmem_limit_bytes=1 << 20),
        cost_estimate=pl.CostEstimate(
            flops=0, bytes_accessed=4 * shape[0] * shape[1], transcendentals=0
        ),
    )(where, *pieces)


def gather_group(shard, me):
    rows, cols = shard.shape
    size = lax.axis_size(AXES)
    low = size // HI
    half = cols // 2
    got = [shard] + [swap(shard, HI * k) for k in range(1, low)]
    hi = me % HI
    lo = me // HI
    if rows % 16:
        lined = jnp.take(jnp.stack(got), lo ^ jnp.arange(low, dtype=jnp.int32), axis=0)
        got, rows, low, lo = [lined.reshape(-1, cols)], rows * low, 1, 0
    pieces = []
    for part, order in ((slice(0, half), (2, 4)), (slice(half, cols), (4, 2))):
        have = {0: jnp.concatenate([g[:, part] for g in got], axis=0)}
        for mask in order + (1,):
            have.update({j | mask: swap(have[j], mask) for j in list(have)})
        pieces += [have[j] for j in range(HI)]
    where = jnp.stack(
        [(hi ^ j) * (low * rows) + (lo ^ k) * rows for j in range(HI) for k in range(low)]
    )
    moves = [
        (p * HI + j, k * rows, rows, j * low + k, p * half, half)
        for p in range(2)
        for j in range(HI)
        for k in range(low)
    ]
    return place(pieces, where, moves, (HI * low * rows, cols))


def gather_passages(own, me):
    rows, cols = own.shape
    group = lax.axis_size("fsdp")
    have = {0: own}
    mask = group // 2
    while mask:
        have.update({j | mask: swap(have[j], mask) for j in list(have)})
        mask //= 2
    index = me % group
    where = jnp.stack([(index ^ j) * rows for j in range(group)])
    moves = [(j, 0, rows, j, 0, cols) for j in range(group)]
    return place([have[j] for j in range(group)], where, moves, (group * rows, cols))


def reduce_passages(whole, me):
    group = lax.axis_size("fsdp")
    blocks = whole.reshape(group, -1, whole.shape[1])
    index = me % group
    have = {j: lax.dynamic_index_in_dim(blocks, index ^ j, 0, keepdims=False) for j in range(group)}
    mask = 1
    while mask < group:
        have = {
            j: (have[j].astype(f32) + swap(have[j | mask].astype(bf), mask).astype(f32))
            for j in have
            if not j & mask
        }
        mask *= 2
    return have[0].astype(bf)


def grad_theirs_kernel(me_ref, x_ref, dz_ref, out_ref, xt_ref):
    block = x_ref.shape[1] // HI

    @pl.when(pl.program_id(0) == 0)
    def _():
        for at, j in enumerate((1, 3, 5, 7)):
            first = pl.multiple_of((j ^ me_ref[0]) * block, block)
            xt_ref[at * block : (at + 1) * block, :] = x_ref[:, pl.ds(first, block)].T

    out_ref[...] = nn(xt_ref[...], dz_ref[...]).astype(bf)


def grad_mine_kernel(half_tiles, me_ref, x_ref, dz_ref, got_ref, keep_ref, sa_ref, sb_ref, xt_ref):
    step = pl.program_id(0)
    block = x_ref.shape[1] // HI

    @pl.when(step == 0)
    def _():
        for at, j in enumerate((0, 2, 4, 6)):
            first = pl.multiple_of((j ^ me_ref[0]) * block, block)
            xt_ref[at * block : (at + 1) * block, :] = x_ref[:, pl.ds(first, block)].T

    full = (nn(xt_ref[...], dz_ref[...]) + got_ref[...].astype(f32)).astype(bf)
    b0, b2, b4, b6 = [full[i * block : (i + 1) * block] for i in range(4)]
    keep_ref[:block, :] = b0

    @pl.when(step < half_tiles)
    def _():
        keep_ref[block:, :] = b4
        sa_ref[:block, :] = b2
        sa_ref[block:, :] = b6

    @pl.when(step >= half_tiles)
    def _():
        keep_ref[block:, :] = b2
        sb_ref[:block, :] = b4
        sb_ref[block:, :] = b6


def second_kernel(half_tiles, keep_ref, ra_ref, rb_ref, out_ref, sa_ref, sb_ref):
    step = pl.program_id(0)
    block = out_ref.shape[0]

    @pl.when(step < half_tiles)
    def _():
        total = (keep_ref[...].astype(f32) + ra_ref[...].astype(f32)).astype(bf)
        out_ref[...] = total[:block]
        sa_ref[...] = total[block:]

    @pl.when(step >= half_tiles)
    def _():
        total = (keep_ref[...].astype(f32) + rb_ref[...].astype(f32)).astype(bf)
        out_ref[...] = total[:block]
        sb_ref[...] = total[block:]


def reduce_group(lhs, dz, me):
    tokens, width = lhs.shape
    cols = dz.shape[1]
    size = lax.axis_size(AXES)
    low = size // HI
    block = width // HI
    tile = min(512, cols // 2)
    tiles = cols // tile
    half_tiles = tiles // 2
    half = cols // 2
    hi = (me % HI).reshape(1)
    big = pltpu.CompilerParams(vmem_limit_bytes=40 << 20)
    cost = pl.CostEstimate(
        flops=tokens * width * cols, bytes_accessed=4 * tokens * cols, transcendentals=0
    )
    whole = pl.BlockSpec((tokens, width), lambda t, *_: (0, 0))
    dz_spec = pl.BlockSpec((tokens, tile), lambda t, *_: (0, t))
    xt = pltpu.VMEM((width // 2, tokens), bf)
    theirs = pl.pallas_call(
        grad_theirs_kernel,
        grid_spec=pltpu.PrefetchScalarGridSpec(
            num_scalar_prefetch=1,
            grid=(tiles,),
            in_specs=[whole, dz_spec],
            out_specs=pl.BlockSpec((width // 2, tile), lambda t, *_: (0, t)),
            scratch_shapes=[xt],
        ),
        out_shape=jax.ShapeDtypeStruct((width // 2, cols), bf),
        compiler_params=big,
        cost_estimate=cost,
    )(hi, lhs, dz)
    got = swap(theirs, 1)
    a_map = lambda t, *_: (0, jnp.minimum(t, half_tiles - 1))
    b_map = lambda t, *_: (0, jnp.maximum(t - half_tiles, 0))
    keep, send_a, send_b = pl.pallas_call(
        functools.partial(grad_mine_kernel, half_tiles),
        grid_spec=pltpu.PrefetchScalarGridSpec(
            num_scalar_prefetch=1,
            grid=(tiles,),
            in_specs=[whole, dz_spec, pl.BlockSpec((width // 2, tile), lambda t, *_: (0, t))],
            out_specs=[
                pl.BlockSpec((2 * block, tile), lambda t, *_: (0, t)),
                pl.BlockSpec((2 * block, tile), a_map),
                pl.BlockSpec((2 * block, tile), b_map),
            ],
            scratch_shapes=[xt],
        ),
        out_shape=[
            jax.ShapeDtypeStruct((2 * block, cols), bf),
            jax.ShapeDtypeStruct((2 * block, half), bf),
            jax.ShapeDtypeStruct((2 * block, half), bf),
        ],
        compiler_params=big,
        cost_estimate=cost,
    )(hi, lhs, dz, got)
    ra = swap(send_a, 2)
    rb = swap(send_b, 4)
    keep, send_a, send_b = pl.pallas_call(
        functools.partial(second_kernel, half_tiles),
        grid=(tiles,),
        in_specs=[
            pl.BlockSpec((2 * block, tile), lambda t: (0, t)),
            pl.BlockSpec((2 * block, tile), a_map),
            pl.BlockSpec((2 * block, tile), b_map),
        ],
        out_specs=[
            pl.BlockSpec((block, tile), lambda t: (0, t)),
            pl.BlockSpec((block, tile), a_map),
            pl.BlockSpec((block, tile), b_map),
        ],
        out_shape=[
            jax.ShapeDtypeStruct((block, cols), bf),
            jax.ShapeDtypeStruct((block, half), bf),
            jax.ShapeDtypeStruct((block, half), bf),
        ],
        compiler_params=pltpu.CompilerParams(vmem_limit_bytes=16 << 20),
        cost_estimate=pl.CostEstimate(
            flops=block * cols, bytes_accessed=12 * block * cols, transcendentals=0
        ),
    )(keep, ra, rb)
    ra = swap(send_a, 4)
    rb = swap(send_b, 2)
    last = keep.astype(f32) + jnp.concatenate([ra, rb], axis=1).astype(f32)
    chunks = last.reshape(low, block // low, cols)
    lo = me // HI
    total = lax.dynamic_index_in_dim(chunks, lo, 0, keepdims=False)
    for k in range(1, low):
        send = lax.dynamic_index_in_dim(chunks, lo ^ k, 0, keepdims=False).astype(bf)
        total = total + swap(send, HI * k).astype(f32)
    return total


def update_kernel(which_ref, basis_ref, g_ref, m_ref, v_ref, w_ref, first_ref, second_ref, new_ref):
    corr_one = 1.0 - beta_one**STEP
    corr_two = 1.0 - beta_two**STEP
    basis = basis_ref[0].astype(bf)
    turned = tn(g_ref[0], basis).T
    first = beta_one * m_ref[...] + (1.0 - beta_one) * turned
    second = beta_two * v_ref[...] + (1.0 - beta_two) * turned * turned
    first_ref[...] = first
    second_ref[...] = second
    step = (first / corr_one) / (jnp.sqrt(second / corr_two) + adam_eps)
    back = nn(basis, step.astype(bf))
    weights = w_ref[...]
    new_ref[...] = weights - rate_mat * (back + decay * weights)


def update(which, bases, grads, first, second, weights):
    count, width, cols = grads.shape
    spec = pl.BlockSpec((width, cols), lambda s, *_: (0, s))
    sds = jax.ShapeDtypeStruct(weights.shape, f32)
    return pl.pallas_call(
        update_kernel,
        grid_spec=pltpu.PrefetchScalarGridSpec(
            num_scalar_prefetch=1,
            grid=(count,),
            in_specs=[
                pl.BlockSpec((1, width, width), lambda s, which_ref: (which_ref[s], 0, 0)),
                pl.BlockSpec((1, width, cols), lambda s, *_: (s, 0, 0)),
                spec,
                spec,
                spec,
            ],
            out_specs=[spec] * 3,
        ),
        out_shape=[sds] * 3,
        compiler_params=pltpu.CompilerParams(vmem_limit_bytes=48 << 20),
        cost_estimate=pl.CostEstimate(
            flops=4 * width * width * cols * count,
            bytes_accessed=4 * count * width * (width + 6 * cols),
            transcendentals=0,
        ),
    )(which, bases, grads, first, second, weights)


def shards(
    hidden_in,
    cotangent,
    seg_lengths,
    retrieved,
    encoder_states,
    master_weights,
    first_moment,
    second_moment,
    slot_block,
    bases,
    vector_params,
    vector_first,
    vector_second,
):
    micro, rows_dev, row_len, width = hidden_in.shape
    segs = seg_lengths.shape[2]
    nret = retrieved.shape[3]
    elen = encoder_states.shape[1]
    size = lax.axis_size(AXES)
    low = size // HI
    me = lax.axis_index(AXES)
    nblk = slot_block.shape[0]
    per_dev = nblk // size
    bcols = master_weights.shape[1] // per_dev
    cols = nblk * bcols
    rp = width // size
    rows = micro * rows_dev
    tokens = rows * row_len
    hidden = (cols - 8 * width) // 2
    nvec = vector_params.shape[0]
    pass_grp = encoder_states.shape[0] * lax.axis_size("fsdp")
    lens = seg_lengths.reshape(rows, segs)
    ids = retrieved.reshape(rows, segs * nret) - lax.axis_index("dp") * pass_grp
    inverse = jnp.zeros((nblk,), jnp.int32).at[slot_block].set(jnp.arange(nblk, dtype=jnp.int32))

    send = (
        master_weights.astype(bf)
        .reshape(HI, low, rp, per_dev, bcols)
        .transpose(1, 0, 3, 2, 4)
        .reshape(size, per_dev, rp, bcols)
    )
    slots = lax.all_to_all(send, AXES, 0, 0, tiled=True).reshape(nblk, rp, bcols)
    natural = jnp.take(slots, inverse, axis=0).transpose(1, 0, 2).reshape(rp, cols)

    part = lax.axis_size(AXES)
    vcols = vector_params.shape[1]
    vecs = lax.dynamic_update_slice(
        jnp.zeros((nvec, vcols * part), bf), vector_params.astype(bf), (0, me * vcols)
    )
    mask = 1
    while mask < size:
        vecs = vecs + swap(vecs, mask)
        mask *= 2
    vecs = vecs.astype(f32)

    enc = gather_passages(encoder_states.reshape(-1, width), me)
    cuts = [0, 3 * width, 5 * width, 8 * width, 8 * width + hidden, cols]
    g_qkv, g_ocq, g_ckvo, w_up, w_dt = [
        gather_group(natural[:, a:b], me) for a, b in zip(cuts[:-1], cuts[1:])
    ]
    w_o, c_q = g_ocq[:, :width], g_ocq[:, width:]
    c_kv, c_o = g_ckvo[:, : 2 * width], g_ckvo[:, 2 * width :]
    zero = jnp.zeros((width,), f32)
    b_up = vecs[13:].reshape(-1)

    x = hidden_in.reshape(tokens, width)
    cot = cotangent.reshape(tokens, width)
    qkv = (nn(x, g_qkv) + jnp.concatenate([vecs[0], zero, vecs[1]])).astype(bf)
    attn = self_fwd(lens, qkv, rows)
    hid_one, normed_one, inv_one = norm_forward(
        x.astype(f32) + nn(attn, w_o) + vecs[2], vecs[3], vecs[4]
    )
    hid_low = hid_one.astype(bf)
    cq = (nn(hid_low, c_q) + vecs[5]).astype(bf)
    kv = (nn(enc, c_kv) + jnp.concatenate([zero, vecs[6]])).astype(bf)
    attn_c = cross_fwd(lens, ids, cq, kv, rows, nret, elen)
    hid_two, normed_two, inv_two = norm_forward(
        hid_one + nn(attn_c, c_o) + vecs[7], vecs[8], vecs[9]
    )
    hid_two_low = hid_two.astype(bf)
    upper = nn(hid_two_low, w_up) + b_up
    act = jax.nn.gelu(upper, approximate=False).astype(bf)
    out, normed_three, inv_three = norm_forward(
        hid_two + nt(act, w_dt) + vecs[10], vecs[11], vecs[12]
    )
    d_resid3, d_g3, d_e3 = norm_backward(cot.astype(f32), normed_three, inv_three, vecs[11])
    d_branch3 = d_resid3.astype(bf)
    d_bdown = jnp.sum(d_branch3.astype(f32), axis=0)
    s_dt = reduce_group(d_branch3, act, me)
    d_upper = (nn(d_branch3, w_dt) * gelu_slope(upper)).astype(bf)
    d_bup = jnp.sum(d_upper.astype(f32), axis=0)
    s_up = reduce_group(hid_two_low, d_upper, me)
    d_hid_two = d_resid3 + nt(d_upper, w_up)
    d_resid2, d_g2, d_e2 = norm_backward(d_hid_two, normed_two, inv_two, vecs[8])
    d_branch2 = d_resid2.astype(bf)
    d_cbo = jnp.sum(d_branch2.astype(f32), axis=0)
    s_co = reduce_group(attn_c, d_branch2, me)
    d_attn_c = nt(d_branch2, c_o).astype(bf)
    g_cq, g_ckv = cross_bwd(lens, ids, cq, kv, d_attn_c, rows, nret, elen)
    d_cbq = jnp.sum(g_cq.astype(f32), axis=0)
    d_cbv = jnp.sum(g_ckv[:, width:].astype(f32), axis=0)
    s_cq = reduce_group(hid_low, g_cq, me)
    s_ckv = reduce_group(enc, g_ckv, me)
    d_hid_one = d_resid2 + nt(g_cq, c_q)
    d_resid1, d_g1, d_e1 = norm_backward(d_hid_one, normed_one, inv_one, vecs[3])
    d_branch1 = d_resid1.astype(bf)
    d_bo = jnp.sum(d_branch1.astype(f32), axis=0)
    s_o = reduce_group(attn, d_branch1, me)
    d_attn = nt(d_branch1, w_o).astype(bf)
    encoder_grad = reduce_passages(nt(g_ckv, c_kv), me)
    g_in = self_bwd(lens, qkv, d_attn, rows)
    d_bq = jnp.sum(g_in[:, :width].astype(f32), axis=0)
    d_bv = jnp.sum(g_in[:, 2 * width :].astype(f32), axis=0)
    s_qkv = reduce_group(x, g_in, me)
    d_x = d_resid1 + nt(g_in, g_qkv)

    vec_grad = jnp.concatenate(
        [
            jnp.stack(
                [d_bq, d_bv, d_bo, d_g1, d_e1, d_cbq, d_cbv, d_cbo, d_g2, d_e2, d_bdown, d_g3, d_e3]
            ),
            d_bup.reshape(-1, width),
        ],
        axis=0,
    )
    mask = 1
    while mask < size:
        vec_grad = vec_grad + swap(vec_grad, mask)
        mask *= 2
    share_vec = lax.dynamic_slice(vec_grad, (0, me * vcols), (nvec, vcols))

    mine = jnp.concatenate([s_qkv, s_o, s_cq, s_ckv, s_co, s_up, s_dt], axis=1).astype(bf)
    blocks = jnp.take(mine.reshape(rp, nblk, bcols).transpose(1, 0, 2), slot_block, axis=0)
    got = lax.all_to_all(blocks.reshape(size, per_dev, rp, bcols), AXES, 0, 0, tiled=True)
    grads = (
        got.reshape(low, HI, per_dev, rp, bcols)
        .transpose(2, 1, 0, 3, 4)
        .reshape(per_dev, width, bcols)
    )
    my_blocks = lax.dynamic_slice(slot_block, (me * per_dev,), (per_dev,))
    bounds = jnp.array([width * j for j in range(1, 9)] + [8 * width + hidden], jnp.int32)
    which = jnp.sum((my_blocks[:, None] * bcols >= bounds[None, :]).astype(jnp.int32), axis=1)
    first_new, second_new, master_new = update(
        which, bases, grads, first_moment, second_moment, master_weights
    )
    corr_one = 1.0 - beta_one**STEP
    corr_two = 1.0 - beta_two**STEP
    vf_new = beta_one * vector_first + (1.0 - beta_one) * share_vec
    vs_new = beta_two * vector_second + (1.0 - beta_two) * share_vec * share_vec
    vec_new = vector_params - rate_vec * (vf_new / corr_one) / (
        jnp.sqrt(vs_new / corr_two) + adam_eps
    )
    return (
        out.astype(bf).reshape(hidden_in.shape),
        d_x.astype(bf).reshape(hidden_in.shape),
        encoder_grad.reshape(encoder_states.shape),
        first_new,
        second_new,
        master_new,
        vf_new,
        vs_new,
        vec_new,
        share_vec,
    )


def solution(mesh):
    spread_rows = P(None, ("dp", "fsdp"), None, None)
    spread_cols = P(None, ("dp", "fsdp"))
    in_specs = (
        spread_rows,
        spread_rows,
        P(None, ("dp", "fsdp"), None),
        spread_rows,
        P(("dp", "fsdp"), None, None),
        spread_cols,
        spread_cols,
        spread_cols,
        P(),
        P(),
        spread_cols,
        spread_cols,
        spread_cols,
    )
    out_specs = (spread_rows, spread_rows, P(("dp", "fsdp"), None, None)) + (spread_cols,) * 7
    return jax.shard_map(shards, mesh=mesh, in_specs=in_specs, out_specs=out_specs, check_vma=False)
```

time: 2270 us -> 1040 us (0.46)
  waiting for transfers between devices: 779 us -> 253 us
  local copies, waits for them, and re-layouts: 570 us -> 57.8 us
  matrix products: 637 us -> 160 us
  Pallas kernels: 0 us -> 343 us
  starting transfers between devices: 0.2 us -> 164 us
  other arithmetic: 198 us -> 45.5 us
  blocking collectives: 44.3 us -> 0 us
    reduce_scatter x1 -> x0, waiting for transfers between devices: 609 us -> none  [shards(): lax.psum_scatter(slot_layout(mb_mat, slot_block, block_cols), ('dp', 'fsd...]
    dot_general x160 -> x14, matrix products: 637 us -> 160 us  [the longest x7 94 us: nn(): lax.dot_general(a, b, (((1,), (0,)), ((), ())), preferred_element_type=f32)]
    pallas_call x0 -> x32, Pallas kernels: none -> 343 us  [the longest x1 89.5 us: cross_bwd(): pl.pallas_call(functools.partial(cross_bwd_kernel, segs, nret, elen, rows...]
    ppermute x0 -> x157, waiting for transfers between devices: none -> 244 us  [swap(): return lax.ppermute(value, AXES, [(i, i ^ mask) for i in range(size)])]
    all_gather x2 -> x0, waiting for transfers between devices: 169 us -> none  [the longest x1 169 us: shards(): lax.all_gather(send_wide, ('dp', 'fsdp'), axis=1, tiled=True)]
    gather x7 -> x2, local copies, waits for them, and re-layouts: 167 us -> 3.95 us  [the longest x1 3.19 us: shards(): jnp.take(slots, inverse, axis=0).transpose(1, 0, 2).reshape(rp, cols)]
    ppermute x0 -> x157, starting transfers between devices: none -> 150 us  [swap(): return lax.ppermute(value, AXES, [(i, i ^ mask) for i in range(size)])]
    reshape x7 -> x2, local copies, waits for them, and re-layouts: 138 us -> 2.29 us  [the longest x1 2.28 us: shards(): send = master_weights.astype(bf).reshape(HI, low, rp, per_dev, bcols).tra...]
  transfers between devices with their start and end apart: 5 -> 159, of which waited for: 2 -> 50; matrix products, arithmetic and copies ran while one was open for 26% -> 13% of each run, Pallas kernels for 0% -> 19%
where the time goes in v1:
time: 1040 us; the launch traced here: 1030 us
  Pallas kernels  343 us (33%)
  waiting for transfers between devices  253 us (24%)
  starting transfers between devices  164 us (16%)
  matrix products  160 us (15%)
  local copies, waits for them, and re-layouts  57.8 us (6%)
  other arithmetic  45.5 us (4%)
    ppermute x157, waiting for transfers between devices, swap(): return lax.ppermute(value, AXES, [(i, i ^ mask) for i in range(size)])  244 us
    ppermute x157, starting transfers between devices, swap(): return lax.ppermute(value, AXES, [(i, i ^ mask) for i in range(size)])  150 us
    dot_general x7, matrix products, nn(): lax.dot_general(a, b, (((1,), (0,)), ((), ())), preferred_element_type=f32)  94 us
    pallas_call x1, Pallas kernels, cross_bwd(): pl.pallas_call(functools.partial(cross_bwd_kernel, segs, nret, elen, rows...  89.5 us
    dot_general x7, matrix products, nt(): lax.dot_general(a, b, (((1,), (1,)), ((), ())), preferred_element_type=f32)  66.5 us
    pallas_call x1, Pallas kernels, cross_fwd(): pl.pallas_call(functools.partial(cross_fwd_kernel, segs, nret, elen), gri...  62.3 us
    pallas_call x1, Pallas kernels, self_bwd(): pl.pallas_call(functools.partial(self_bwd_kernel, lens.shape[1]), grid_sp...  46.3 us
    pallas_call x7, Pallas kernels, reduce_group(): pl.pallas_call(functools.partial(grad_mine_kernel, half_tiles), grid_spec...  44.9 us
  transfers between devices with their start and end apart: 159, of which 50 were waited for; matrix products, arithmetic and copies ran while one was open for 13% of the time, Pallas kernels for 19%

profile of v1, /device:TPU:0, one launch (start us, length us, event | category | flops | bytes accessed | tf_op | source)
XLA Modules:
  0.0 1026.6 jit_solution(12546387088248016791)
XLA Ops:
  20.1 17.9 %collective-permute-done.18 = bf16[17,1024]{1,0:T(8,128)(2,1)S(1)} collective-permute-done((bf16[17,1024]{1,0:T(8,128)(2,1)S(1)}, bf16[17,1024]{1,0:T(8,128)(2,1)S(1)}, u32[]{:S(2)}, u32[]{:S(2)}) %collective-permute-start.18) | collective-permute-done | bytes 34848 | tf_op jit(solution)/shard_map/ppermute | solution.py:341
  78.2 9.5 collective-permute-start.24
  87.7 10.7 %collective-permute-done.23 = bf16[32,2048]{1,0:T(8,128)(2,1)S(1)} collective-permute-done((bf16[32,2048]{1,0:T(8,128)(2,1)S(1)}, bf16[32,2048]{1,0:T(8,128)(2,1)S(1)}, u32[]{:S(2)}, u32[]{:S(2)}) %collective-permute-start.23) | collective-permute-done | bytes 131104 | tf_op jit(solution)/shard_map/ppermute | solution.py:341
  125.6 8.4 collective-permute-done.1
  144.6 11.3 %collective-permute-done.60 = bf16[32,4096]{1,0:T(8,128)(2,1)S(1)} collective-permute-done((bf16[32,4096]{1,0:T(8,128)(2,1)S(1)}, bf16[32,4096]{1,0:T(8,128)(2,1)S(1)}, u32[]{:S(2)}, u32[]{:S(2)}) %collective-permute-start.60) | collective-permute-done | bytes 262176 | tf_op jit(solution)/shard_map/ppermute | solution.py:341
  232.0 8.6 fusion.16.q_ref.k_ref.v_ref
  240.6 18.8 %shard_map.214.x_ref = bf16[1024,1024]{1,0:T(8,128)(2,1)S(1)} custom-call(s32[2,4]{1,0:T(2,128)S(1)} %bitcast.287, bf16[1024,3072]{1,0:T(8,128)(2,1)} %fusion.16.q_ref.k_ref.v_ref, bf16[1024,3072]{1,0:T(8,128)(2,1)} %fusion.16.q_ref.k_ref.v_ref, bf16[1024,3072]{1,0:T(8,128)(2,1)} %fusion.16.q_ref.k_ref.v_ref), custom_call_target="tpu_custom_call" | custom-call | flops 1073741824 | bytes 8388608 | tf_op jit(solution)/shard_map/pallas_call | solution.py:92
  282.7 10.9 %add_convert_fusion.k_ref.v_ref = bf16[2048,2048]{1,0:T(8,128)(2,1)} fusion(f32[2048]{0:T(1024)S(1)} %copy-done.130, bf16[2048,1024]{1,0:T(8,128)(2,1)S(1)} %shard_map.216.x_ref, bf16[1024,3072]{1,0:T(8,128)(2,1)S(1)} %shard_map.217), kind=kOutput, calls=%fused_computation.28 | convolution fusion | flops 8598323200 | bytes 16785408 | tf_op jit(solution)/shard_map/dot_general | solution.py:28
  301.2 19.6 %collective-permute-done.72.refs_12_ = bf16[128,2048]{1,0:T(8,128)(2,1)S(1)} collective-permute-done((bf16[128,2048]{1,0:T(8,128)(2,1)}, bf16[128,2048]{1,0:T(8,128)(2,1)S(1)}, u32[]{:S(2)}, u32[]{:S(2)}) %collective-permute-start.72) | collective-permute-done | bytes 524320 | tf_op jit(solution)/shard_map/ppermute | solution.py:341
  326.8 62.3 %shard_map.218.x_ref = bf16[1024,1024]{1,0:T(8,128)(2,1)S(1)} custom-call(s32[2,4]{1,0:T(2,128)S(1)} %bitcast.288, s32[2,20]{1,0:T(2,128)S(1)} %sub.88.ids_ref, bf16[1024,1024]{1,0:T(8,128)(2,1)S(1)} %add_convert_fusion.4.q_ref, bf16[2048,2048]{1,0:T(8,128)(2,1)} %add_convert_fusion.k_ref.v_ref, bf16[2048,2048]{1,0:T(8,128)(2,1)} %add_convert_fusion.k_ref.v_ref), custom_call_target="tpu_custom_call" | custom-call | flops 2684354560 | bytes 8388608 | tf_op jit(solution)/shard_map/pallas_call | solution.py:227
  412.8 45.8 %fusion.2 = (bf16[1024,4096]{1,0:T(8,128)(2,1)}, f32[1024,4096]{1,0:T(8,128)}) fusion(f32[4096]{0:T(1024)S(1)} %bitcast.337, bf16[1024,1024]{1,0:T(8,128)(2,1)S(1)} %fusion.25.x_ref, bf16[1024,4096]{1,0:T(8,128)(2,1)S(1)} %shard_map.219), kind=kOutput, calls=%fused_computation.7 | convolution fusion | flops 8866758656 | bytes 35667968 | tf_op jit(solution)/shard_map/dot_general | solution.py:28
  466.6 15.2 %fusion.119 = (f32[1024]{0:T(1024)S(1)}, f32[1024,1024]{1,0:T(8,128)S(1)}) fusion(f32[1024]{0:T(1024)S(1)} %bitcast.347, bf16[1024,4096]{1,0:T(8,128)(2,1)} %get-tuple-element.258.dz_ref, bf16[1024,4096]{1,0:T(8,128)(2,1)} %copy-done.17, f32[1024]{0:T(1024)S(1)} %bitcast.330, f32[1024]{0:T(1024)S(1)} %bitcast.324, f32[1024]{0:T(1024)S(1)} %copy-done.118, ...), kind=kOutput, calls=%fused_computation.254 | convolution fusion | flops 8597273600 | bytes 25190400 | tf_op jit(solution)/shard_map/dot_general | solution.py:27
  489.1 19.0 %convert_reduce_fusion = (f32[4096]{0:T(1024)S(1)}, bf16[1024,4096]{1,0:T(8,128)(2,1)}) fusion(f32[1024,4096]{1,0:T(8,128)} %get-tuple-element.259, f32[4096]{0:T(1024)S(1)} %bitcast.338, bf16[1024,1024]{1,0:T(8,128)(2,1)S(1)} %get-tuple-element.164.x_ref, bf16[1024,4096]{1,0:T(8,128)(2,1)S(1)} %bitcast.279), kind=kOutput, calls=%fused_computation.14 | convolution fusion | flops 8644456448 | bytes 35684352 | tf_op jit(solution)/shard_map/dot_general | solution.py:28
  508.1 14.4 %multiply_reduce_fusion = (f32[1024]{0:T(1024)S(1)}, f32[1024]{0:T(1024)S(1)}, f32[1024]{0:T(1024)S(1)}, f32[1024]{0:T(1024)S(1)}, f32[1024,1024]{1,0:T(8,128)}) fusion(f32[1024,1024]{1,0:T(8,128)S(1)} %copy-done.87, f32[1024]{0:T(1024)S(1)} %copy-done.118, f32[1024]{0:T(1024)S(1)} %copy-done.114, f32[1024]{0:T(1024)S(1)} %bitcast.325, ...), kind=kOutput, calls=%fused_computation.46 | convolution fusion | flops 8600416256 | bytes 29388800 | tf_op jit(solution)/shard_map/dot_general | solution.py:27
  533.7 89.5 %shard_map.221 = (bf16[1024,1024]{1,0:T(8,128)(2,1)}, bf16[2048,2048]{1,0:T(8,128)(2,1)}) custom-call(s32[2,4]{1,0:T(2,128)} %bitcast.286, s32[2,20]{1,0:T(2,128)} %copy-done.79, bf16[1024,1024]{1,0:T(8,128)(2,1)} %copy-done.33, bf16[2048,2048]{1,0:T(8,128)(2,1)} %add_convert_fusion.k_ref.v_ref, bf16[2048,2048]{1,0:T(8,128)(2,1)} %add_convert_fusion.k_ref.v_ref, ...), custom_call_target="tpu_custom_call" | custom-call | flops 6710886400 | bytes 14680064 | tf_op jit(solution)/shard_map/pallas_call | solution.py:304
  626.1 13.4 %fusion.26 = f32[2048,1024]{1,0:T(8,128)} fusion(bf16[2048,2048]{1,0:T(8,128)(2,1)} %get-tuple-element.59.dz_ref, bf16[1024,3072]{1,0:T(8,128)(2,1)S(1)} %bitcast.281), kind=kOutput, calls=%fused_computation.73 | convolution fusion | flops 8589934592 | bytes 20971520 | tf_op jit(solution)/shard_map/dot_general | solution.py:27
  650.1 46.3 %shard_map.222.dz_ref = bf16[1024,3072]{1,0:T(8,128)(2,1)} custom-call(s32[2,4]{1,0:T(2,128)S(1)} %bitcast.289, bf16[1024,3072]{1,0:T(8,128)(2,1)} %fusion.16.q_ref.k_ref.v_ref, bf16[1024,3072]{1,0:T(8,128)(2,1)} %fusion.16.q_ref.k_ref.v_ref, bf16[1024,3072]{1,0:T(8,128)(2,1)} %fusion.16.q_ref.k_ref.v_ref, bf16[1024,1024]{1,0:T(8,128)(2,1)S(1)} %convolution_convert_fusion.g_ref), custom_call_target="tpu_custom_call" | custom-call | flops 2684354560 | bytes 14680064 | tf_op jit(solution)/shard_map/pallas_call | solution.py:150
  716.5 9.2 shard_map.232
  734.2 10.8 %shard_map.238 = bf16[512,4096]{1,0:T(8,128)(2,1)} custom-call(s32[1]{0:T(128)} %bitcast.68.me_ref, bf16[1024,1024]{1,0:T(8,128)(2,1)S(1)} %copy-done.29, bf16[1024,4096]{1,0:T(8,128)(2,1)} %get-tuple-element.265.dz_ref), custom_call_target="tpu_custom_call" | custom-call | flops 4294967296 | bytes 16777216 | tf_op jit(solution)/shard_map/pallas_call | solution.py:514
  777.3 9.2 shard_map.241
  800.3 8.2 shard_map.233
  812.4 8.2 collective-permute-done.121.ra_ref
  824.1 7.9 shard_map.224
  836.5 11.5 %collective-permute-done.97.ra_ref = bf16[256,1536]{1,0:T(8,128)(2,1)S(1)} collective-permute-done((bf16[256,1536]{1,0:T(8,128)(2,1)S(1)}, bf16[256,1536]{1,0:T(8,128)(2,1)S(1)}, u32[]{:S(2)}, u32[]{:S(2)}) %collective-permute-start.97) | collective-permute-done | bytes 786464 | tf_op jit(solution)/shard_map/ppermute | solution.py:341
  851.9 11.1 %shard_map.239 = (bf16[256,4096]{1,0:T(8,128)(2,1)S(1)}, bf16[256,2048]{1,0:T(8,128)(2,1)}, bf16[256,2048]{1,0:T(8,128)(2,1)S(1)}) custom-call(s32[1]{0:T(128)} %bitcast.68.me_ref, bf16[1024,1024]{1,0:T(8,128)(2,1)S(1)} %copy-done.30, bf16[1024,4096]{1,0:T(8,128)(2,1)} %get-tuple-element.265.dz_ref, bf16[512,4096]{1,0:T(8,128)(2,1)} %collective-permute-done.136.got_ref), custom_call_target="tpu_custom_call" | custom-call | flops 4294967296 | bytes 16777216 | tf_op jit(solution)/shard_map/pallas_call | solution.py:530
  877.0 9.6 shard_map.242
  941.4 12.6 %collective-permute-done.142 = bf16[32,4096]{1,0:T(8,128)(2,1)S(1)} collective-permute-done((bf16[32,4096]{1,0:T(8,128)(2,1)S(1)}, bf16[32,4096]{1,0:T(8,128)(2,1)S(1)}, u32[]{:S(2)}, u32[]{:S(2)}) %collective-permute-start.142) | collective-permute-done | bytes 262176 | tf_op jit(solution)/shard_map/ppermute | solution.py:341
  958.4 18.1 %collective-permute-done.150 = bf16[32,4096]{1,0:T(8,128)(2,1)S(1)} collective-permute-done((bf16[32,4096]{1,0:T(8,128)(2,1)S(1)}, bf16[32,4096]{1,0:T(8,128)(2,1)S(1)}, u32[]{:S(2)}, u32[]{:S(2)}) %collective-permute-start.150) | collective-permute-done | bytes 262176 | tf_op jit(solution)/shard_map/ppermute | solution.py:341
  978.7 8.4 all-to-all-start.1
  987.2 12.3 %add_convert_fusion.2 = bf16[1024,1024]{1,0:T(8,128)(2,1)} fusion(f32[1024,1024]{1,0:T(8,128)} %get-tuple-element.170, bf16[1024,3072]{1,0:T(8,128)(2,1)} %shard_map.222.dz_ref, bf16[1024,3072]{1,0:T(8,128)(2,1)} %copy-done.18), kind=kOutput, calls=%fused_computation.53 | convolution fusion | flops 6444548096 | bytes 18874368 | tf_op jit(solution)/shard_map/dot_general | solution.py:27
  1004.8 8.6 all-to-all-done.1
  1015.1 11.0 %shard_map.244 = (f32[1024,512]{1,0:T(8,128)}, f32[1024,512]{1,0:T(8,128)}, f32[1024,512]{1,0:T(8,128)}) custom-call(s32[4]{0:T(128)S(1)} %convert_reduce_fusion.9.which_ref, f32[10,1024,1024]{2,1,0:T(8,128)} %basis_ref.1, bf16[4,1024,128]{2,1,0:T(8,128)(2,1)S(1)} %bitcast.282, f32[1024,512]{1,0:T(8,128)S(1)} %copy-done.26, f32[1024,512]{1,0:T(8,128)S(1)} %copy-done.27, ...), custom_call_target="tpu_custom_call" | custom-call | flops 2147483648 | bytes 29360128 | tf_op jit(solution)/shard_map/pallas_call | solution.py:607
  (753 shorter events, 444.8 us)
Async XLA Ops:
  0.7 55.4 %collective-permute-start.40 = (bf16[512,1024]{1,0:T(8,128)(2,1)}, bf16[512,1024]{1,0:T(8,128)(2,1)S(1)}, u32[]{:S(2)}, u32[]{:S(2)}) collective-permute-start(bf16[512,1024]{1,0:T(8,128)(2,1)} %bitcast.283), channel_id=1, source_target_pairs={{0,2},{1,3},{2,0},{3,1},{4,6},{5,7},{6,4},{7,5},{8,10},{9,11},{10,... | collective-permute-start | bytes 3145736 | tf_op jit(solution)/shard_map/ppermute | solution.py:341
  3.7 62.6 %collective-permute-start.39 = (bf16[512,1024]{1,0:T(8,128)(2,1)}, bf16[512,1024]{1,0:T(8,128)(2,1)}, u32[]{:S(2)}, u32[]{:S(2)}) collective-permute-start(bf16[512,1024]{1,0:T(8,128)(2,1)} %bitcast.284), channel_id=1, source_target_pairs={{0,1},{1,0},{2,3},{3,2},{4,5},{5,4},{6,7},{7,6},{8,9},{9,8},{10,11... | collective-permute-start | bytes 3145736 | tf_op jit(solution)/shard_map/ppermute | solution.py:341
  11.1 45.1 %all-to-all-start = ((bf16[32,4,32,128]{3,2,1,0:T(8,128)(2,1)}), bf16[32,4,32,128]{3,2,1,0:T(8,128)(2,1)}, u32[]{:S(2)}, u32[]{:S(2)}) async-start(bf16[32,4,32,128]{3,2,1,0:T(8,128)(2,1)} %bitcast.301), calls=%async_computation | async-start | bytes 2097152 | tf_op jit(solution)/shard_map/all_to_all | solution.py:673
  60.9 77.9 %collective-permute-start.76 = (bf16[32,4096]{1,0:T(8,128)(2,1)S(1)}, bf16[32,4096]{1,0:T(8,128)(2,1)S(1)}, u32[]{:S(2)}, u32[]{:S(2)}) collective-permute-start(bf16[32,4096]{1,0:T(8,128)(2,1)S(1)} %get-tuple-element.192), channel_id=1, source_target_pairs={{0,8},{1,9},{2,10},{3,11},{4,12},{5,13},{6,14},{7,15},{8,0},{9,1},... | collective-permute-start | bytes 786440 | tf_op jit(solution)/shard_map/ppermute | solution.py:341
  63.1 76.3 %collective-permute-start.77 = (bf16[32,4096]{1,0:T(8,128)(2,1)S(1)}, bf16[32,4096]{1,0:T(8,128)(2,1)S(1)}, u32[]{:S(2)}, u32[]{:S(2)}) collective-permute-start(bf16[32,4096]{1,0:T(8,128)(2,1)S(1)} %get-tuple-element.192), channel_id=1, source_target_pairs={{0,16},{1,17},{2,18},{3,19},{4,20},{5,21},{6,22},{7,23},{8,24},{9,... | collective-permute-start | bytes 786440 | tf_op jit(solution)/shard_map/ppermute | solution.py:341
  66.3 74.5 %collective-permute-start.78 = (bf16[32,4096]{1,0:T(8,128)(2,1)S(1)}, bf16[32,4096]{1,0:T(8,128)(2,1)S(1)}, u32[]{:S(2)}, u32[]{:S(2)}) collective-permute-start(bf16[32,4096]{1,0:T(8,128)(2,1)S(1)} %get-tuple-element.192), channel_id=1, source_target_pairs={{0,24},{1,25},{2,26},{3,27},{4,28},{5,29},{6,30},{7,31},{8,16},{9,... | collective-permute-start | bytes 786440 | tf_op jit(solution)/shard_map/ppermute | solution.py:341
  231.8 34.8 %collective-permute-start.58 = (bf16[128,1536]{1,0:T(8,128)(2,1)}, bf16[128,1536]{1,0:T(8,128)(2,1)S(1)}, u32[]{:S(2)}, u32[]{:S(2)}) collective-permute-start(bf16[128,1536]{1,0:T(8,128)(2,1)} %collective-permute-done.57.refs_14_), channel_id=1, source_target_pairs={{0,1},{1,0},{2,3},{3,2},{4,5},{5,4},{6,7},{7,6},{8,9},{9,8},{10,11... | collective-permute-start | bytes 1179656 | tf_op jit(solution)/shard_map/ppermute | solution.py:341
  260.2 36.5 %collective-permute-start.80 = (bf16[128,2048]{1,0:T(8,128)(2,1)S(1)}, bf16[128,2048]{1,0:T(8,128)(2,1)S(1)}, u32[]{:S(2)}, u32[]{:S(2)}) collective-permute-start(bf16[128,2048]{1,0:T(8,128)(2,1)S(1)} %pad_maximum_fusion.2.refs_0_), channel_id=1, source_target_pairs={{0,2},{1,3},{2,0},{3,1},{4,6},{5,7},{6,4},{7,5},{8,10},{9,11},{10,... | collective-permute-start | bytes 1572872 | tf_op jit(solution)/shard_map/ppermute | solution.py:341
  262.0 36.9 %collective-permute-start.82 = (bf16[128,2048]{1,0:T(8,128)(2,1)S(1)}, bf16[128,2048]{1,0:T(8,128)(2,1)}, u32[]{:S(2)}, u32[]{:S(2)}) collective-permute-start(bf16[128,2048]{1,0:T(8,128)(2,1)S(1)} %pad_maximum_fusion.2.refs_0_), channel_id=1, source_target_pairs={{0,4},{1,5},{2,6},{3,7},{4,0},{5,1},{6,2},{7,3},{8,12},{9,13},{10,... | collective-permute-start | bytes 1572872 | tf_op jit(solution)/shard_map/ppermute | solution.py:341
  265.6 35.1 %collective-permute-start.87 = (bf16[128,2048]{1,0:T(8,128)(2,1)S(1)}, bf16[128,2048]{1,0:T(8,128)(2,1)}, u32[]{:S(2)}, u32[]{:S(2)}) collective-permute-start(bf16[128,2048]{1,0:T(8,128)(2,1)S(1)} %pad_maximum_fusion.3.refs_8_), channel_id=1, source_target_pairs={{0,2},{1,3},{2,0},{3,1},{4,6},{5,7},{6,4},{7,5},{8,10},{9,11},{10,... | collective-permute-start | bytes 1572872 | tf_op jit(solution)/shard_map/ppermute | solution.py:341
  300.6 88.5 %collective-permute-start.62 = (bf16[128,2048]{1,0:T(8,128)(2,1)S(1)}, bf16[128,2048]{1,0:T(8,128)(2,1)S(1)}, u32[]{:S(2)}, u32[]{:S(2)}) collective-permute-start(bf16[128,2048]{1,0:T(8,128)(2,1)S(1)} %pad_maximum_fusion.refs_0_), channel_id=1, source_target_pairs={{0,1},{1,0},{2,3},{3,2},{4,5},{5,4},{6,7},{7,6},{8,9},{9,8},{10,11... | collective-permute-start | bytes 1572872 | tf_op jit(solution)/shard_map/ppermute | solution.py:341
  300.7 88.6 %collective-permute-start.69 = (bf16[128,2048]{1,0:T(8,128)(2,1)}, bf16[128,2048]{1,0:T(8,128)(2,1)S(1)}, u32[]{:S(2)}, u32[]{:S(2)}) collective-permute-start(bf16[128,2048]{1,0:T(8,128)(2,1)} %pad_maximum_fusion.1.refs_8_), channel_id=1, source_target_pairs={{0,1},{1,0},{2,3},{3,2},{4,5},{5,4},{6,7},{7,6},{8,9},{9,8},{10,11... | collective-permute-start | bytes 1572872 | tf_op jit(solution)/shard_map/ppermute | solution.py:341
  320.9 68.8 %collective-permute-start.67 = (bf16[128,2048]{1,0:T(8,128)(2,1)}, bf16[128,2048]{1,0:T(8,128)(2,1)S(1)}, u32[]{:S(2)}, u32[]{:S(2)}) collective-permute-start(bf16[128,2048]{1,0:T(8,128)(2,1)} %collective-permute-done.63.refs_2_), channel_id=1, source_target_pairs={{0,4},{1,5},{2,6},{3,7},{4,0},{5,1},{6,2},{7,3},{8,12},{9,13},{10,... | collective-permute-start | bytes 1572872 | tf_op jit(solution)/shard_map/ppermute | solution.py:341
  321.8 68.4 %collective-permute-start.64 = (bf16[128,2048]{1,0:T(8,128)(2,1)}, bf16[128,2048]{1,0:T(8,128)(2,1)S(1)}, u32[]{:S(2)}, u32[]{:S(2)}) collective-permute-start(bf16[128,2048]{1,0:T(8,128)(2,1)} %collective-permute-done.63.refs_2_), channel_id=1, source_target_pairs={{0,1},{1,0},{2,3},{3,2},{4,5},{5,4},{6,7},{7,6},{8,9},{9,8},{10,11... | collective-permute-start | bytes 1572872 | tf_op jit(solution)/shard_map/ppermute | solution.py:341
  321.8 68.0 %collective-permute-start.74 = (bf16[128,2048]{1,0:T(8,128)(2,1)S(1)}, bf16[128,2048]{1,0:T(8,128)(2,1)}, u32[]{:S(2)}, u32[]{:S(2)}) collective-permute-start(bf16[128,2048]{1,0:T(8,128)(2,1)S(1)} %collective-permute-done.72.refs_12_), channel_id=1, source_target_pairs={{0,2},{1,3},{2,0},{3,1},{4,6},{5,7},{6,4},{7,5},{8,10},{9,11},{10,... | collective-permute-start | bytes 1572872 | tf_op jit(solution)/shard_map/ppermute | solution.py:341
  404.3 54.3 %collective-permute-start.90 = (bf16[128,2048]{1,0:T(8,128)(2,1)}, bf16[128,2048]{1,0:T(8,128)(2,1)}, u32[]{:S(2)}, u32[]{:S(2)}) collective-permute-start(bf16[128,2048]{1,0:T(8,128)(2,1)} %collective-permute-done.89.refs_12_), channel_id=1, source_target_pairs={{0,1},{1,0},{2,3},{3,2},{4,5},{5,4},{6,7},{7,6},{8,9},{9,8},{10,11... | collective-permute-start | bytes 1572872 | tf_op jit(solution)/shard_map/ppermute | solution.py:341
  404.5 54.1 %collective-permute-start.83 = (bf16[128,2048]{1,0:T(8,128)(2,1)}, bf16[128,2048]{1,0:T(8,128)(2,1)}, u32[]{:S(2)}, u32[]{:S(2)}) collective-permute-start(bf16[128,2048]{1,0:T(8,128)(2,1)} %collective-permute-done.82.refs_4_), channel_id=1, source_target_pairs={{0,1},{1,0},{2,3},{3,2},{4,5},{5,4},{6,7},{7,6},{8,9},{9,8},{10,11... | collective-permute-start | bytes 1572872 | tf_op jit(solution)/shard_map/ppermute | solution.py:341
  411.0 47.7 %collective-permute-start.88 = (bf16[128,2048]{1,0:T(8,128)(2,1)}, bf16[128,2048]{1,0:T(8,128)(2,1)}, u32[]{:S(2)}, u32[]{:S(2)}) collective-permute-start(bf16[128,2048]{1,0:T(8,128)(2,1)} %collective-permute-done.87.refs_10_), channel_id=1, source_target_pairs={{0,1},{1,0},{2,3},{3,2},{4,5},{5,4},{6,7},{7,6},{8,9},{9,8},{10,11... | collective-permute-start | bytes 1572872 | tf_op jit(solution)/shard_map/ppermute | solution.py:341
  412.3 46.4 %collective-permute-start.85 = (bf16[128,2048]{1,0:T(8,128)(2,1)}, bf16[128,2048]{1,0:T(8,128)(2,1)}, u32[]{:S(2)}, u32[]{:S(2)}) collective-permute-start(bf16[128,2048]{1,0:T(8,128)(2,1)} %collective-permute-done.84.refs_6_), channel_id=1, source_target_pairs={{0,1},{1,0},{2,3},{3,2},{4,5},{5,4},{6,7},{7,6},{8,9},{9,8},{10,11... | collective-permute-start | bytes 1572872 | tf_op jit(solution)/shard_map/ppermute | solution.py:341
  412.3 46.4 %collective-permute-start.92 = (bf16[128,2048]{1,0:T(8,128)(2,1)}, bf16[128,2048]{1,0:T(8,128)(2,1)}, u32[]{:S(2)}, u32[]{:S(2)}) collective-permute-start(bf16[128,2048]{1,0:T(8,128)(2,1)} %collective-permute-done.91.refs_14_), channel_id=1, source_target_pairs={{0,1},{1,0},{2,3},{3,2},{4,5},{5,4},{6,7},{7,6},{8,9},{9,8},{10,11... | collective-permute-start | bytes 1572872 | tf_op jit(solution)/shard_map/ppermute | solution.py:341
  707.7 37.3 %collective-permute-start.112 = (bf16[512,1024]{1,0:T(8,128)(2,1)S(1)}, bf16[512,1024]{1,0:T(8,128)(2,1)S(1)}, u32[]{:S(2)}, u32[]{:S(2)}) collective-permute-start(bf16[512,1024]{1,0:T(8,128)(2,1)S(1)} %shard_map.229), channel_id=1, source_target_pairs={{0,1},{1,0},{2,3},{3,2},{4,5},{5,4},{6,7},{7,6},{8,9},{9,8},{10,11... | collective-permute-start | bytes 3145736 | tf_op jit(solution)/shard_map/ppermute | solution.py:341
  709.9 39.1 %collective-permute-start.104 = (bf16[512,1024]{1,0:T(8,128)(2,1)S(1)}, bf16[512,1024]{1,0:T(8,128)(2,1)S(1)}, u32[]{:S(2)}, u32[]{:S(2)}) collective-permute-start(bf16[512,1024]{1,0:T(8,128)(2,1)S(1)} %shard_map.226), channel_id=1, source_target_pairs={{0,1},{1,0},{2,3},{3,2},{4,5},{5,4},{6,7},{7,6},{8,9},{9,8},{10,11... | collective-permute-start | bytes 3145736 | tf_op jit(solution)/shard_map/ppermute | solution.py:341
  715.4 34.8 %collective-permute-start.94 = (bf16[512,1024]{1,0:T(8,128)(2,1)}, bf16[512,1024]{1,0:T(8,128)(2,1)}, u32[]{:S(2)}, u32[]{:S(2)}) collective-permute-start(bf16[512,1024]{1,0:T(8,128)(2,1)} %get-tuple-element.172), channel_id=1, source_target_pairs={{0,1},{1,0},{2,3},{3,2},{4,5},{5,4},{6,7},{7,6},{8,9},{9,8},{10,11... | collective-permute-start | bytes 3145736 | tf_op jit(solution)/shard_map/ppermute | solution.py:341
  733.6 65.6 %collective-permute-start.120 = (bf16[512,2048]{1,0:T(8,128)(2,1)}, bf16[512,2048]{1,0:T(8,128)(2,1)}, u32[]{:S(2)}, u32[]{:S(2)}) collective-permute-start(bf16[512,2048]{1,0:T(8,128)(2,1)} %shard_map.232), channel_id=1, source_target_pairs={{0,1},{1,0},{2,3},{3,2},{4,5},{5,4},{6,7},{7,6},{8,9},{9,8},{10,11... | collective-permute-start | bytes 6291464 | tf_op jit(solution)/shard_map/ppermute | solution.py:341
  733.7 90.4 %collective-permute-start.96 = (bf16[512,3072]{1,0:T(8,128)(2,1)}, bf16[512,3072]{1,0:T(8,128)(2,1)}, u32[]{:S(2)}, u32[]{:S(2)}) collective-permute-start(bf16[512,3072]{1,0:T(8,128)(2,1)} %shard_map.223), channel_id=1, source_target_pairs={{0,1},{1,0},{2,3},{3,2},{4,5},{5,4},{6,7},{7,6},{8,9},{9,8},{10,11... | collective-permute-start | bytes 9437192 | tf_op jit(solution)/shard_map/ppermute | solution.py:341
  745.0 105.9 %collective-permute-start.136 = (bf16[512,4096]{1,0:T(8,128)(2,1)}, bf16[512,4096]{1,0:T(8,128)(2,1)}, u32[]{:S(2)}, u32[]{:S(2)}) collective-permute-start(bf16[512,4096]{1,0:T(8,128)(2,1)} %shard_map.238), channel_id=1, source_target_pairs={{0,1},{1,0},{2,3},{3,2},{4,5},{5,4},{6,7},{7,6},{8,9},{9,8},{10,11... | collective-permute-start | bytes 12582920 | tf_op jit(solution)/shard_map/ppermute | solution.py:341
  787.4 86.5 %collective-permute-start.144 = (bf16[512,4096]{1,0:T(8,128)(2,1)S(1)}, bf16[512,4096]{1,0:T(8,128)(2,1)S(1)}, u32[]{:S(2)}, u32[]{:S(2)}) collective-permute-start(bf16[512,4096]{1,0:T(8,128)(2,1)S(1)} %shard_map.241), channel_id=1, source_target_pairs={{0,1},{1,0},{2,3},{3,2},{4,5},{5,4},{6,7},{7,6},{8,9},{9,8},{10,11... | collective-permute-start | bytes 12582920 | tf_op jit(solution)/shard_map/ppermute | solution.py:341
  866.2 38.1 %collective-permute-start.137 = (bf16[256,2048]{1,0:T(8,128)(2,1)}, bf16[256,2048]{1,0:T(8,128)(2,1)S(1)}, u32[]{:S(2)}, u32[]{:S(2)}) collective-permute-start(bf16[256,2048]{1,0:T(8,128)(2,1)} %get-tuple-element.91), channel_id=1, source_target_pairs={{0,2},{1,3},{2,0},{3,1},{4,6},{5,7},{6,4},{7,5},{8,10},{9,11},{10,... | collective-permute-start | bytes 3145736 | tf_op jit(solution)/shard_map/ppermute | solution.py:341
  867.0 37.3 %collective-permute-start.138 = (bf16[256,2048]{1,0:T(8,128)(2,1)S(1)}, bf16[256,2048]{1,0:T(8,128)(2,1)S(1)}, u32[]{:S(2)}, u32[]{:S(2)}) collective-permute-start(bf16[256,2048]{1,0:T(8,128)(2,1)S(1)} %get-tuple-element.92), channel_id=1, source_target_pairs={{0,4},{1,5},{2,6},{3,7},{4,0},{5,1},{6,2},{7,3},{8,12},{9,13},{10,... | collective-permute-start | bytes 3145736 | tf_op jit(solution)/shard_map/ppermute | solution.py:341
  916.1 85.0 %collective-permute-start.93 = (bf16[512,1024]{1,0:T(8,128)(2,1)}, bf16[512,1024]{1,0:T(8,128)(2,1)}, u32[]{:S(2)}, u32[]{:S(2)}) collective-permute-start(bf16[512,1024]{1,0:T(8,128)(2,1)} %get-tuple-element.171), channel_id=1, source_target_pairs={{0,1},{1,0},{2,3},{3,2},{4,5},{5,4},{6,7},{7,6},{8,9},{9,8},{10,11... | collective-permute-start | bytes 3145736 | tf_op jit(solution)/shard_map/ppermute | solution.py:341
  920.4 79.1 %collective-permute-start.156 = (f32[17,1024]{1,0:T(8,128)}, f32[17,1024]{1,0:T(8,128)S(1)}, u32[]{:S(2)}, u32[]{:S(2)}) collective-permute-start(f32[17,1024]{1,0:T(8,128)} %add.727), channel_id=1, source_target_pairs={{0,16},{1,17},{2,18},{3,19},{4,20},{5,21},{6,22},{7,23},{8,24},{9,... | collective-permute-start | bytes 208904 | tf_op jit(solution)/shard_map/ppermute | solution.py:341
  957.9 43.2 %collective-permute-start.95 = (bf16[512,1024]{1,0:T(8,128)(2,1)}, bf16[512,1024]{1,0:T(8,128)(2,1)}, u32[]{:S(2)}, u32[]{:S(2)}) collective-permute-start(bf16[512,1024]{1,0:T(8,128)(2,1)} %fusion.29), channel_id=1, source_target_pairs={{0,2},{1,3},{2,0},{3,1},{4,6},{5,7},{6,4},{7,5},{8,10},{9,11},{10,... | collective-permute-start | bytes 3145736 | tf_op jit(solution)/shard_map/ppermute | solution.py:341
  (274 other events, 5312.1 us)

commit v2 on v1

v2 whole, which is shorter than its diff:
```python
import functools

import jax
import jax.numpy as jnp
from jax import lax
from jax.experimental import pallas as pl
from jax.experimental.pallas import tpu as pltpu
from jax.sharding import PartitionSpec as P

HD = 64
STEP = 5
NH = 4
TR = 128
TQ = 128
TC = 64
AXES = ("dp", "fsdp")
HI = 8

bf = jnp.bfloat16
f32 = jnp.float32
eps_norm = 1e-05
beta_one = 0.9
beta_two = 0.999
adam_eps = 1e-08
rate_mat = 0.03
rate_vec = 0.25
decay = 0.01

def nt(a,b): return lax.dot_general(a,b,(((1,),(1,)),((),())),preferred_element_type=f32)
def nn(a,b): return lax.dot_general(a,b,(((1,),(0,)),((),())),preferred_element_type=f32)
def tn(a,b): return lax.dot_general(a,b,(((0,),(0,)),((),())),preferred_element_type=f32)

def spread(tile, scale):
    lane_head = lax.broadcasted_iota(jnp.int32, tile.shape, 1) // HD
    tile = tile * jnp.asarray(scale, tile.dtype) if scale != 1.0 else tile
    zero = jnp.zeros_like(tile)
    return jnp.concatenate([jnp.where(lane_head == h, tile, zero) for h in range(NH)], axis=0)

def collect(big):
    tr = big.shape[0] // NH
    lane_head = lax.broadcasted_iota(jnp.int32, (tr, big.shape[1]), 1) // HD
    out = big[:tr]
    for h in range(1, NH):
        out = jnp.where(lane_head == h, big[h*tr:(h+1)*tr], out)
    return out

def softmax_t(scores):
    top = jnp.max(scores, axis=0, keepdims=True)
    expo = jnp.exp(scores - top)
    total = jnp.sum(expo, axis=0, keepdims=True)
    return expo * (1.0 / total)

def seg_of(pos, lens_ref, row, segs):
    end = lens_ref[row, 0]
    seg = (pos >= end).astype(jnp.int32)
    for i in range(1, segs - 1):
        end = end + lens_ref[row, i]
        seg = seg + (pos >= end).astype(jnp.int32)
    return seg

def build_bias(bias_ref, lens_ref, row, segs, flip=False):
    n = bias_ref.shape[0]
    key = lax.broadcasted_iota(jnp.int32, (n, n), 0 if flip else 1)
    que = lax.broadcasted_iota(jnp.int32, (n, n), 1 if flip else 0)
    aseg = seg_of(lax.broadcasted_iota(jnp.int32, (n, 1), 0), lens_ref, row, segs)
    bseg = seg_of(lax.broadcasted_iota(jnp.int32, (1, n), 1), lens_ref, row, segs)
    ok = (aseg == bseg) & (key <= que)
    bias_ref[...] = jnp.where(ok, 0.0, -1e30)

def bias_tile(bias_ref, first, width, tr):
    piece = bias_ref[:width, first:first+tr]
    return jnp.concatenate([piece]*NH, axis=1)

SUBF = 4
def self_fwd_kernel(segs, lens_ref, q_ref, k_ref, v_ref, o_ref, bias_ref):
    row = pl.program_id(0)
    n = q_ref.shape[0]
    lanes = NH * HD
    @pl.when(pl.program_id(1) == 0)
    def _():
        build_bias(bias_ref, lens_ref, row, segs)
    for t in range(n // TQ):
        w = (t + 1) * TQ
        bias = jnp.concatenate([bias_ref[t*TQ:(t+1)*TQ, :w]] * NH, axis=0)
        for b in range(q_ref.shape[1] // lanes):
            cols = slice(b*lanes, (b+1)*lanes)
            big = spread(q_ref[t*TQ:(t+1)*TQ, cols], HD ** -0.5)
            s = nt(big, k_ref[:w, cols]) + bias
            e = jnp.exp(s - jnp.max(s, axis=1, keepdims=True))
            inv = 1.0 / jnp.sum(e, axis=1, keepdims=True)
            o_ref[t*TQ:(t+1)*TQ, cols] = collect(nn(e.astype(bf), v_ref[:w, cols]) * inv).astype(bf)

def self_fwd(lens, qkv, rows):
    tok, width3 = qkv.shape
    width = width3 // 3
    n = tok // rows
    lanes = NH * HD * SUBF
    nb = width // lanes
    spec = lambda off: pl.BlockSpec((n, lanes), lambda r, h, *_: (r, off*nb + h))
    return pl.pallas_call(
        functools.partial(self_fwd_kernel, lens.shape[1]),
        grid_spec=pltpu.PrefetchScalarGridSpec(num_scalar_prefetch=1, grid=(rows, nb),
            in_specs=[spec(0), spec(1), spec(2)], out_specs=spec(0),
            scratch_shapes=[pltpu.VMEM((n, n), f32)]),
        out_shape=jax.ShapeDtypeStruct((tok, width), bf),
        compiler_params=pltpu.CompilerParams(vmem_limit_bytes=48<<20),
        cost_estimate=pl.CostEstimate(flops=2*tok*n*width, bytes_accessed=8*tok*width, transcendentals=tok*n*width//HD//2),
    )(lens, qkv, qkv, qkv)

SUBSB = 4
SUBCB = 4
def self_bwd_kernel(segs, lens_ref, q_ref, k_ref, v_ref, g_ref, out_ref, bias_ref, ak_ref, av_ref):
    row = pl.program_id(0)
    part = pl.program_id(2)

    @pl.when((pl.program_id(1) == 0) & (part == 0))
    def _():
        build_bias(bias_ref, lens_ref, row, segs, True)

    @pl.when(part == 0)
    def _():
        self_bwd_body(q_ref, k_ref, v_ref, g_ref, bias_ref, out_ref, ak_ref, av_ref)

    @pl.when(part == 1)
    def _():
        out_ref[...] = ak_ref[...].astype(bf)

    @pl.when(part == 2)
    def _():
        out_ref[...] = av_ref[...].astype(bf)

def self_bwd_body(q_ref, k_ref, v_ref, g_ref, bias_ref, dq_ref, ak_ref, av_ref):
    n = q_ref.shape[0]
    lanes = NH * HD
    for t in reversed(range(n // TR)):
        w = (t + 1) * TR
        rows = slice(t*TR, (t+1)*TR)
        bias = bias_tile(bias_ref, t*TR, w, TR)
        for b in range(q_ref.shape[1] // lanes):
            cols = slice(b*lanes, (b+1)*lanes)
            big = spread(q_ref[rows, cols], HD ** -0.5)
            gbig = spread(g_ref[rows, cols], 1.0)
            k = k_ref[:w, cols]
            p = softmax_t(nt(k, big) + bias)
            u = p * nt(v_ref[:w, cols], gbig)
            ds = (u - p * jnp.sum(u, axis=0, keepdims=True)).astype(bf)
            av = nn(p.astype(bf), gbig)
            ak = nn(ds, big)
            if t == n // TR - 1:
                av_ref[:, cols] = av
                ak_ref[:, cols] = ak
            else:
                av_ref[:w, cols] += av
                ak_ref[:w, cols] += ak
            dq_ref[rows, cols] = (collect(tn(ds, k)) * HD ** -0.5).astype(bf)

def self_bwd(lens, qkv, grad, rows):
    tok, width3 = qkv.shape
    width = width3 // 3
    n = tok // rows
    lanes = NH * HD * SUBSB
    nb = width // lanes
    spec = lambda off: pl.BlockSpec((n, lanes), lambda r, h, *_: (r, off*nb + h))
    return pl.pallas_call(
        functools.partial(self_bwd_kernel, lens.shape[1]),
        grid_spec=pltpu.PrefetchScalarGridSpec(num_scalar_prefetch=1, grid=(rows, nb, 3),
            in_specs=[spec(0), spec(1), spec(2), spec(0)],
            out_specs=pl.BlockSpec((n, lanes), lambda r, h, p, *_: (r, p*nb + h)),
            scratch_shapes=[pltpu.VMEM((n, n), f32), pltpu.VMEM((n, lanes), f32), pltpu.VMEM((n, lanes), f32)]),
        out_shape=jax.ShapeDtypeStruct((tok, width3), bf),
        compiler_params=pltpu.CompilerParams(vmem_limit_bytes=48<<20),
        cost_estimate=pl.CostEstimate(flops=5*tok*n*width, bytes_accessed=14*tok*width, transcendentals=tok*n*width//HD//2),
    )(lens, qkv, qkv, qkv, grad)

def seg_bounds(lens_ref, row, segs):
    ends = []
    acc = 0
    for i in range(segs):
        acc = acc + lens_ref[row, i]
        ends.append(acc)
    return ends

def first_seg(ends, pos):
    seg = 0
    for e in ends[:-1]:
        seg = seg + (pos >= e).astype(jnp.int32)
    return seg

def load_keys(ids_ref, row, segs, nret, elen, src_ref, dst_ref):
    for j in range(segs * nret):
        ident = ids_ref[row, j]
        dst_ref[j*elen:(j+1)*elen, :] = src_ref[pl.ds(pl.multiple_of(ident*elen, elen), elen), :]

def lane_seg(ends, t):
    pos = lax.broadcasted_iota(jnp.int32, (1, TR), 1) + t * TR
    seg = jnp.zeros((1, TR), jnp.int32)
    for e in ends[:-1]:
        seg = seg + (pos >= e).astype(jnp.int32)
    return jnp.concatenate([seg]*NH, axis=1)

def row_seg(ends, t, lanes):
    pos = lax.broadcasted_iota(jnp.int32, (lanes, 1), 0) + t * lanes
    seg = jnp.zeros((lanes, 1), jnp.int32)
    for e in ends[:-1]:
        seg = seg + (pos >= e).astype(jnp.int32)
    return seg

SUBC = 4
def cross_fwd_kernel(segs, nret, elen, lens_ref, ids_ref, q_ref, k_ref, v_ref, o_ref, ks_ref, vs_ref):
    row = pl.program_id(1)
    n = q_ref.shape[0]
    width = nret * elen
    lanes = NH * HD
    load_keys(ids_ref, row, segs, nret, elen, k_ref, ks_ref)
    load_keys(ids_ref, row, segs, nret, elen, v_ref, vs_ref)
    ends = seg_bounds(lens_ref, row, segs)
    def tile(t, carry):
        rows = pl.ds(pl.multiple_of(t * TC, TC), TC)
        lo = first_seg(ends, t * TC)
        hi = first_seg(ends, t * TC + TC - 1)
        qseg = row_seg(ends, t, TC)
        def pair(s, acc):
            keys = pl.ds(pl.multiple_of(s * width, elen), width)
            got = []
            for b in range(q_ref.shape[1] // lanes):
                cols = slice(b*lanes, (b+1)*lanes)
                big = spread(q_ref[rows, cols], HD ** -0.5)
                sc = nt(big, ks_ref[keys, cols])
                e = jnp.exp(sc - jnp.max(sc, axis=1, keepdims=True))
                inv = 1.0 / jnp.sum(e, axis=1, keepdims=True)
                got.append(collect(nn(e.astype(bf), vs_ref[keys, cols]) * inv))
            for b, g in enumerate(got):
                cols = slice(b*lanes, (b+1)*lanes)
                o_ref[rows, cols] = jnp.where(qseg == s, g, o_ref[rows, cols].astype(f32)).astype(bf)
            return acc
        lax.fori_loop(lo, hi + 1, pair, 0)
        return carry
    lax.fori_loop(0, n // TC, tile, 0)

def cross_fwd(lens, ids, cq, kv, rows, nret, elen):
    tok, width = cq.shape
    n = tok // rows
    lanes = NH * HD * SUBC
    nb = width // lanes
    segs = lens.shape[1]
    pool = kv.shape[0]
    qspec = pl.BlockSpec((n, lanes), lambda h, r, *_: (r, h))
    kspec = lambda off: pl.BlockSpec((pool, lanes), lambda h, r, *_: (0, off*nb + h))
    keys = segs*nret*elen
    return pl.pallas_call(
        functools.partial(cross_fwd_kernel, segs, nret, elen),
        grid_spec=pltpu.PrefetchScalarGridSpec(num_scalar_prefetch=2, grid=(nb, rows),
            in_specs=[qspec, kspec(0), kspec(1)], out_specs=qspec,
            scratch_shapes=[pltpu.VMEM((keys, lanes), bf)]*2),
        out_shape=jax.ShapeDtypeStruct((tok, width), bf),
        compiler_params=pltpu.CompilerParams(vmem_limit_bytes=48<<20),
        cost_estimate=pl.CostEstimate(flops=2*tok*keys*width, bytes_accessed=8*tok*width, transcendentals=tok*keys*width//HD//2),
    )(lens, ids, cq, kv, kv)

def cross_bwd_kernel(segs, nret, elen, rows_n, lens_ref, ids_ref, q_ref, k_ref, v_ref, g_ref, dq_ref, dkv_ref, ks_ref, vs_ref, pk_ref, pv_ref):
    row = pl.program_id(1)

    @pl.when(row == 0)
    def _():
        pk_ref[...] = jnp.zeros_like(pk_ref)
        pv_ref[...] = jnp.zeros_like(pv_ref)

    @pl.when(row < rows_n)
    def _():
        cross_bwd_body(segs, nret, elen, row, lens_ref, ids_ref, q_ref, k_ref, v_ref, g_ref, dq_ref, ks_ref, vs_ref, pk_ref, pv_ref)

    @pl.when(row == rows_n - 1)
    def _():
        dkv_ref[...] = pk_ref[...].astype(bf)

    @pl.when(row == rows_n)
    def _():
        dkv_ref[...] = pv_ref[...].astype(bf)

def cross_bwd_body(segs, nret, elen, row, lens_ref, ids_ref, q_ref, k_ref, v_ref, g_ref, dq_ref, ks_ref, vs_ref, pk_ref, pv_ref):
    n = q_ref.shape[0]
    width = nret * elen
    lanes = NH * HD
    load_keys(ids_ref, row, segs, nret, elen, k_ref, ks_ref)
    load_keys(ids_ref, row, segs, nret, elen, v_ref, vs_ref)
    dq_ref[...] = jnp.zeros_like(dq_ref)
    ends = seg_bounds(lens_ref, row, segs)
    def tile(t, carry):
        rows = pl.ds(pl.multiple_of(t * TR, TR), TR)
        lo = first_seg(ends, t * TR)
        hi = first_seg(ends, t * TR + TR - 1)
        qseg = lane_seg(ends, t)
        kseg = row_seg(ends, t, TR)
        def pair(s, acc):
            keys = pl.ds(pl.multiple_of(s * width, elen), width)
            spots = [pl.ds(pl.multiple_of(ids_ref[row, s * nret + j] * elen, elen), elen) for j in range(nret)]
            made = []
            for b in range(q_ref.shape[1] // lanes):
                cols = slice(b*lanes, (b+1)*lanes)
                big = spread(q_ref[rows, cols], HD ** -0.5)
                gbig = spread(g_ref[rows, cols], 1.0)
                k = ks_ref[keys, cols]
                sc = nt(k, big)
                expo = jnp.exp(sc - jnp.max(sc, axis=0, keepdims=True))
                inv = 1.0 / jnp.sum(expo, axis=0, keepdims=True)
                p = expo * jnp.where(qseg == s, inv, 0.0)
                u = p * nt(vs_ref[keys, cols], gbig)
                ds = (u - p * jnp.sum(u, axis=0, keepdims=True)).astype(bf)
                made.append((cols, nn(p.astype(bf), gbig), nn(ds, big), collect(tn(ds, k)) * HD ** -0.5))
            for cols, av, ak, dq in made:
                for j, spot in enumerate(spots):
                    pv_ref[spot, cols] += av[j*elen:(j+1)*elen]
                    pk_ref[spot, cols] += ak[j*elen:(j+1)*elen]
                dq_ref[rows, cols] = jnp.where(kseg == s, dq, dq_ref[rows, cols].astype(f32)).astype(bf)
            return acc
        lax.fori_loop(lo, hi + 1, pair, 0)
        return carry
    lax.fori_loop(0, n // TR, tile, 0)

def cross_bwd(lens, ids, cq, kv, grad, rows, nret, elen):
    tok, width = cq.shape
    n = tok // rows
    pool = kv.shape[0]
    lanes = NH * HD * (SUBCB if pool <= 2048 else SUBCB // 2)
    nb = width // lanes
    segs = lens.shape[1]
    qspec = pl.BlockSpec((n, lanes), lambda h, r, *_: (jnp.minimum(r, rows - 1), h))
    kspec = lambda off: pl.BlockSpec((pool, lanes), lambda h, r, *_: (0, off*nb + h))
    keys = segs*nret*elen
    return pl.pallas_call(
        functools.partial(cross_bwd_kernel, segs, nret, elen, rows),
        grid_spec=pltpu.PrefetchScalarGridSpec(num_scalar_prefetch=2, grid=(nb, rows + 1),
            in_specs=[qspec, kspec(0), kspec(1), qspec],
            out_specs=[qspec, pl.BlockSpec((pool, lanes), lambda h, r, *_: (0, jnp.where(r < rows, 0, nb) + h))],
            scratch_shapes=[pltpu.VMEM((keys, lanes), bf)]*2+[pltpu.VMEM((pool, lanes), f32)]*2),
        out_shape=[jax.ShapeDtypeStruct((tok, width), bf), jax.ShapeDtypeStruct(kv.shape, bf)],
        compiler_params=pltpu.CompilerParams(vmem_limit_bytes=60<<20),
        cost_estimate=pl.CostEstimate(flops=5*tok*keys*width, bytes_accessed=14*tok*width, transcendentals=tok*keys*width//HD//2),
    )(lens, ids, cq, kv, kv, grad)


def norm_forward(resid, gain, shift):
    mean_row = jnp.mean(resid, axis=-1, keepdims=True)
    centred = resid - mean_row
    inv = lax.rsqrt(jnp.mean(centred * centred, axis=-1, keepdims=True) + eps_norm)
    normed = centred * inv
    return (normed * gain + shift, normed, inv)


def norm_backward(grad_out, normed, inv, gain):
    scaled = grad_out * gain
    grad_in = inv * (
        scaled
        - jnp.mean(scaled, axis=-1, keepdims=True)
        - normed * jnp.mean(scaled * normed, axis=-1, keepdims=True)
    )
    return (grad_in, jnp.sum(grad_out * normed, axis=0), jnp.sum(grad_out, axis=0))


def swap(value, mask):
    size = lax.axis_size(AXES)
    return lax.ppermute(value, AXES, [(i, i ^ mask) for i in range(size)])


def place_kernel(moves, count, where_ref, *refs):
    pieces, outs, sems = refs[: -count - 1], refs[-count - 1 : -1], refs[-1]
    copies = []
    for index, (src, row, rows, col, cols, slot, out, to) in enumerate(moves):
        first = pl.multiple_of(where_ref[slot], rows)
        copies.append(
            pltpu.make_async_copy(
                pieces[src].at[pl.ds(row, rows), pl.ds(col, cols)],
                outs[out].at[pl.ds(first, rows), pl.ds(to, cols)],
                sems.at[index],
            )
        )
    for copy in copies:
        copy.start()
    for copy in copies:
        copy.wait()


def place(pieces, where, moves, shapes):
    anywhere = pl.BlockSpec(memory_space=pl.ANY)
    total = sum(a * b for a, b in shapes)
    return pl.pallas_call(
        functools.partial(place_kernel, tuple(moves), len(shapes)),
        grid_spec=pltpu.PrefetchScalarGridSpec(
            num_scalar_prefetch=1,
            grid=(),
            in_specs=[anywhere] * len(pieces),
            out_specs=[anywhere] * len(shapes),
            scratch_shapes=[pltpu.SemaphoreType.DMA((len(moves),))],
        ),
        out_shape=[jax.ShapeDtypeStruct(shape, bf) for shape in shapes],
        compiler_params=pltpu.CompilerParams(vmem_limit_bytes=1 << 20),
        cost_estimate=pl.CostEstimate(flops=0, bytes_accessed=4 * total, transcendentals=0),
    )(where, *pieces)


class Gather:
    def __init__(self, shard, widths, me):
        self.rows, self.cols = shard.shape
        self.widths = widths
        self.me = me
        self.low = lax.axis_size(AXES) // HI
        self.shard = shard

    def far(self):
        self.got = [self.shard] + [swap(self.shard, HI * k) for k in range(1, self.low)]

    def first(self):
        half = self.cols // 2
        got, self.sub = self.got, self.low
        if self.rows % 16:
            order = (self.me // HI) ^ jnp.arange(self.low, dtype=jnp.int32)
            got = [jnp.take(jnp.stack(got), order, axis=0).reshape(-1, self.cols)]
            self.sub = 1
        self.own = [jnp.concatenate([g[:, p * half : (p + 1) * half] for g in got]) for p in (0, 1)]
        self.near = [swap(self.own[p], 2 << p) for p in (0, 1)]

    def second(self):
        self.wide = [jnp.concatenate([self.own[p], self.near[p]]) for p in (0, 1)]
        self.across = [swap(self.wide[p], 4 >> p) for p in (0, 1)]
        self.pair = [swap(self.wide[p], 1) for p in (0, 1)]

    def third(self):
        self.pair2 = [swap(self.across[p], 1) for p in (0, 1)]

    def finish(self):
        half = self.cols // 2
        block = self.low * self.rows
        rows = block // self.sub
        hi = self.me % HI
        lo = self.me // HI if self.sub > 1 else 0
        where = jnp.stack(
            [(hi ^ j) * block + (lo ^ k) * rows for j in range(HI) for k in range(self.sub)]
        )
        pieces, moves = [], []
        for p in (0, 1):
            near, across = 2 << p, 4 >> p
            for value, base in (
                (self.wide[p], 0),
                (self.across[p], across),
                (self.pair[p], 1),
                (self.pair2[p], across | 1),
            ):
                for i, j in enumerate((base, base | near)):
                    for k in range(self.sub):
                        start = 0
                        for out, width in enumerate(self.widths):
                            lower = max(start, p * half)
                            upper = min(start + width, (p + 1) * half)
                            if lower < upper:
                                moves.append(
                                    (
                                        len(pieces),
                                        i * block + k * rows,
                                        rows,
                                        lower - p * half,
                                        upper - lower,
                                        j * self.sub + k,
                                        out,
                                        lower - start,
                                    )
                                )
                            start += width
                pieces.append(value)
        return place(pieces, where, moves, [(HI * block, width) for width in self.widths])


class Passages:
    def __init__(self, own, me):
        self.have = {0: own}
        self.me = me

    def across(self):
        mask = lax.axis_size("fsdp") // 2
        while mask > 1:
            self.have.update({j | mask: swap(self.have[j], mask) for j in list(self.have)})
            mask //= 2

    def pair(self):
        self.have.update({j | 1: swap(self.have[j], 1) for j in list(self.have)})

    def finish(self):
        group = lax.axis_size("fsdp")
        rows, cols = self.have[0].shape
        index = self.me % group
        where = jnp.stack([(index ^ j) * rows for j in range(group)])
        moves = [(j, 0, rows, 0, cols, j, 0, 0) for j in range(group)]
        return place([self.have[j] for j in range(group)], where, moves, [(group * rows, cols)])[0]


class ReducePassages:
    def __init__(self, whole, me):
        self.group = lax.axis_size("fsdp")
        blocks = whole.reshape(self.group, -1, whole.shape[1])
        index = me % self.group
        self.have = {
            j: lax.dynamic_index_in_dim(blocks, index ^ j, 0, keepdims=False)
            for j in range(self.group)
        }
        self.mask = 1
        self.send()

    def send(self):
        self.got = {
            j: swap(self.have[j | self.mask], self.mask) for j in self.have if not j & self.mask
        }

    def step(self):
        self.have = {
            j: (self.have[j].astype(f32) + got.astype(f32)).astype(bf)
            for j, got in self.got.items()
        }
        self.mask *= 2
        if self.mask < self.group:
            self.send()


def grad_theirs_kernel(me_ref, x_ref, dz_ref, out_ref, xt_ref):
    block = x_ref.shape[1] // HI

    @pl.when(pl.program_id(0) == 0)
    def _():
        for at, j in enumerate((1, 3, 5, 7)):
            first = pl.multiple_of((j ^ me_ref[0]) * block, block)
            xt_ref[at * block : (at + 1) * block, :] = x_ref[:, pl.ds(first, block)].T

    out_ref[...] = nn(xt_ref[...], dz_ref[...]).astype(bf)


def grad_mine_kernel(half_tiles, me_ref, x_ref, dz_ref, got_ref, keep_ref, sa_ref, sb_ref, xt_ref):
    step = pl.program_id(0)
    block = x_ref.shape[1] // HI

    @pl.when(step == 0)
    def _():
        for at, j in enumerate((0, 2, 4, 6)):
            first = pl.multiple_of((j ^ me_ref[0]) * block, block)
            xt_ref[at * block : (at + 1) * block, :] = x_ref[:, pl.ds(first, block)].T

    full = (nn(xt_ref[...], dz_ref[...]) + got_ref[...].astype(f32)).astype(bf)
    b0, b2, b4, b6 = [full[i * block : (i + 1) * block] for i in range(4)]
    keep_ref[:block, :] = b0

    @pl.when(step < half_tiles)
    def _():
        keep_ref[block:, :] = b4
        sa_ref[:block, :] = b2
        sa_ref[block:, :] = b6

    @pl.when(step >= half_tiles)
    def _():
        keep_ref[block:, :] = b2
        sb_ref[:block, :] = b4
        sb_ref[block:, :] = b6


def second_kernel(half_tiles, keep_ref, ra_ref, rb_ref, out_ref, sa_ref, sb_ref):
    step = pl.program_id(0)
    block = out_ref.shape[0]

    @pl.when(step < half_tiles)
    def _():
        total = (keep_ref[...].astype(f32) + ra_ref[...].astype(f32)).astype(bf)
        out_ref[...] = total[:block]
        sa_ref[...] = total[block:]

    @pl.when(step >= half_tiles)
    def _():
        total = (keep_ref[...].astype(f32) + rb_ref[...].astype(f32)).astype(bf)
        out_ref[...] = total[:block]
        sb_ref[...] = total[block:]


def third_kernel(half_tiles, rp, lo_ref, keep_ref, ra_ref, rb_ref, *refs):
    outs, sum_ref = refs[:-1], refs[-1]
    step = pl.program_id(0)

    @pl.when(step < half_tiles)
    def _():
        sum_ref[...] = keep_ref[...].astype(f32) + ra_ref[...].astype(f32)

    @pl.when(step >= half_tiles)
    def _():
        sum_ref[...] = keep_ref[...].astype(f32) + rb_ref[...].astype(f32)

    for k, out in enumerate(outs):
        first = pl.multiple_of((lo_ref[0] ^ k) * rp, rp)
        out[...] = sum_ref[pl.ds(first, rp), :].astype(bf)


class Reduce:
    def __init__(self, lhs, dz, me):
        self.lhs, self.dz = lhs, dz
        self.tokens, self.width = lhs.shape
        self.cols = dz.shape[1]
        self.low = lax.axis_size(AXES) // HI
        self.block = self.width // HI
        self.tile = min(512, self.cols // 2)
        self.tiles = self.cols // self.tile
        self.half_tiles = self.tiles // 2
        self.lo = me // HI
        self.hi = (me % HI).reshape(1)
        self.a_map = lambda t, *_: (0, jnp.minimum(t, self.half_tiles - 1))
        self.b_map = lambda t, *_: (0, jnp.maximum(t - self.half_tiles, 0))
        self.big = pltpu.CompilerParams(vmem_limit_bytes=40 << 20)
        self.cost = pl.CostEstimate(
            flops=self.tokens * self.width * self.cols,
            bytes_accessed=4 * self.tokens * self.cols,
            transcendentals=0,
        )

    def spec(self, rows, index=None):
        return pl.BlockSpec((rows, self.tile), index or (lambda t, *_: (0, t)))

    def shape(self, rows, cols):
        return jax.ShapeDtypeStruct((rows, cols), bf)

    def theirs(self):
        half = self.width // 2
        out = pl.pallas_call(
            grad_theirs_kernel,
            grid_spec=pltpu.PrefetchScalarGridSpec(
                num_scalar_prefetch=1,
                grid=(self.tiles,),
                in_specs=[
                    pl.BlockSpec((self.tokens, self.width), lambda t, *_: (0, 0)),
                    self.spec(self.tokens),
                ],
                out_specs=self.spec(half),
                scratch_shapes=[pltpu.VMEM((half, self.tokens), bf)],
            ),
            out_shape=self.shape(half, self.cols),
            compiler_params=self.big,
            cost_estimate=self.cost,
        )(self.hi, self.lhs, self.dz)
        self.got = swap(out, 1)
        return out

    def mine(self):
        half = self.width // 2
        two = 2 * self.block
        self.keep, send_a, send_b = pl.pallas_call(
            functools.partial(grad_mine_kernel, self.half_tiles),
            grid_spec=pltpu.PrefetchScalarGridSpec(
                num_scalar_prefetch=1,
                grid=(self.tiles,),
                in_specs=[
                    pl.BlockSpec((self.tokens, self.width), lambda t, *_: (0, 0)),
                    self.spec(self.tokens),
                    self.spec(half),
                ],
                out_specs=[self.spec(two), self.spec(two, self.a_map), self.spec(two, self.b_map)],
                scratch_shapes=[pltpu.VMEM((half, self.tokens), bf)],
            ),
            out_shape=[
                self.shape(two, self.cols),
                self.shape(two, self.cols // 2),
                self.shape(two, self.cols // 2),
            ],
            compiler_params=self.big,
            cost_estimate=self.cost,
        )(self.hi, self.lhs, self.dz, self.got)
        self.ra, self.rb = swap(send_a, 2), swap(send_b, 4)
        return self.keep

    def second(self):
        two, one = 2 * self.block, self.block
        self.keep, send_a, send_b = pl.pallas_call(
            functools.partial(second_kernel, self.half_tiles),
            grid=(self.tiles,),
            in_specs=[self.spec(two), self.spec(two, self.a_map), self.spec(two, self.b_map)],
            out_specs=[self.spec(one), self.spec(one, self.a_map), self.spec(one, self.b_map)],
            out_shape=[
                self.shape(one, self.cols),
                self.shape(one, self.cols // 2),
                self.shape(one, self.cols // 2),
            ],
            compiler_params=pltpu.CompilerParams(vmem_limit_bytes=16 << 20),
            cost_estimate=pl.CostEstimate(
                flops=one * self.cols, bytes_accessed=12 * one * self.cols, transcendentals=0
            ),
        )(self.keep, self.ra, self.rb)
        self.ra, self.rb = swap(send_a, 4), swap(send_b, 2)
        return self.keep

    def third(self):
        one = self.block
        rp = one // self.low
        if rp % 16:
            last = self.keep.astype(f32) + jnp.concatenate([self.ra, self.rb], axis=1).astype(f32)
            chunks = last.reshape(self.low, rp, self.cols)
            parts = [
                lax.dynamic_index_in_dim(chunks, self.lo ^ k, 0, keepdims=False).astype(bf)
                for k in range(self.low)
            ]
        else:
            parts = pl.pallas_call(
                functools.partial(third_kernel, self.half_tiles, rp),
                grid_spec=pltpu.PrefetchScalarGridSpec(
                    num_scalar_prefetch=1,
                    grid=(self.tiles,),
                    in_specs=[
                        self.spec(one),
                        self.spec(one, self.a_map),
                        self.spec(one, self.b_map),
                    ],
                    out_specs=[self.spec(rp)] * self.low,
                    scratch_shapes=[pltpu.VMEM((one, self.tile), f32)],
                ),
                out_shape=[self.shape(rp, self.cols)] * self.low,
                compiler_params=pltpu.CompilerParams(vmem_limit_bytes=16 << 20),
                cost_estimate=pl.CostEstimate(
                    flops=one * self.cols, bytes_accessed=8 * one * self.cols, transcendentals=0
                ),
            )(self.lo.reshape(1), self.keep, self.ra, self.rb)
        self.parts = [parts[0]] + [swap(parts[k], HI * k) for k in range(1, self.low)]
        return parts[0]

    def last(self):
        return sum(part.astype(f32) for part in self.parts).astype(bf)


def up_kernel(h_ref, w_ref, b_ref, act_ref, slope_ref):
    upper = nn(h_ref[...], w_ref[...]) + b_ref[...]
    dens = jnp.exp(-0.5 * upper * upper)
    t = 1.0 / (1.0 + (0.3275911 * 2.0**-0.5) * jnp.abs(upper))
    poly = 0.5 * 1.061405429
    for coef in (-1.453152027, 1.421413741, -0.284496736, 0.254829592):
        poly = poly * t + 0.5 * coef
    tail = poly * t * dens
    cdf = jnp.where(upper < 0.0, tail, 1.0 - tail)
    act_ref[...] = (upper * cdf).astype(bf)
    slope_ref[...] = (cdf + upper * dens * (2.0 * jnp.pi) ** -0.5).astype(bf)


def up_project(h, w, b):
    tokens, width = h.shape
    cols = w.shape[1]
    tile = 512
    spec = pl.BlockSpec((tokens, tile), lambda t: (0, t))
    return pl.pallas_call(
        up_kernel,
        grid=(cols // tile,),
        in_specs=[
            pl.BlockSpec((tokens, width), lambda t: (0, 0)),
            pl.BlockSpec((width, tile), lambda t: (0, t)),
            pl.BlockSpec((1, tile), lambda t: (0, t)),
        ],
        out_specs=[spec, spec],
        out_shape=[jax.ShapeDtypeStruct((tokens, cols), bf)] * 2,
        compiler_params=pltpu.CompilerParams(vmem_limit_bytes=40 << 20),
        cost_estimate=pl.CostEstimate(
            flops=2 * tokens * width * cols,
            bytes_accessed=4 * tokens * cols + 2 * width * cols,
            transcendentals=tokens * cols,
        ),
    )(h, w, b)


def update_kernel(which_ref, basis_ref, g_ref, m_ref, v_ref, w_ref, first_ref, second_ref, new_ref):
    corr_one = 1.0 - beta_one**STEP
    corr_two = 1.0 - beta_two**STEP
    basis = basis_ref[0].astype(bf)
    turned = tn(g_ref[0], basis).T
    first = beta_one * m_ref[...] + (1.0 - beta_one) * turned
    second = beta_two * v_ref[...] + (1.0 - beta_two) * turned * turned
    first_ref[...] = first
    second_ref[...] = second
    step = (first / corr_one) / (jnp.sqrt(second / corr_two) + adam_eps)
    back = nn(basis, step.astype(bf))
    weights = w_ref[...]
    new_ref[...] = weights - rate_mat * (back + decay * weights)


def update(which, bases, grads, first, second, weights):
    count, width, cols = grads.shape
    spec = pl.BlockSpec((width, cols), lambda s, *_: (0, s))
    sds = jax.ShapeDtypeStruct(weights.shape, f32)
    return pl.pallas_call(
        update_kernel,
        grid_spec=pltpu.PrefetchScalarGridSpec(
            num_scalar_prefetch=1,
            grid=(count,),
            in_specs=[
                pl.BlockSpec((1, width, width), lambda s, which_ref: (which_ref[s], 0, 0)),
                pl.BlockSpec((1, width, cols), lambda s, *_: (s, 0, 0)),
                spec,
                spec,
                spec,
            ],
            out_specs=[spec] * 3,
        ),
        out_shape=[sds] * 3,
        compiler_params=pltpu.CompilerParams(vmem_limit_bytes=48 << 20),
        cost_estimate=pl.CostEstimate(
            flops=4 * width * width * cols * count,
            bytes_accessed=4 * count * width * (width + 6 * cols),
            transcendentals=0,
        ),
    )(which, bases, grads, first, second, weights)


def shards(
    hidden_in,
    cotangent,
    seg_lengths,
    retrieved,
    encoder_states,
    master_weights,
    first_moment,
    second_moment,
    slot_block,
    bases,
    vector_params,
    vector_first,
    vector_second,
):
    micro, rows_dev, row_len, width = hidden_in.shape
    segs = seg_lengths.shape[2]
    nret = retrieved.shape[3]
    elen = encoder_states.shape[1]
    size = lax.axis_size(AXES)
    low = size // HI
    me = lax.axis_index(AXES)
    nblk = slot_block.shape[0]
    per_dev = nblk // size
    bcols = master_weights.shape[1] // per_dev
    cols = nblk * bcols
    rp = width // size
    rows = micro * rows_dev
    tokens = rows * row_len
    hidden = (cols - 8 * width) // 2
    nvec = vector_params.shape[0]
    pass_grp = encoder_states.shape[0] * lax.axis_size("fsdp")
    lens = seg_lengths.reshape(rows, segs)
    ids = retrieved.reshape(rows, segs * nret) - lax.axis_index("dp") * pass_grp
    inverse = jnp.zeros((nblk,), jnp.int32).at[slot_block].set(jnp.arange(nblk, dtype=jnp.int32))

    passages = Passages(encoder_states.reshape(-1, width), me)
    passages.across()
    send = (
        master_weights.astype(bf)
        .reshape(HI, low, rp, per_dev, bcols)
        .transpose(1, 0, 3, 2, 4)
        .reshape(size, per_dev, rp, bcols)
    )
    slots = lax.all_to_all(send, AXES, 0, 0, tiled=True).reshape(nblk, rp, bcols)
    natural = jnp.take(slots, inverse, axis=0).transpose(1, 0, 2).reshape(rp, cols)

    vcols = vector_params.shape[1]
    vec_pad = jnp.pad(vector_params.astype(bf).T, ((0, 0), (0, 2 * bcols - nvec)))
    zero = jnp.zeros((width,), f32)
    x = hidden_in.reshape(tokens, width)
    cot = cotangent.reshape(tokens, width)

    cuts = [0, 3 * width, 7 * width, 8 * width + hidden, cols]
    parts = [natural[:, i:j] for i, j in zip(cuts[:-1], cuts[1:])]
    parts[0] = jnp.concatenate([parts[0], vec_pad], axis=1)
    widths = [(3 * width, 2 * bcols), (width, width, 2 * width), (width, hidden), (hidden,)]
    ga, gb, gc, gd = [Gather(p, w, me) for p, w in zip(parts, widths)]

    def after(value, *done):
        return lax.optimization_barrier((value, done))[0]

    ga.far()
    ga.first()
    gb.shard = after(gb.shard, ga.own)
    gb.far()
    ga.second()
    gb.got = after(gb.got, ga.wide)
    gb.first()
    gc.shard = after(gc.shard, gb.own)
    gc.far()
    ga.across = after(ga.across, gb.own)
    ga.third()
    gb.near = after(gb.near, gc.shard)
    gb.second()
    gc.got = after(gc.got, gb.wide)
    gc.first()
    ga.pair2, gd.shard = after((ga.pair2, gd.shard), gc.own)
    gd.far()
    passages.have = after(passages.have, ga.pair2)
    passages.pair()
    w_qkv, w_vec = ga.finish()
    vecs = (
        w_vec[:, :nvec].reshape(HI, low, rp, nvec).transpose(3, 1, 0, 2).reshape(nvec, width)
    ).astype(f32)

    b_up = vecs[13:].reshape(1, -1)
    qkv = (nn(x, w_qkv) + jnp.concatenate([vecs[0], zero, vecs[1]])).astype(bf)
    passages.have = after(passages.have, qkv)
    enc = passages.finish()
    attn = self_fwd(lens, after(qkv, enc), rows)
    gb.across, gc.near, gd.got = after((gb.across, gc.near, gd.got), attn)
    gb.third()
    gc.second()
    gd.got = after(gd.got, gc.wide)
    gd.first()
    gb.pair2 = after(gb.pair2, gd.own)
    w_o, c_q, c_kv = gb.finish()
    hid_one, normed_one, inv_one = norm_forward(
        x.astype(f32) + nn(attn, w_o) + vecs[2], vecs[3], vecs[4]
    )
    hid_low = hid_one.astype(bf)
    cq = (nn(hid_low, c_q) + vecs[5]).astype(bf)
    kv = (nn(after(enc, cq), c_kv) + jnp.concatenate([zero, vecs[6]])).astype(bf)
    attn_c = cross_fwd(lens, ids, cq, kv, rows, nret, elen)
    gc.across, gd.near = after((gc.across, gd.near), attn_c)
    gc.third()
    gd.second()
    gc.pair2 = after(gc.pair2, gd.wide)
    c_o, w_up = gc.finish()
    hid_two, normed_two, inv_two = norm_forward(
        hid_one + nn(attn_c, c_o) + vecs[7], vecs[8], vecs[9]
    )
    hid_two_low = hid_two.astype(bf)
    act, slope = up_project(hid_two_low, w_up, b_up)
    gd.across = after(gd.across, act)
    gd.third()
    (w_dt,) = gd.finish()
    out, normed_three, inv_three = norm_forward(
        hid_two + nt(act, w_dt) + vecs[10], vecs[11], vecs[12]
    )

    d_resid3, d_g3, d_e3 = norm_backward(cot.astype(f32), normed_three, inv_three, vecs[11])
    d_branch3 = d_resid3.astype(bf)
    d_bdown = jnp.sum(d_branch3.astype(f32), axis=0)
    r_dt = Reduce(d_branch3, act, me)
    done = r_dt.theirs()
    d_branch3 = after(d_branch3, done)
    d_upper = (nn(d_branch3, w_dt) * slope.astype(f32)).astype(bf)
    d_bup = jnp.sum(d_upper.astype(f32), axis=0)
    r_dt.got = after(r_dt.got, d_upper)
    done = r_dt.mine()
    r_up = Reduce(hid_two_low, after(d_upper, done), me)
    done = r_up.theirs()
    d_upper = after(d_upper, done)
    d_hid_two = d_resid3 + nt(d_upper, w_up)
    d_resid2, d_g2, d_e2 = norm_backward(d_hid_two, normed_two, inv_two, vecs[8])
    d_branch2 = d_resid2.astype(bf)
    d_cbo = jnp.sum(d_branch2.astype(f32), axis=0)
    r_dt.ra = after(r_dt.ra, d_branch2)
    done = r_dt.second()
    r_up.got = after(r_up.got, done)
    done = r_up.mine()
    d_branch2 = after(d_branch2, done)
    d_attn_c = nt(d_branch2, c_o).astype(bf)
    r_co = Reduce(attn_c, after(d_branch2, d_attn_c), me)
    done = r_co.theirs()
    r_dt.ra = after(r_dt.ra, done)
    done = r_dt.third()
    r_up.ra = after(r_up.ra, done)
    done = r_up.second()
    g_cq, g_ckv = cross_bwd(lens, ids, cq, kv, after(d_attn_c, done), rows, nret, elen)
    r_dt.parts, r_co.got = after((r_dt.parts, r_co.got), g_cq)
    s_dt = r_dt.last()
    r_co.got = after(r_co.got, s_dt)
    done = r_co.mine()
    r_up.ra = after(r_up.ra, done)
    done = r_up.third()
    r_cq = Reduce(hid_low, after(g_cq, done), me)
    done = r_cq.theirs()
    r_ckv = Reduce(enc, after(g_ckv, done), me)
    done = r_ckv.theirs()
    d_cbq = jnp.sum(g_cq.astype(f32), axis=0)
    d_cbv = jnp.sum(g_ckv[:, width:].astype(f32), axis=0)
    d_hid_one = d_resid2 + nt(after(g_cq, done), c_q)
    d_resid1, d_g1, d_e1 = norm_backward(d_hid_one, normed_one, inv_one, vecs[3])
    d_branch1 = d_resid1.astype(bf)
    d_bo = jnp.sum(d_branch1.astype(f32), axis=0)
    r_up.parts, r_co.ra = after((r_up.parts, r_co.ra), d_branch1)
    s_up = r_up.last()
    r_co.ra = after(r_co.ra, s_up)
    done = r_co.second()
    r_cq.got = after(r_cq.got, done)
    done = r_cq.mine()
    r_ckv.got = after(r_ckv.got, done)
    done = r_ckv.mine()
    r_o = Reduce(attn, after(d_branch1, done), me)
    done = r_o.theirs()
    d_attn = nt(after(d_branch1, done), w_o).astype(bf)
    d_enc = nt(after(g_ckv, d_attn), c_kv).astype(bf)
    r_enc = ReducePassages(d_enc, me)
    r_co.ra = after(r_co.ra, r_enc.have)
    done = r_co.third()
    r_cq.ra = after(r_cq.ra, done)
    done = r_cq.second()
    r_ckv.ra = after(r_ckv.ra, done)
    done = r_ckv.second()
    r_o.got = after(r_o.got, done)
    done = r_o.mine()
    r_enc.got = after(r_enc.got, done)
    r_enc.step()
    r_co.parts = after(r_co.parts, r_enc.have)
    s_co = r_co.last()
    g_in = self_bwd(lens, qkv, after(d_attn, r_enc.have, s_co), rows)
    r_in = Reduce(x, g_in, me)
    done = r_in.theirs()
    r_cq.ra, r_ckv.ra, r_o.ra = after((r_cq.ra, r_ckv.ra, r_o.ra), done)
    done = r_cq.third(), r_ckv.third(), r_o.second()
    g_in = after(g_in, done)
    d_bq = jnp.sum(g_in[:, :width].astype(f32), axis=0)
    d_bv = jnp.sum(g_in[:, 2 * width :].astype(f32), axis=0)
    r_in.got = after(r_in.got, d_bq, d_bv)
    done = r_in.mine()
    while r_enc.mask < r_enc.group:
        r_enc.step()
    encoder_grad = r_enc.have[0]
    r_cq.parts, r_ckv.parts = after((r_cq.parts, r_ckv.parts), done)
    s_cq, s_ckv = r_cq.last(), r_ckv.last()
    done = done, s_cq, s_ckv
    vec_grad = jnp.concatenate(
        [
            jnp.stack(
                [d_bq, d_bv, d_bo, d_g1, d_e1, d_cbq, d_cbv, d_cbo, d_g2, d_e2, d_bdown, d_g3, d_e3]
            ),
            d_bup.reshape(-1, width),
        ],
        axis=0,
    )
    g_in = after(g_in, done)
    d_x = (d_resid1 + nt(g_in, w_qkv)).astype(bf)
    r_o.ra = after(r_o.ra, d_x)
    done = r_o.third()
    r_in.ra = after(r_in.ra, done)
    done = r_in.second()
    vec_out = lax.optimization_barrier(vec_grad).reshape(nvec, size, vcols).transpose(1, 0, 2).reshape(size, nvec * vcols)
    vec_high = lax.optimization_barrier(vec_out.astype(bf))
    vec_low = (vec_out - vec_high.astype(f32)).astype(bf)
    vec_out = jnp.pad(
        jnp.concatenate([vec_high, vec_low], axis=1),
        ((0, 0), (0, 16 * bcols - 2 * nvec * vcols)),
    ).reshape(size, 16, bcols)
    r_in.ra, vec_out, r_o.parts = after((r_in.ra, vec_out, r_o.parts), done)
    done = r_in.third()
    s_o = r_o.last()
    r_in.parts = after(r_in.parts, s_o)
    s_in = r_in.last()

    mine = jnp.concatenate([s_in, s_o, s_cq, s_ckv, s_co, s_up, s_dt], axis=1)
    blocks = jnp.take(mine.reshape(rp, nblk, bcols).transpose(1, 0, 2), slot_block, axis=0)
    blocks = jnp.concatenate([blocks.reshape(size, per_dev * rp, bcols), vec_out], axis=1)
    got = lax.all_to_all(blocks, AXES, 0, 0, tiled=True)
    vec_in = got[:, per_dev * rp :].reshape(size, 16 * bcols)[:, : 2 * nvec * vcols].astype(f32)
    share_vec = jnp.sum(vec_in.reshape(size, 2, nvec, vcols), axis=(0, 1))
    grads = (
        got[:, : per_dev * rp]
        .reshape(low, HI, per_dev, rp, bcols)
        .transpose(2, 1, 0, 3, 4)
        .reshape(per_dev, width, bcols)
    )
    my_blocks = lax.dynamic_slice(slot_block, (me * per_dev,), (per_dev,))
    bounds = jnp.array([width * j for j in range(1, 9)] + [8 * width + hidden], jnp.int32)
    which = jnp.sum((my_blocks[:, None] * bcols >= bounds[None, :]).astype(jnp.int32), axis=1)
    first_new, second_new, master_new = update(
        which, bases, grads, first_moment, second_moment, master_weights
    )
    corr_one = 1.0 - beta_one**STEP
    corr_two = 1.0 - beta_two**STEP
    vf_new = beta_one * vector_first + (1.0 - beta_one) * share_vec
    vs_new = beta_two * vector_second + (1.0 - beta_two) * share_vec * share_vec
    vec_new = vector_params - rate_vec * (vf_new / corr_one) / (
        jnp.sqrt(vs_new / corr_two) + adam_eps
    )
    return (
        out.astype(bf).reshape(hidden_in.shape),
        d_x.reshape(hidden_in.shape),
        encoder_grad.reshape(encoder_states.shape),
        first_new,
        second_new,
        master_new,
        vf_new,
        vs_new,
        vec_new,
        share_vec,
    )


def solution(mesh):
    spread_rows = P(None, ("dp", "fsdp"), None, None)
    spread_cols = P(None, ("dp", "fsdp"))
    in_specs = (
        spread_rows,
        spread_rows,
        P(None, ("dp", "fsdp"), None),
        spread_rows,
        P(("dp", "fsdp"), None, None),
        spread_cols,
        spread_cols,
        spread_cols,
        P(),
        P(),
        spread_cols,
        spread_cols,
        spread_cols,
    )
    out_specs = (spread_rows, spread_rows, P(("dp", "fsdp"), None, None)) + (spread_cols,) * 7
    return jax.shard_map(shards, mesh=mesh, in_specs=in_specs, out_specs=out_specs, check_vma=False)
```

time: 1040 us -> 890 us (0.86)
  matrix products: 160 us -> 110 us
  Pallas kernels: 343 us -> 299 us
  waiting for transfers between devices: 253 us -> 213 us
  starting transfers between devices: 164 us -> 127 us
  local copies, waits for them, and re-layouts: 57.8 us -> 86 us
    ppermute x157 -> x106, waiting for transfers between devices: 244 us -> 159 us  [swap(): return lax.ppermute(value, AXES, [(i, i ^ mask) for i in range(size)])]
    dot_general x7 -> x6, matrix products: 94 us -> 43.6 us  [nn(): lax.dot_general(a, b, (((1,), (0,)), ((), ())), preferred_element_type=f32)]
    pallas_call x27 -> x34, Pallas kernels: 115 us -> 163 us  [the longest x7 45 us: mine(): pl.pallas_call(functools.partial(grad_mine_kernel, self.half_tiles), grid...]
    ppermute x157 -> x106, starting transfers between devices: 150 us -> 114 us  [swap(): return lax.ppermute(value, AXES, [(i, i ^ mask) for i in range(size)])]
    pallas_call x1, Pallas kernels: 62.3 us -> 26.1 us  [cross_fwd(): pl.pallas_call(functools.partial(cross_fwd_kernel, segs, nret, elen), gri...]
    pallas_call x1, Pallas kernels: 89.5 us -> 55 us  [cross_bwd(): pl.pallas_call(functools.partial(cross_bwd_kernel, segs, nret, elen, rows...]
    all_to_all x1, waiting for transfers between devices: 0.01 us -> 25.1 us  [shards(): lax.all_to_all(send, AXES, 0, 0, tiled=True).reshape(nblk, rp, bcols)]
    all_to_all x1, waiting for transfers between devices: 8.59 us -> 28.8 us  [shards(): got = lax.all_to_all(blocks, AXES, 0, 0, tiled=True)]
  transfers between devices with their start and end apart: 159 -> 108, of which waited for: 50 -> 31; matrix products, arithmetic and copies ran while one was open for 13% -> 19% of each run, Pallas kernels for 19% -> 23%
where the time goes in v2:
time: 890 us; the launch traced here: 883 us
  Pallas kernels  299 us (34%)
  waiting for transfers between devices  213 us (24%)
  starting transfers between devices  127 us (14%)
  matrix products  110 us (12%)
  local copies, waits for them, and re-layouts  86 us (10%)
  other arithmetic  45.3 us (5%)
    ppermute x106, waiting for transfers between devices, swap(): return lax.ppermute(value, AXES, [(i, i ^ mask) for i in range(size)])  159 us
    ppermute x106, starting transfers between devices, swap(): return lax.ppermute(value, AXES, [(i, i ^ mask) for i in range(size)])  114 us
    dot_general x7, matrix products, nt(): lax.dot_general(a, b, (((1,), (1,)), ((), ())), preferred_element_type=f32)  66.8 us
    pallas_call x1, Pallas kernels, cross_bwd(): pl.pallas_call(functools.partial(cross_bwd_kernel, segs, nret, elen, rows...  55 us
    unnamed x200, local copies, waits for them, and re-layouts  48.7 us
    pallas_call x7, Pallas kernels, mine(): pl.pallas_call(functools.partial(grad_mine_kernel, self.half_tiles), grid...  45 us
    dot_general x6, matrix products, nn(): lax.dot_general(a, b, (((1,), (0,)), ((), ())), preferred_element_type=f32)  43.6 us
    pallas_call x7, Pallas kernels, theirs(): pl.pallas_call(grad_theirs_kernel, grid_spec=pltpu.PrefetchScalarGridSpec...  41.7 us
  transfers between devices with their start and end apart: 108, of which 31 were waited for; matrix products, arithmetic and copies ran while one was open for 19% of the time, Pallas kernels for 23%

profile of v2, /device:TPU:0, one launch (start us, length us, event | category | flops | bytes accessed | tf_op | source)
XLA Modules:
  0.0 883.1 jit_solution(2174599003307298056)
XLA Ops:
  12.4 25.1 %all-to-all-done = bf16[32,4,32,128]{3,2,1,0:T(8,128)(2,1)S(1)} async-done(((bf16[32,4,32,128]{3,2,1,0:T(8,128)(2,1)}), bf16[32,4,32,128]{3,2,1,0:T(8,128)(2,1)S(1)}, u32[]{:S(2)}, u32[]{:S(2)}) %all-to-all-start) | async-done | bytes 1048608 | tf_op jit(solution)/shard_map/all_to_all | solution.py:851
  49.1 9.1 %collective-permute-done.1 = bf16[32,3328]{1,0:T(8,128)(2,1)S(1)} collective-permute-done((bf16[32,3328]{1,0:T(8,128)(2,1)S(1)}, bf16[32,3328]{1,0:T(8,128)(2,1)S(1)}, u32[]{:S(2)}, u32[]{:S(2)}) %collective-permute-start.1) | collective-permute-done | bytes 213024 | tf_op jit(solution)/shard_map/ppermute | solution.py:362
  75.4 11.8 %collective-permute-done.8 = bf16[32,4096]{1,0:T(8,128)(2,1)S(1)} collective-permute-done((bf16[32,4096]{1,0:T(8,128)(2,1)S(1)}, bf16[32,4096]{1,0:T(8,128)(2,1)S(1)}, u32[]{:S(2)}, u32[]{:S(2)}) %collective-permute-start.8) | collective-permute-done | bytes 262176 | tf_op jit(solution)/shard_map/ppermute | solution.py:362
  107.3 12.4 %collective-permute-done.14 = bf16[32,5120]{1,0:T(8,128)(2,1)S(1)} collective-permute-done((bf16[32,5120]{1,0:T(8,128)(2,1)S(1)}, bf16[32,5120]{1,0:T(8,128)(2,1)S(1)}, u32[]{:S(2)}, u32[]{:S(2)}) %collective-permute-start.14) | collective-permute-done | bytes 327712 | tf_op jit(solution)/shard_map/ppermute | solution.py:362
  122.3 15.9 %collective-permute-done.6.refs_5_ = bf16[256,1664]{1,0:T(8,128)(2,1)S(1)} collective-permute-done((bf16[256,1664]{1,0:T(8,128)(2,1)}, bf16[256,1664]{1,0:T(8,128)(2,1)S(1)}, u32[]{:S(2)}, u32[]{:S(2)}) %collective-permute-start.6) | collective-permute-done | bytes 852000 | tf_op jit(solution)/shard_map/ppermute | solution.py:362
  174.9 11.2 %fusion.q_ref.k_ref.v_ref = bf16[1024,3072]{1,0:T(8,128)(2,1)} fusion(f32[3072]{0:T(1024)S(1)} %pad_maximum_fusion.9, bf16[1024,1024]{1,0:T(8,128)(2,1)} %bitcast.187, bf16[1024,3072]{1,0:T(8,128)(2,1)} %copy-done.38), kind=kOutput, calls=%fused_computation.8 | convolution fusion | flops 6448742400 | bytes 14692352 | tf_op jit(solution)/shard_map/dot_general | solution.py:30
  190.7 13.4 %shard_map.215.x_ref = bf16[1024,1024]{1,0:T(8,128)(2,1)S(1)} custom-call(s32[2,4]{1,0:T(2,128)S(1)} %bitcast.184, bf16[1024,3072]{1,0:T(8,128)(2,1)} %fusion.q_ref.k_ref.v_ref, bf16[1024,3072]{1,0:T(8,128)(2,1)} %fusion.q_ref.k_ref.v_ref, bf16[1024,3072]{1,0:T(8,128)(2,1)} %fusion.q_ref.k_ref.v_ref), custom_call_target="tpu_custom_call" | custom-call | flops 1073741824 | bytes 8388608 | tf_op jit(solution)/shard_map/pallas_call | solution.py:100
  220.1 8.0 shard_map.216
  235.2 11.0 %add_convert_fusion.k_ref.v_ref = bf16[2048,2048]{1,0:T(8,128)(2,1)} fusion(f32[2048]{0:T(1024)S(1)} %concatenate.93, bf16[2048,1024]{1,0:T(8,128)(2,1)S(1)} %shard_map.214.x_ref, bf16[1024,2048]{1,0:T(8,128)(2,1)S(1)} %get-tuple-element.254), kind=kOutput, calls=%fused_computation.5 | convolution fusion | flops 8598323200 | bytes 16785408 | tf_op jit(solution)/shard_map/dot_general | solution.py:30
  246.2 26.1 %shard_map.217.x_ref = bf16[1024,1024]{1,0:T(8,128)(2,1)S(1)} custom-call(s32[2,4]{1,0:T(2,128)S(1)} %bitcast.185, s32[2,20]{1,0:T(2,128)S(1)} %sub.90.ids_ref, bf16[1024,1024]{1,0:T(8,128)(2,1)S(1)} %add_convert_fusion.4.q_ref, bf16[2048,2048]{1,0:T(8,128)(2,1)} %add_convert_fusion.k_ref.v_ref, bf16[2048,2048]{1,0:T(8,128)(2,1)} %add_convert_fusion.k_ref.v_ref), custom_call_target="tpu_custom_call" | custom-call | flops 2684354560 | bytes 8388608 | tf_op jit(solution)/shard_map/pallas_call | solution.py:250
  296.0 26.2 %shard_map.219 = (bf16[1024,4096]{1,0:T(8,128)(2,1)S(1)}, bf16[1024,4096]{1,0:T(8,128)(2,1)}) custom-call(bf16[1024,1024]{1,0:T(8,128)(2,1)S(1)} %fusion.9.h_ref.x_ref, bf16[1024,4096]{1,0:T(8,128)(2,1)} %copy-done.37, f32[1,4096]{1,0:T(1,128)S(1)} %reshape.232.b_ref), custom_call_target="tpu_custom_call" | custom-call | flops 8589934592 | bytes 25165824 | tf_op jit(solution)/shard_map/pallas_call | solution.py:745
  336.0 12.7 %fusion.32 = (f32[1024]{0:T(1024)S(1)}, f32[1024,1024]{1,0:T(8,128)S(1)}) fusion(f32[1024]{0:T(1024)S(1)} %add.522, bf16[1024,4096]{1,0:T(8,128)(2,1)} %copy-done.55, bf16[1024,4096]{1,0:T(8,128)(2,1)S(1)} %shard_map.220, f32[1024]{0:T(1024)S(1)} %copy-done.76, f32[1024]{0:T(1024)S(1)} %mul.169, f32[1024]{0:T(1024)S(1)} %add_rsqrt_fusion.1, ...), kind=kOutput, calls=%fused_computation.179 | convolution fusion | flops 8597273600 | bytes 25190400 | tf_op jit(solution)/shard_map/dot_general | solution.py:29
  357.1 10.5 %shard_map.221 = bf16[512,4096]{1,0:T(8,128)(2,1)} custom-call(s32[1]{0:T(128)} %bitcast.50.me_ref, bf16[1024,1024]{1,0:T(8,128)(2,1)S(1)} %get-tuple-element.266.x_ref, bf16[1024,4096]{1,0:T(8,128)(2,1)} %copy-done.55), custom_call_target="tpu_custom_call" | custom-call | flops 4294967296 | bytes 16777216 | tf_op jit(solution)/shard_map/pallas_call | solution.py:624
  367.9 13.7 %convert_reduce_fusion = (f32[4096]{0:T(1024)}, bf16[1024,4096]{1,0:T(8,128)(2,1)}) fusion(bf16[1024,4096]{1,0:T(8,128)(2,1)} %get-tuple-element.267, bf16[1024,1024]{1,0:T(8,128)(2,1)S(1)} %get-tuple-element.266.x_ref, bf16[1024,4096]{1,0:T(8,128)(2,1)S(1)} %shard_map.220), kind=kOutput, calls=%fused_computation.3 | convolution fusion | flops 8610902016 | bytes 27279360 | tf_op jit(solution)/shard_map/dot_general | solution.py:30
  381.7 10.6 %shard_map.222 = (bf16[256,4096]{1,0:T(8,128)(2,1)S(1)}, bf16[256,2048]{1,0:T(8,128)(2,1)}, bf16[256,2048]{1,0:T(8,128)(2,1)}) custom-call(s32[1]{0:T(128)} %bitcast.50.me_ref, bf16[1024,1024]{1,0:T(8,128)(2,1)S(1)} %get-tuple-element.266.x_ref, bf16[1024,4096]{1,0:T(8,128)(2,1)} %copy-done.55, bf16[512,4096]{1,0:T(8,128)(2,1)S(1)} %collective-permute-done.47.got_ref), custom_call_target="tpu_custom_call" | custom-call | flops 4294967296 | bytes 16777216 | tf_op jit(solution)/shard_map/pallas_call | solution.py:646
  392.3 10.4 %shard_map.223 = bf16[512,4096]{1,0:T(8,128)(2,1)} custom-call(s32[1]{0:T(128)} %bitcast.50.me_ref, bf16[1024,1024]{1,0:T(8,128)(2,1)S(1)} %copy-done.16, bf16[1024,4096]{1,0:T(8,128)(2,1)} %get-tuple-element.271.dz_ref), custom_call_target="tpu_custom_call" | custom-call | flops 4294967296 | bytes 16777216 | tf_op jit(solution)/shard_map/pallas_call | solution.py:624
  406.2 18.8 %multiply_reduce_fusion = (f32[1024]{0:T(1024)}, f32[1024]{0:T(1024)S(1)}, f32[1024]{0:T(1024)S(1)}, f32[1024]{0:T(1024)}, f32[1024,1024]{1,0:T(8,128)}) fusion(f32[1024,1024]{1,0:T(8,128)} %copy-done.59, f32[1024]{0:T(1024)S(1)} %add_rsqrt_fusion.1, f32[1024]{0:T(1024)S(1)} %broadcast_multiply_fusion.6, f32[1024]{0:T(1024)S(1)} %mul.169, ...), kind=kOutput, calls=%fused_computation.21 | convolution fusion | flops 8600416256 | bytes 29388800 | tf_op jit(solution)/shard_map/dot_general | solution.py:29
  436.9 11.3 %shard_map.225 = (bf16[256,4096]{1,0:T(8,128)(2,1)S(1)}, bf16[256,2048]{1,0:T(8,128)(2,1)}, bf16[256,2048]{1,0:T(8,128)(2,1)}) custom-call(s32[1]{0:T(128)} %bitcast.50.me_ref, bf16[1024,1024]{1,0:T(8,128)(2,1)S(1)} %copy-done.16, bf16[1024,4096]{1,0:T(8,128)(2,1)} %get-tuple-element.271.dz_ref, bf16[512,4096]{1,0:T(8,128)(2,1)} %collective-permute-done.48.got_ref), custom_call_target="tpu_custom_call" | custom-call | flops 4294967296 | bytes 16777216 | tf_op jit(solution)/shard_map/pallas_call | solution.py:646
  465.0 7.5 collective-permute-done.51.ra_ref
  483.0 55.0 %shard_map.229 = (bf16[1024,1024]{1,0:T(8,128)(2,1)}, bf16[2048,2048]{1,0:T(8,128)(2,1)}) custom-call(s32[2,4]{1,0:T(2,128)} %bitcast.183, s32[2,20]{1,0:T(2,128)} %copy-done.36, bf16[1024,1024]{1,0:T(8,128)(2,1)} %copy-done.19, bf16[2048,2048]{1,0:T(8,128)(2,1)} %add_convert_fusion.k_ref.v_ref, bf16[2048,2048]{1,0:T(8,128)(2,1)} %add_convert_fusion.k_ref.v_ref, ...), custom_call_target="tpu_custom_call" | custom-call | flops 6710886400 | bytes 14680064 | tf_op jit(solution)/shard_map/pallas_call | solution.py:330
  557.9 7.9 shard_map.233
  585.8 9.3 %collective-permute-done.64 = bf16[32,4096]{1,0:T(8,128)(2,1)S(1)} collective-permute-done((bf16[32,4096]{1,0:T(8,128)(2,1)S(1)}, bf16[32,4096]{1,0:T(8,128)(2,1)S(1)}, u32[]{:S(2)}, u32[]{:S(2)}) %collective-permute-start.64) | collective-permute-done | bytes 262176 | tf_op jit(solution)/shard_map/ppermute | solution.py:362
  598.3 8.1 shard_map.236
  611.0 12.7 %convolution_convert_fusion = bf16[2048,1024]{1,0:T(8,128)(2,1)} fusion(bf16[2048,2048]{1,0:T(8,128)(2,1)} %get-tuple-element.326.dz_ref, bf16[1024,2048]{1,0:T(8,128)(2,1)S(1)} %copy-done.40), kind=kOutput, calls=%fused_computation.46 | convolution fusion | flops 8592031744 | bytes 16777216 | tf_op jit(solution)/shard_map/dot_general | solution.py:29
  643.9 9.4 %collective-permute-done.71.ra_ref = bf16[256,1024]{1,0:T(8,128)(2,1)S(1)} collective-permute-done((bf16[256,1024]{1,0:T(8,128)(2,1)S(1)}, bf16[256,1024]{1,0:T(8,128)(2,1)S(1)}, u32[]{:S(2)}, u32[]{:S(2)}) %collective-permute-start.71) | collective-permute-done | bytes 524320 | tf_op jit(solution)/shard_map/ppermute | solution.py:362
  666.8 14.0 %collective-permute-done.93 = bf16[512,1024]{1,0:T(8,128)(2,1)S(1)} collective-permute-done((bf16[512,1024]{1,0:T(8,128)(2,1)S(1)}, bf16[512,1024]{1,0:T(8,128)(2,1)S(1)}, u32[]{:S(2)}, u32[]{:S(2)}) %collective-permute-start.93) | collective-permute-done | bytes 1048608 | tf_op jit(solution)/shard_map/ppermute | solution.py:362
  683.2 30.3 %shard_map.242.dz_ref = bf16[1024,3072]{1,0:T(8,128)(2,1)} custom-call(s32[2,4]{1,0:T(2,128)S(1)} %bitcast.186, bf16[1024,3072]{1,0:T(8,128)(2,1)} %fusion.q_ref.k_ref.v_ref, bf16[1024,3072]{1,0:T(8,128)(2,1)} %fusion.q_ref.k_ref.v_ref, bf16[1024,3072]{1,0:T(8,128)(2,1)} %fusion.q_ref.k_ref.v_ref, bf16[1024,1024]{1,0:T(8,128)(2,1)S(1)} %convolution_convert_fusion.1.g_ref), custom_call_target="tpu_custom_call" | custom-call | flops 2684354560 | bytes 14680064 | tf_op jit(solution)/shard_map/pallas_call | solution.py:164
  758.9 8.5 shard_map.247
  775.9 9.8 %add_convert_fusion.2 = bf16[1024,1024]{1,0:T(8,128)(2,1)} fusion(f32[1024,1024]{1,0:T(8,128)S(1)} %copy-done.61, bf16[1024,3072]{1,0:T(8,128)(2,1)S(1)} %bitcast.181, bf16[1024,3072]{1,0:T(8,128)(2,1)} %copy-done.38), kind=kOutput, calls=%fused_computation.26 | convolution fusion | flops 6444548096 | bytes 18874368 | tf_op jit(solution)/shard_map/dot_general | solution.py:29
  816.1 8.5 collective-permute-done.104
  838.3 28.8 %all-to-all-done.1 = bf16[32,144,128]{2,1,0:T(8,128)(2,1)} async-done(((bf16[32,144,128]{2,1,0:T(8,128)(2,1)}), bf16[32,144,128]{2,1,0:T(8,128)(2,1)}, u32[]{:S(2)}, u32[]{:S(2)}) %all-to-all-start.1) | async-done | bytes 1179680 | tf_op jit(solution)/shard_map/all_to_all | solution.py:1047
  871.9 11.0 %shard_map.251 = (f32[1024,512]{1,0:T(8,128)}, f32[1024,512]{1,0:T(8,128)}, f32[1024,512]{1,0:T(8,128)}) custom-call(s32[4]{0:T(128)S(1)} %convert_reduce_fusion.10.which_ref, f32[10,1024,1024]{2,1,0:T(8,128)} %basis_ref.1, bf16[4,1024,128]{2,1,0:T(8,128)(2,1)S(1)} %bitcast.182, f32[1024,512]{1,0:T(8,128)S(1)} %copy-done.13, f32[1024,512]{1,0:T(8,128)S(1)} %copy-done.14, ...), custom_call_target="tpu_custom_call" | custom-call | flops 2147483648 | bytes 29360128 | tf_op jit(solution)/shard_map/pallas_call | solution.py:783
  (558 shorter events, 401.9 us)
Async XLA Ops:
  3.9 33.5 %all-to-all-start = ((bf16[32,4,32,128]{3,2,1,0:T(8,128)(2,1)}), bf16[32,4,32,128]{3,2,1,0:T(8,128)(2,1)S(1)}, u32[]{:S(2)}, u32[]{:S(2)}) async-start(bf16[32,4,32,128]{3,2,1,0:T(8,128)(2,1)} %bitcast.35), calls=%async_computation | async-start | bytes 2097152 | tf_op jit(solution)/shard_map/all_to_all | solution.py:851
  89.9 53.3 %collective-permute-start.19 = (bf16[512,1024]{1,0:T(8,128)(2,1)}, bf16[512,1024]{1,0:T(8,128)(2,1)}, u32[]{:S(2)}, u32[]{:S(2)}) collective-permute-start(bf16[512,1024]{1,0:T(8,128)(2,1)} %bitcast.46.refs_0_), channel_id=1, source_target_pairs={{0,2},{1,3},{2,0},{3,1},{4,6},{5,7},{6,4},{7,5},{8,10},{9,11},{10,... | collective-permute-start | bytes 3145736 | tf_op jit(solution)/shard_map/ppermute | solution.py:362
  104.2 34.0 %collective-permute-start.6 = (bf16[256,1664]{1,0:T(8,128)(2,1)}, bf16[256,1664]{1,0:T(8,128)(2,1)S(1)}, u32[]{:S(2)}, u32[]{:S(2)}) collective-permute-start(bf16[256,1664]{1,0:T(8,128)(2,1)} %constant_dynamic-update-slice_fusion.5.refs_4_), channel_id=1, source_target_pairs={{0,2},{1,3},{2,0},{3,1},{4,6},{5,7},{6,4},{7,5},{8,10},{9,11},{10,... | collective-permute-start | bytes 2555912 | tf_op jit(solution)/shard_map/ppermute | solution.py:362
  105.9 32.3 %collective-permute-start.4 = (bf16[256,1664]{1,0:T(8,128)(2,1)}, bf16[256,1664]{1,0:T(8,128)(2,1)S(1)}, u32[]{:S(2)}, u32[]{:S(2)}) collective-permute-start(bf16[256,1664]{1,0:T(8,128)(2,1)} %constant_dynamic-update-slice_fusion.refs_0_), channel_id=1, source_target_pairs={{0,4},{1,5},{2,6},{3,7},{4,0},{5,1},{6,2},{7,3},{8,12},{9,13},{10,... | collective-permute-start | bytes 2555912 | tf_op jit(solution)/shard_map/ppermute | solution.py:362
  143.2 29.3 %collective-permute-start.20 = (bf16[512,1024]{1,0:T(8,128)(2,1)}, bf16[512,1024]{1,0:T(8,128)(2,1)}, u32[]{:S(2)}, u32[]{:S(2)}) collective-permute-start(bf16[512,1024]{1,0:T(8,128)(2,1)} %bitcast.46.refs_0_), channel_id=1, source_target_pairs={{0,1},{1,0},{2,3},{3,2},{4,5},{5,4},{6,7},{7,6},{8,9},{9,8},{10,11... | collective-permute-start | bytes 3145736 | tf_op jit(solution)/shard_map/ppermute | solution.py:362
  143.2 29.3 %collective-permute-start.21 = (bf16[512,1024]{1,0:T(8,128)(2,1)}, bf16[512,1024]{1,0:T(8,128)(2,1)}, u32[]{:S(2)}, u32[]{:S(2)}) collective-permute-start(bf16[512,1024]{1,0:T(8,128)(2,1)} %collective-permute-done.19.refs_2_), channel_id=1, source_target_pairs={{0,1},{1,0},{2,3},{3,2},{4,5},{5,4},{6,7},{7,6},{8,9},{9,8},{10,11... | collective-permute-start | bytes 3145736 | tf_op jit(solution)/shard_map/ppermute | solution.py:362
  145.8 58.3 %collective-permute-start.23 = (bf16[256,2048]{1,0:T(8,128)(2,1)S(1)}, bf16[256,2048]{1,0:T(8,128)(2,1)}, u32[]{:S(2)}, u32[]{:S(2)}) collective-permute-start(bf16[256,2048]{1,0:T(8,128)(2,1)S(1)} %constant_dynamic-update-slice_fusion.15.refs_4_), channel_id=1, source_target_pairs={{0,2},{1,3},{2,0},{3,1},{4,6},{5,7},{6,4},{7,5},{8,10},{9,11},{10,... | collective-permute-start | bytes 3145736 | tf_op jit(solution)/shard_map/ppermute | solution.py:362
  163.3 40.8 %collective-permute-start.22 = (bf16[256,2048]{1,0:T(8,128)(2,1)S(1)}, bf16[256,2048]{1,0:T(8,128)(2,1)}, u32[]{:S(2)}, u32[]{:S(2)}) collective-permute-start(bf16[256,2048]{1,0:T(8,128)(2,1)S(1)} %constant_dynamic-update-slice_fusion.10.refs_0_), channel_id=1, source_target_pairs={{0,4},{1,5},{2,6},{3,7},{4,0},{5,1},{6,2},{7,3},{8,12},{9,13},{10,... | collective-permute-start | bytes 3145736 | tf_op jit(solution)/shard_map/ppermute | solution.py:362
  165.1 39.5 %collective-permute-start.26 = (bf16[32,4096]{1,0:T(8,128)(2,1)}, bf16[32,4096]{1,0:T(8,128)(2,1)}, u32[]{:S(2)}, u32[]{:S(2)}) collective-permute-start(bf16[32,4096]{1,0:T(8,128)(2,1)} %get-tuple-element.245), channel_id=1, source_target_pairs={{0,8},{1,9},{2,10},{3,11},{4,12},{5,13},{6,14},{7,15},{8,0},{9,1},... | collective-permute-start | bytes 786440 | tf_op jit(solution)/shard_map/ppermute | solution.py:362
  172.5 32.2 %collective-permute-start.27 = (bf16[32,4096]{1,0:T(8,128)(2,1)}, bf16[32,4096]{1,0:T(8,128)(2,1)}, u32[]{:S(2)}, u32[]{:S(2)}) collective-permute-start(bf16[32,4096]{1,0:T(8,128)(2,1)} %get-tuple-element.245), channel_id=1, source_target_pairs={{0,16},{1,17},{2,18},{3,19},{4,20},{5,21},{6,22},{7,23},{8,24},{9,... | collective-permute-start | bytes 786440 | tf_op jit(solution)/shard_map/ppermute | solution.py:362
  172.5 32.1 %collective-permute-start.28 = (bf16[32,4096]{1,0:T(8,128)(2,1)}, bf16[32,4096]{1,0:T(8,128)(2,1)}, u32[]{:S(2)}, u32[]{:S(2)}) collective-permute-start(bf16[32,4096]{1,0:T(8,128)(2,1)} %get-tuple-element.245), channel_id=1, source_target_pairs={{0,24},{1,25},{2,26},{3,27},{4,28},{5,29},{6,30},{7,31},{8,16},{9,... | collective-permute-start | bytes 786440 | tf_op jit(solution)/shard_map/ppermute | solution.py:362
  205.9 66.5 %collective-permute-start.34 = (bf16[256,2560]{1,0:T(8,128)(2,1)S(1)}, bf16[256,2560]{1,0:T(8,128)(2,1)}, u32[]{:S(2)}, u32[]{:S(2)}) collective-permute-start(bf16[256,2560]{1,0:T(8,128)(2,1)S(1)} %constant_dynamic-update-slice_fusion.25.refs_4_), channel_id=1, source_target_pairs={{0,2},{1,3},{2,0},{3,1},{4,6},{5,7},{6,4},{7,5},{8,10},{9,11},{10,... | collective-permute-start | bytes 3932168 | tf_op jit(solution)/shard_map/ppermute | solution.py:362
  216.4 55.9 %collective-permute-start.36 = (bf16[128,2048]{1,0:T(8,128)(2,1)}, bf16[128,2048]{1,0:T(8,128)(2,1)}, u32[]{:S(2)}, u32[]{:S(2)}) collective-permute-start(bf16[128,2048]{1,0:T(8,128)(2,1)} %pad_maximum_fusion.6), channel_id=1, source_target_pairs={{0,4},{1,5},{2,6},{3,7},{4,0},{5,1},{6,2},{7,3},{8,12},{9,13},{10,... | collective-permute-start | bytes 1572872 | tf_op jit(solution)/shard_map/ppermute | solution.py:362
  216.7 55.7 %collective-permute-start.35 = (bf16[128,2048]{1,0:T(8,128)(2,1)}, bf16[128,2048]{1,0:T(8,128)(2,1)S(1)}, u32[]{:S(2)}, u32[]{:S(2)}) collective-permute-start(bf16[128,2048]{1,0:T(8,128)(2,1)} %pad_maximum_fusion.5), channel_id=1, source_target_pairs={{0,2},{1,3},{2,0},{3,1},{4,6},{5,7},{6,4},{7,5},{8,10},{9,11},{10,... | collective-permute-start | bytes 1572872 | tf_op jit(solution)/shard_map/ppermute | solution.py:362
  218.4 54.0 %collective-permute-start.33 = (bf16[256,2560]{1,0:T(8,128)(2,1)}, bf16[256,2560]{1,0:T(8,128)(2,1)}, u32[]{:S(2)}, u32[]{:S(2)}) collective-permute-start(bf16[256,2560]{1,0:T(8,128)(2,1)} %constant_dynamic-update-slice_fusion.20.refs_0_), channel_id=1, source_target_pairs={{0,4},{1,5},{2,6},{3,7},{4,0},{5,1},{6,2},{7,3},{8,12},{9,13},{10,... | collective-permute-start | bytes 3932168 | tf_op jit(solution)/shard_map/ppermute | solution.py:362
  279.4 46.1 %collective-permute-start.42 = (bf16[256,2048]{1,0:T(8,128)(2,1)}, bf16[256,2048]{1,0:T(8,128)(2,1)}, u32[]{:S(2)}, u32[]{:S(2)}) collective-permute-start(bf16[256,2048]{1,0:T(8,128)(2,1)} %constant_dynamic-update-slice_fusion.35.refs_4_), channel_id=1, source_target_pairs={{0,2},{1,3},{2,0},{3,1},{4,6},{5,7},{6,4},{7,5},{8,10},{9,11},{10,... | collective-permute-start | bytes 3145736 | tf_op jit(solution)/shard_map/ppermute | solution.py:362
  281.6 47.8 %collective-permute-start.45 = (bf16[256,2048]{1,0:T(8,128)(2,1)}, bf16[256,2048]{1,0:T(8,128)(2,1)}, u32[]{:S(2)}, u32[]{:S(2)}) collective-permute-start(bf16[256,2048]{1,0:T(8,128)(2,1)} %constant_dynamic-update-slice_fusion.35.refs_4_), channel_id=1, source_target_pairs={{0,1},{1,0},{2,3},{3,2},{4,5},{5,4},{6,7},{7,6},{8,9},{9,8},{10,11... | collective-permute-start | bytes 3145736 | tf_op jit(solution)/shard_map/ppermute | solution.py:362
  281.9 43.6 %collective-permute-start.41 = (bf16[256,2048]{1,0:T(8,128)(2,1)}, bf16[256,2048]{1,0:T(8,128)(2,1)}, u32[]{:S(2)}, u32[]{:S(2)}) collective-permute-start(bf16[256,2048]{1,0:T(8,128)(2,1)} %constant_dynamic-update-slice_fusion.30.refs_0_), channel_id=1, source_target_pairs={{0,4},{1,5},{2,6},{3,7},{4,0},{5,1},{6,2},{7,3},{8,12},{9,13},{10,... | collective-permute-start | bytes 3145736 | tf_op jit(solution)/shard_map/ppermute | solution.py:362
  282.2 47.2 %collective-permute-start.43 = (bf16[256,2048]{1,0:T(8,128)(2,1)}, bf16[256,2048]{1,0:T(8,128)(2,1)}, u32[]{:S(2)}, u32[]{:S(2)}) collective-permute-start(bf16[256,2048]{1,0:T(8,128)(2,1)} %constant_dynamic-update-slice_fusion.30.refs_0_), channel_id=1, source_target_pairs={{0,1},{1,0},{2,3},{3,2},{4,5},{5,4},{6,7},{7,6},{8,9},{9,8},{10,11... | collective-permute-start | bytes 3145736 | tf_op jit(solution)/shard_map/ppermute | solution.py:362
  402.7 34.1 %collective-permute-start.48 = (bf16[512,4096]{1,0:T(8,128)(2,1)}, bf16[512,4096]{1,0:T(8,128)(2,1)}, u32[]{:S(2)}, u32[]{:S(2)}) collective-permute-start(bf16[512,4096]{1,0:T(8,128)(2,1)} %shard_map.223), channel_id=1, source_target_pairs={{0,1},{1,0},{2,3},{3,2},{4,5},{5,4},{6,7},{7,6},{8,9},{9,8},{10,11... | collective-permute-start | bytes 12582920 | tf_op jit(solution)/shard_map/ppermute | solution.py:362
  402.9 28.3 %collective-permute-start.49 = (bf16[256,2048]{1,0:T(8,128)(2,1)}, bf16[256,2048]{1,0:T(8,128)(2,1)S(1)}, u32[]{:S(2)}, u32[]{:S(2)}) collective-permute-start(bf16[256,2048]{1,0:T(8,128)(2,1)} %get-tuple-element.272), channel_id=1, source_target_pairs={{0,2},{1,3},{2,0},{3,1},{4,6},{5,7},{6,4},{7,5},{8,10},{9,11},{10,... | collective-permute-start | bytes 3145736 | tf_op jit(solution)/shard_map/ppermute | solution.py:362
  457.6 80.4 %collective-permute-start.59 = (bf16[512,1024]{1,0:T(8,128)(2,1)}, bf16[512,1024]{1,0:T(8,128)(2,1)S(1)}, u32[]{:S(2)}, u32[]{:S(2)}) collective-permute-start(bf16[512,1024]{1,0:T(8,128)(2,1)} %shard_map.226), channel_id=1, source_target_pairs={{0,1},{1,0},{2,3},{3,2},{4,5},{5,4},{6,7},{7,6},{8,9},{9,8},{10,11... | collective-permute-start | bytes 3145736 | tf_op jit(solution)/shard_map/ppermute | solution.py:362
  463.0 75.0 %collective-permute-start.56 = (bf16[32,4096]{1,0:T(8,128)(2,1)}, bf16[32,4096]{1,0:T(8,128)(2,1)S(1)}, u32[]{:S(2)}, u32[]{:S(2)}) collective-permute-start(bf16[32,4096]{1,0:T(8,128)(2,1)} %get-tuple-element.292), channel_id=1, source_target_pairs={{0,8},{1,9},{2,10},{3,11},{4,12},{5,13},{6,14},{7,15},{8,0},{9,1},... | collective-permute-start | bytes 786440 | tf_op jit(solution)/shard_map/ppermute | solution.py:362
  464.0 73.9 %collective-permute-start.57 = (bf16[32,4096]{1,0:T(8,128)(2,1)S(1)}, bf16[32,4096]{1,0:T(8,128)(2,1)S(1)}, u32[]{:S(2)}, u32[]{:S(2)}) collective-permute-start(bf16[32,4096]{1,0:T(8,128)(2,1)S(1)} %get-tuple-element.293), channel_id=1, source_target_pairs={{0,16},{1,17},{2,18},{3,19},{4,20},{5,21},{6,22},{7,23},{8,24},{9,... | collective-permute-start | bytes 786440 | tf_op jit(solution)/shard_map/ppermute | solution.py:362
  472.5 65.5 %collective-permute-start.58 = (bf16[32,4096]{1,0:T(8,128)(2,1)S(1)}, bf16[32,4096]{1,0:T(8,128)(2,1)S(1)}, u32[]{:S(2)}, u32[]{:S(2)}) collective-permute-start(bf16[32,4096]{1,0:T(8,128)(2,1)S(1)} %get-tuple-element.294), channel_id=1, source_target_pairs={{0,24},{1,25},{2,26},{3,27},{4,28},{5,29},{6,30},{7,31},{8,16},{9,... | collective-permute-start | bytes 786440 | tf_op jit(solution)/shard_map/ppermute | solution.py:362
  557.8 38.4 %collective-permute-start.62 = (bf16[512,1024]{1,0:T(8,128)(2,1)S(1)}, bf16[512,1024]{1,0:T(8,128)(2,1)S(1)}, u32[]{:S(2)}, u32[]{:S(2)}) collective-permute-start(bf16[512,1024]{1,0:T(8,128)(2,1)S(1)} %shard_map.232), channel_id=1, source_target_pairs={{0,1},{1,0},{2,3},{3,2},{4,5},{5,4},{6,7},{7,6},{8,9},{9,8},{10,11... | collective-permute-start | bytes 3145736 | tf_op jit(solution)/shard_map/ppermute | solution.py:362
  565.8 32.5 %collective-permute-start.61 = (bf16[512,2048]{1,0:T(8,128)(2,1)S(1)}, bf16[512,2048]{1,0:T(8,128)(2,1)S(1)}, u32[]{:S(2)}, u32[]{:S(2)}) collective-permute-start(bf16[512,2048]{1,0:T(8,128)(2,1)S(1)} %shard_map.233), channel_id=1, source_target_pairs={{0,1},{1,0},{2,3},{3,2},{4,5},{5,4},{6,7},{7,6},{8,9},{9,8},{10,11... | collective-permute-start | bytes 6291464 | tf_op jit(solution)/shard_map/ppermute | solution.py:362
  608.5 47.0 %collective-permute-start.70 = (bf16[512,1024]{1,0:T(8,128)(2,1)S(1)}, bf16[512,1024]{1,0:T(8,128)(2,1)S(1)}, u32[]{:S(2)}, u32[]{:S(2)}) collective-permute-start(bf16[512,1024]{1,0:T(8,128)(2,1)S(1)} %shard_map.237), channel_id=1, source_target_pairs={{0,1},{1,0},{2,3},{3,2},{4,5},{5,4},{6,7},{7,6},{8,9},{9,8},{10,11... | collective-permute-start | bytes 3145736 | tf_op jit(solution)/shard_map/ppermute | solution.py:362
  626.3 31.4 %collective-permute-start.68 = (bf16[512,1024]{1,0:T(8,128)(2,1)S(1)}, bf16[512,1024]{1,0:T(8,128)(2,1)S(1)}, u32[]{:S(2)}, u32[]{:S(2)}) collective-permute-start(bf16[512,1024]{1,0:T(8,128)(2,1)S(1)} %get-tuple-element.492), channel_id=1, source_target_pairs={{0,1},{1,0},{2,3},{3,2},{4,5},{5,4},{6,7},{7,6},{8,9},{9,8},{10,11... | collective-permute-start | bytes 3145736 | tf_op jit(solution)/shard_map/ppermute | solution.py:362
  626.9 30.9 %collective-permute-start.69 = (bf16[512,1024]{1,0:T(8,128)(2,1)S(1)}, bf16[512,1024]{1,0:T(8,128)(2,1)S(1)}, u32[]{:S(2)}, u32[]{:S(2)}) collective-permute-start(bf16[512,1024]{1,0:T(8,128)(2,1)S(1)} %get-tuple-element.491), channel_id=1, source_target_pairs={{0,1},{1,0},{2,3},{3,2},{4,5},{5,4},{6,7},{7,6},{8,9},{9,8},{10,11... | collective-permute-start | bytes 3145736 | tf_op jit(solution)/shard_map/ppermute | solution.py:362
  722.5 33.9 %collective-permute-start.86 = (bf16[512,3072]{1,0:T(8,128)(2,1)}, bf16[512,3072]{1,0:T(8,128)(2,1)}, u32[]{:S(2)}, u32[]{:S(2)}) collective-permute-start(bf16[512,3072]{1,0:T(8,128)(2,1)} %shard_map.243), channel_id=1, source_target_pairs={{0,1},{1,0},{2,3},{3,2},{4,5},{5,4},{6,7},{7,6},{8,9},{9,8},{10,11... | collective-permute-start | bytes 9437192 | tf_op jit(solution)/shard_map/ppermute | solution.py:362
  831.9 35.2 %all-to-all-start.1 = ((bf16[32,144,128]{2,1,0:T(8,128)(2,1)}), bf16[32,144,128]{2,1,0:T(8,128)(2,1)}, u32[]{:S(2)}, u32[]{:S(2)}) async-start(bf16[32,144,128]{2,1,0:T(8,128)(2,1)} %pad_maximum_fusion), calls=%async_computation.1 | async-start | bytes 2359296 | tf_op jit(solution)/shard_map/all_to_all | solution.py:1047
  (166 other events, 2351.4 us)
